TPU v7x, 32 devices: a whole 2x2x4 slice. The times are simulated.
32 devices in a mesh: occ: 4 (over y, core), vir: 8 (over z, x).
Axes of the slice: x: 2, y: 2, z: 4, core: 2. Of those that a mesh axis runs over, the one named last changes fastest.
Arguments:
- amplitudes: bfloat16 [8, 1024, 1024], P('occ', 'vir'), may hold values from -6 to 6
- factors: bfloat16 [24, 1024, 1024], P('vir'), may hold values from -0.0625 to 0.0625
- occ_energy: float32 [100], replicated, may hold values from -2 to -0.3
- vir_energy: float32 [1024], replicated, may hold values from 0.3 to 4
- occ_irrep: int32 [100], replicated, may hold values from 0 to 7
- vir_irrep: int32 [1024], replicated, may hold values from 0 to 7
- pair_orbitals: int32 [8, 2], replicated, may hold values from 0 to 99, as said below
Outputs:
- update: float32 [8, 1024, 1024], P('occ', 'vir')
Inputs may be any that keep to these rules, and one draw needn't show every extreme that they name: `pair_orbitals`: pair p + 4 is pair p with i and j swapped; the orbitals named by the first 4 pairs are all distinct.
All inputs are finite; a program needn't handle non-finite values.
Results may differ from a plain program's by a relative error of at most 0.0029.
Values may be sent and summed in bfloat16 or wider, within the bound.
No kernel may reach another device: no remote copies, remote signals or barrier semaphores. Data moves between devices by JAX's collectives and lax.ppermute only.
A program may use at most 128 MiB of HBM per device.

v0:
```python
import functools

import jax
import jax.numpy as jnp
from jax import lax
from jax.experimental import pallas as pl
from jax.experimental.pallas import tpu as pltpu
from jax.sharding import PartitionSpec as P

GROUP_ROWS = 256


def dot_nt(left, right):
    return lax.dot_general(left, right, (((1,), (1,)), ((), ())), preferred_element_type=jnp.float32)


def ladder_kernel(distances, inner, kept_count, has_total, splits, factor_ref, *refs):
    block_count = len(distances)
    vir_index = lax.axis_index("vir")
    z_index = vir_index // inner
    x_index = vir_index % inner
    z_low = z_index % 2
    pair_refs, refs = refs[: 2 * block_count], refs[2 * block_count :]
    total_ref = None
    if has_total:
        total_ref, refs = refs[0], refs[1:]
    out_count = 4 if splits else 1
    out_refs, refs = refs[:out_count], refs[out_count:]
    rows_ref, left_ref, right_ref = refs[:3]
    factor_count, size, _ = factor_ref.shape
    half = pair_refs[0].shape[0]
    width = block_count * GROUP_ROWS

    flip = x_index if inner == 2 else 0
    for block in range(block_count):
        first = block * GROUP_ROWS + flip * half
        second = block * GROUP_ROWS + (1 - flip) * half
        rows_ref[pl.ds(pl.multiple_of(first, half), half), :] = pair_refs[2 * block][...]
        rows_ref[pl.ds(pl.multiple_of(second, half), half), :] = pair_refs[2 * block + 1][...]

    if splits:
        other_left_ref = refs[3]
    for q in range(factor_count):
        if block_count == 1:
            halves = dot_nt(rows_ref[...], factor_ref[q]).T.astype(jnp.bfloat16)
        else:
            halves = dot_nt(factor_ref[q], rows_ref[...]).astype(jnp.bfloat16)
        for block in range(block_count):
            column = pl.multiple_of((z_index ^ distances[block]) * GROUP_ROWS, GROUP_ROWS)
            taken = factor_ref[q, :, pl.ds(column, GROUP_ROWS)]
            made = halves[:, block * GROUP_ROWS : (block + 1) * GROUP_ROWS]
            target = pl.ds(q * width + block * GROUP_ROWS, GROUP_ROWS)
            if block < kept_count:
                left_value, right_value = taken, made
            else:
                left_value, right_value = made, taken
            right_ref[:, target] = right_value
            if not splits:
                left_ref[:, target] = left_value
                continue
            for c in range(size // GROUP_ROWS):
                piece = left_value[c * GROUP_ROWS : (c + 1) * GROUP_ROWS]
                for x in range(2):
                    first = jnp.where(x_index == x, size // 2, 0) + c * half
                    left_ref[pl.ds(pl.multiple_of(first, half), half), target] = piece[x * half : (x + 1) * half]
                first = jnp.where(z_low == c % 2, size // 2, 0) + (c // 2) * GROUP_ROWS
                other_left_ref[pl.ds(pl.multiple_of(first, GROUP_ROWS), GROUP_ROWS), target] = piece

    if not splits:
        product = dot_nt(left_ref[...], right_ref[...])
        out_refs[0][...] = product + total_ref[...] if has_total else product
        return

    middle = size // 2
    for sent in (True, False):
        for number, source in enumerate((left_ref, other_left_ref)):
            columns = pl.ds(number * middle, middle)
            target = out_refs[number if sent else 2 + number]
            length = half if number == 0 else GROUP_ROWS
            product = dot_nt(source[pl.ds(0 if sent else middle, middle), :], right_ref[columns, :])
            for part in range(middle // length):
                if number == 0:
                    first = part * GROUP_ROWS + jnp.where(x_index == (0 if sent else 1), half, 0)
                else:
                    first = part * 2 * GROUP_ROWS + jnp.where(z_low == (0 if sent else 1), GROUP_ROWS, 0)
                before = total_ref[pl.ds(pl.multiple_of(first, length), length), columns]
                value = product[part * length : (part + 1) * length] + before
                target[part, :, :] = value.astype(target.dtype)


def ladder(distances, inner, factors, kept, swapped, total, splits=False):
    factor_count, size, _ = factors.shape
    pairs = list(kept) + list(swapped)
    width = len(pairs) * GROUP_ROWS
    middle = size // 2
    half = GROUP_ROWS // 2
    whole = pl.BlockSpec(memory_space=pltpu.VMEM)
    operands = [half_block for pair in pairs for half_block in pair]
    if total is not None:
        operands.append(total)
    in_specs = [whole] * (1 + len(operands))
    scratch = [
        pltpu.VMEM((width, size), jnp.bfloat16),
        pltpu.VMEM((size, factor_count * width), jnp.bfloat16),
        pltpu.VMEM((size, factor_count * width), jnp.bfloat16),
    ]
    out_shape = [jax.ShapeDtypeStruct((size, size), jnp.float32)]
    if splits:
        shapes = [(size // GROUP_ROWS, half, middle), (size // (2 * GROUP_ROWS), GROUP_ROWS, middle)]
        kinds = [(shape, kind) for kind in (jnp.bfloat16, jnp.float32) for shape in shapes]
        scratch.append(pltpu.VMEM((size, factor_count * width), jnp.bfloat16))
        out_shape = [jax.ShapeDtypeStruct(shape, kind) for shape, kind in kinds]
    out = pl.pallas_call(
        functools.partial(ladder_kernel, distances, inner, len(kept), total is not None, splits),
        out_shape=out_shape,
        in_specs=in_specs,
        out_specs=[whole] * len(out_shape),
        scratch_shapes=scratch,
        input_output_aliases={} if splits or total is None else {len(operands): 0},
        compiler_params=pltpu.CompilerParams(vmem_limit_bytes=24 * 1024 * 1024),
        cost_estimate=pl.CostEstimate(
            flops=4 * factor_count * width * size * size,
            bytes_accessed=2 * factor_count * size * size + 8 * size * size + 2 * width * size,
            transcendentals=0,
        ),
    )(factors, *operands)
    return out if splits else out[0]


def per_device(amplitudes, factors, occ_energy, vir_energy, occ_irrep, vir_irrep, pair_orbitals):
    local_pairs, row_count, size = amplitudes.shape
    occ_total = occ_energy.shape[0]
    occ_devices = lax.axis_size("occ")
    vir_devices = lax.axis_size("vir")
    inner = GROUP_ROWS // row_count
    outer = vir_devices // inner
    assert local_pairs == 2 and outer == 4 and inner * row_count == GROUP_ROWS
    occ_index = lax.axis_index("occ")
    vir_index = lax.axis_index("vir")
    z_index = vir_index // inner
    x_index = vir_index % inner
    side = occ_index // (occ_devices // 2)
    across = occ_devices // 2

    def z_swap(block, distance):
        route = [(i, (i // inner ^ distance) * inner + i % inner) for i in range(vir_devices)]
        return lax.ppermute(block, "vir", route)

    def y_swap(block):
        return lax.ppermute(block, "occ", [(i, (i + across) % occ_devices) for i in range(occ_devices)])

    inner_groups = [[g * inner + i for i in range(inner)] for g in range(outer)]

    def x_swap(block):
        return lax.ppermute(block, "vir", [(i, i ^ 1) for i in range(vir_devices)])

    def x_gather(block):
        if inner == 2:
            return block, x_swap(block)
        whole = lax.all_gather(block, "vir", axis_index_groups=inner_groups, axis=0, tiled=True)
        return whole[: GROUP_ROWS // 2], whole[GROUP_ROWS // 2 :]

    def x_scatter(sums):
        return lax.psum_scatter(sums, "vir", scatter_dimension=1, axis_index_groups=inner_groups)

    def z_scatter(sums, axis, distance, bit):
        sent = lax.dynamic_index_in_dim(sums, 1 - bit, axis, keepdims=False).astype(jnp.bfloat16)
        own = lax.dynamic_index_in_dim(sums, bit, axis, keepdims=False)
        return own + z_swap(sent, distance).astype(jnp.float32)

    def halved(own, came, bit, swap):
        came = came.reshape(own.shape)

        def half(index):
            mine = lax.dynamic_index_in_dim(own, index, 1, keepdims=False)
            theirs = lax.dynamic_index_in_dim(came, index, 1, keepdims=False)
            return mine + theirs.astype(jnp.float32)

        return half(bit) + swap(half(1 - bit).astype(jnp.bfloat16)).astype(jnp.float32)

    z_high = z_index // 2
    z_low = z_index % 2

    kept_0 = lax.dynamic_index_in_dim(amplitudes, side, 0, keepdims=False)
    given = lax.dynamic_index_in_dim(amplitudes, 1 - side, 0, keepdims=False)
    swapped_0 = y_swap(given)
    kept_2 = z_swap(kept_0, 2)
    kept_1 = z_swap(kept_0, 1)
    kept_pair_0 = x_gather(kept_0)
    swapped_2 = z_swap(swapped_0, 2)
    swapped_1 = z_swap(swapped_0, 1)
    swapped_pair_0 = x_gather(swapped_0)
    kept_pair_1 = x_gather(kept_1)
    total = ladder((0,), inner, factors, [kept_pair_0], [], None)
    kept_2, swapped_1, total = lax.optimization_barrier((kept_2, swapped_1, total))
    kept_3 = z_swap(kept_2, 1)
    kept_pair_2 = x_gather(kept_2)
    swapped_pair_1 = x_gather(swapped_1)
    total = ladder((1, 0), inner, factors, [kept_pair_1], [swapped_pair_0], total)
    swapped_2, kept_3, total = lax.optimization_barrier((swapped_2, kept_3, total))
    swapped_3 = z_swap(swapped_2, 1)
    swapped_pair_2 = x_gather(swapped_2)
    kept_pair_3 = x_gather(kept_3)
    total = ladder((2, 1), inner, factors, [kept_pair_2], [swapped_pair_1], total)
    swapped_3, total = lax.optimization_barrier((swapped_3, total))
    swapped_pair_3 = x_gather(swapped_3)
    total = ladder((3, 2), inner, factors, [kept_pair_3], [swapped_pair_2], total)

    middle = size // 2
    if inner == 2:
        sent_x, sent_z, own_x, own_z = ladder((3,), inner, factors, [], [swapped_pair_3], total, True)
        left = halved(own_x.reshape(2, 2, row_count, middle), x_swap(sent_x), z_low, lambda b: z_swap(b, 1))
        right = halved(own_z.reshape(2, 2, row_count, middle), z_swap(sent_z, 1), x_index, x_swap)
    else:
        total = ladder((3,), inner, factors, [], [swapped_pair_3], total)
        left = x_scatter(total[:, :middle].reshape(4, inner, row_count, middle))
        left = z_scatter(left.reshape(2, 2, row_count, middle), 1, 1, z_low)
        right = z_scatter(total[:, middle:].reshape(2, 2, GROUP_ROWS, middle), 1, 1, z_low)
        right = x_scatter(right.reshape(2, inner, row_count, middle))
    own_rows = jnp.concatenate([z_scatter(left, 0, 2, z_high), z_scatter(right, 0, 2, z_high)], axis=1)

    packed = own_rows.astype(jnp.bfloat16).reshape(row_count, vir_devices, row_count)
    packed = jnp.transpose(packed, (1, 2, 0))
    if inner == 2:
        def flipped(blocks):
            blocks = blocks.reshape(2, 2, *blocks.shape[1:])
            blocks = jnp.where(z_high == 1, jnp.flip(blocks, 0), blocks)
            blocks = jnp.where(z_low == 1, jnp.flip(blocks, 1), blocks)
            return blocks.reshape(4, *blocks.shape[2:])

        packed = packed.reshape(4, 2, row_count, row_count)
        stays = lax.dynamic_index_in_dim(packed, x_index, 1, keepdims=False)
        leaves = lax.dynamic_index_in_dim(packed, 1 - x_index, 1, keepdims=False)
        came = x_swap(leaves)
        first = jnp.where(x_index == 0, stays, came)
        second = jnp.where(x_index == 0, came, stays)
        turned = flipped(jnp.concatenate([first, second], axis=2))
        came = []
        for step in range(4):
            route = [
                (o * vir_devices + i, ((o + across) % occ_devices) * vir_devices + (i ^ 2 * step))
                for o in range(occ_devices)
                for i in range(vir_devices)
            ]
            came.append(lax.ppermute(turned[step], ("occ", "vir"), route))
        partner = flipped(jnp.stack(came))
    else:
        partner = y_swap(lax.all_to_all(packed, "vir", 0, 0))
    partner = jnp.transpose(partner, (1, 0, 2)).reshape(row_count, size).astype(jnp.float32)

    first = jnp.where(side == 0, own_rows, partner)
    second = jnp.where(side == 0, partner, own_rows)
    numerator = jnp.stack([first, second])

    pair_ids = lax.dynamic_slice_in_dim(pair_orbitals, occ_index * local_pairs, local_pairs, 0)
    row_start = vir_index * row_count
    energy_rows = lax.dynamic_slice_in_dim(vir_energy, row_start, row_count, 0)
    irrep_rows = lax.dynamic_slice_in_dim(vir_irrep, row_start, row_count, 0)
    positions = jnp.arange(occ_total, dtype=jnp.int32)
    first_hot = positions[None, :] == pair_ids[:, 0:1]
    second_hot = positions[None, :] == pair_ids[:, 1:2]
    pair_energy = jnp.sum(jnp.where(first_hot, occ_energy[None, :], 0.0), axis=1) + jnp.sum(
        jnp.where(second_hot, occ_energy[None, :], 0.0), axis=1
    )
    first_irrep = jnp.sum(jnp.where(first_hot, occ_irrep[None, :], 0), axis=1)
    second_irrep = jnp.sum(jnp.where(second_hot, occ_irrep[None, :], 0), axis=1)
    pair_sym = jnp.bitwise_xor(first_irrep, second_irrep)
    combined = jnp.bitwise_xor(
        jnp.bitwise_xor(pair_sym[:, None, None], irrep_rows[None, :, None]),
        vir_irrep[None, None, :],
    )
    allowed = combined == 0
    denominator = (
        energy_rows[None, :, None] + vir_energy[None, None, :] - pair_energy[:, None, None]
    )
    return jnp.where(allowed, numerator / denominator, jnp.float32(0.0))


def solution(mesh):
    return jax.shard_map(
        per_device,
        mesh=mesh,
        in_specs=(P("occ", "vir", None), P("vir", None, None), P(), P(), P(), P(), P()),
        out_specs=P("occ", "vir", None),
        check_vma=False,
    )
```

profile of v0, /device:TPU:0, one launch (start us, length us, event | category | flops | bytes accessed | tf_op | source)
XLA Modules:
  0.0 116.7 jit_solution(5921124133113782616)
XLA Ops:
  1.1 3.0 %collective-permute-start = (bf16[128,1024]{1,0:T(8,128)(2,1)S(1)}, bf16[128,1024]{1,0:T(8,128)(2,1)S(1)}, u32[]{:S(2)}, u32[]{:S(2)}) collective-permute-start(bf16[128,1024]{1,0:T(8,128)(2,1)S(1)} %get-tuple-element.40), channel_id=1, source_target_pairs={{0,16},{8,24},{16,0},{24,8},{1,17},{9,25},{17,1},{25,9},{2,18},{10... | collective-permute-start | bytes 786440 | tf_op jit(solution)/shard_map/ppermute | solution.py:150
  4.1 1.5 %collective-permute-start.4 = (bf16[128,1024]{1,0:T(8,128)(2,1)S(1)}, bf16[128,1024]{1,0:T(8,128)(2,1)S(1)}, u32[]{:S(2)}, u32[]{:S(2)}) collective-permute-start(bf16[128,1024]{1,0:T(8,128)(2,1)S(1)} %get-tuple-element.39.refs_0_), channel_id=1, source_target_pairs={{0,1},{1,0},{2,3},{3,2},{4,5},{5,4},{6,7},{7,6},{8,9},{9,8},{10,11... | collective-permute-start | bytes 786440 | tf_op jit(solution)/shard_map/ppermute | solution.py:155
  5.6 1.6 %collective-permute-start.6 = (bf16[128,1024]{1,0:T(8,128)(2,1)S(1)}, bf16[128,1024]{1,0:T(8,128)(2,1)S(1)}, u32[]{:S(2)}, u32[]{:S(2)}) collective-permute-start(bf16[128,1024]{1,0:T(8,128)(2,1)S(1)} %get-tuple-element.39.refs_0_), channel_id=1, source_target_pairs={{0,2},{1,3},{2,0},{3,1},{4,6},{5,7},{6,4},{7,5},{8,10},{9,11},{10,... | collective-permute-start | bytes 786440 | tf_op jit(solution)/shard_map/ppermute | solution.py:147
  7.2 2.6 %collective-permute-start.2 = (bf16[128,1024]{1,0:T(8,128)(2,1)S(1)}, bf16[128,1024]{1,0:T(8,128)(2,1)S(1)}, u32[]{:S(2)}, u32[]{:S(2)}) collective-permute-start(bf16[128,1024]{1,0:T(8,128)(2,1)S(1)} %get-tuple-element.39.refs_0_), channel_id=1, source_target_pairs={{0,4},{1,5},{2,6},{3,7},{4,0},{5,1},{6,2},{7,3},{8,12},{9,13},{10,... | collective-permute-start | bytes 786440 | tf_op jit(solution)/shard_map/ppermute | solution.py:147
  10.4 1.8 %collective-permute-start.3 = (bf16[128,1024]{1,0:T(8,128)(2,1)S(1)}, bf16[128,1024]{1,0:T(8,128)(2,1)S(1)}, u32[]{:S(2)}, u32[]{:S(2)}) collective-permute-start(bf16[128,1024]{1,0:T(8,128)(2,1)S(1)} %collective-permute-done.refs_2_), channel_id=1, source_target_pairs={{0,2},{1,3},{2,0},{3,1},{4,6},{5,7},{6,4},{7,5},{8,10},{9,11},{10,... | collective-permute-start | bytes 786440 | tf_op jit(solution)/shard_map/ppermute | solution.py:147
  12.2 1.5 %collective-permute-start.8 = (bf16[128,1024]{1,0:T(8,128)(2,1)S(1)}, bf16[128,1024]{1,0:T(8,128)(2,1)S(1)}, u32[]{:S(2)}, u32[]{:S(2)}) collective-permute-start(bf16[128,1024]{1,0:T(8,128)(2,1)S(1)} %collective-permute-done.refs_2_), channel_id=1, source_target_pairs={{0,1},{1,0},{2,3},{3,2},{4,5},{5,4},{6,7},{7,6},{8,9},{9,8},{10,11... | collective-permute-start | bytes 786440 | tf_op jit(solution)/shard_map/ppermute | solution.py:155
  13.7 2.6 %collective-permute-start.1 = (bf16[128,1024]{1,0:T(8,128)(2,1)S(1)}, bf16[128,1024]{1,0:T(8,128)(2,1)S(1)}, u32[]{:S(2)}, u32[]{:S(2)}) collective-permute-start(bf16[128,1024]{1,0:T(8,128)(2,1)S(1)} %collective-permute-done.refs_2_), channel_id=1, source_target_pairs={{0,4},{1,5},{2,6},{3,7},{4,0},{5,1},{6,2},{7,3},{8,12},{9,13},{10,... | collective-permute-start | bytes 786440 | tf_op jit(solution)/shard_map/ppermute | solution.py:147
  16.3 5.3 %collective-permute-done.6.refs_0_ = bf16[128,1024]{1,0:T(8,128)(2,1)S(1)} collective-permute-done((bf16[128,1024]{1,0:T(8,128)(2,1)S(1)}, bf16[128,1024]{1,0:T(8,128)(2,1)S(1)}, u32[]{:S(2)}, u32[]{:S(2)}) %collective-permute-start.6) | collective-permute-done | bytes 262176 | tf_op jit(solution)/shard_map/ppermute | solution.py:147
  22.1 2.8 %copy-done.1 = bf16[3,1024,1024]{2,1,0:T(8,128)(2,1)S(1)} copy-done((bf16[3,1024,1024]{2,1,0:T(8,128)(2,1)S(1)}, bf16[3,1024,1024]{2,1,0:T(8,128)(2,1)}, u32[]{:S(2)}) %copy-start.1) | copy-done | bytes 6291480
  24.9 3.5 %shard_map.73.refs_4_ = f32[1024,1024]{1,0:T(8,128)S(1)} custom-call(bf16[3,1024,1024]{2,1,0:T(8,128)(2,1)S(1)} %copy-done.1, bf16[128,1024]{1,0:T(8,128)(2,1)S(1)} %get-tuple-element.39.refs_0_, bf16[128,1024]{1,0:T(8,128)(2,1)S(1)} %collective-permute-done.4.refs_1_), custom_call_target="tpu_custom_call" | custom-call | flops 3221225472 | bytes 15204352 | tf_op jit(solution)/shard_map/pallas_call | solution.py:113
  28.4 1.5 %collective-permute-done.3.refs_2_ = bf16[128,1024]{1,0:T(8,128)(2,1)S(1)} collective-permute-done((bf16[128,1024]{1,0:T(8,128)(2,1)S(1)}, bf16[128,1024]{1,0:T(8,128)(2,1)S(1)}, u32[]{:S(2)}, u32[]{:S(2)}) %collective-permute-start.3) | collective-permute-done | bytes 262176 | tf_op jit(solution)/shard_map/ppermute | solution.py:147
  30.4 1.5 %collective-permute-start.11 = (bf16[128,1024]{1,0:T(8,128)(2,1)S(1)}, bf16[128,1024]{1,0:T(8,128)(2,1)S(1)}, u32[]{:S(2)}, u32[]{:S(2)}) collective-permute-start(bf16[128,1024]{1,0:T(8,128)(2,1)S(1)} %collective-permute-done.3.refs_2_), channel_id=1, source_target_pairs={{0,1},{1,0},{2,3},{3,2},{4,5},{5,4},{6,7},{7,6},{8,9},{9,8},{10,11... | collective-permute-start | bytes 786440 | tf_op jit(solution)/shard_map/ppermute | solution.py:155
  31.9 6.9 %shard_map.74.refs_4_ = f32[1024,1024]{1,0:T(8,128)S(1)} custom-call(bf16[3,1024,1024]{2,1,0:T(8,128)(2,1)S(1)} %copy-done.1, bf16[128,1024]{1,0:T(8,128)(2,1)S(1)} %collective-permute-done.6.refs_0_, bf16[128,1024]{1,0:T(8,128)(2,1)S(1)} %collective-permute-done.7.refs_1_, ...), custom_call_target="tpu_custom_call", output_to_operand_aliasing={{}: (5, {})} | custom-call | flops 6442450944 | bytes 15728640 | tf_op jit(solution)/shard_map/pallas_call | solution.py:113
  38.8 2.1 %collective-permute-start.9 = (bf16[128,1024]{1,0:T(8,128)(2,1)S(1)}, bf16[128,1024]{1,0:T(8,128)(2,1)S(1)}, u32[]{:S(2)}, u32[]{:S(2)}) collective-permute-start(bf16[128,1024]{1,0:T(8,128)(2,1)S(1)} %collective-permute-done.1.refs_2_), channel_id=1, source_target_pairs={{0,2},{1,3},{2,0},{3,1},{4,6},{5,7},{6,4},{7,5},{8,10},{9,11},{10,... | collective-permute-start | bytes 786440 | tf_op jit(solution)/shard_map/ppermute | solution.py:147
  41.5 1.5 %collective-permute-start.13 = (bf16[128,1024]{1,0:T(8,128)(2,1)S(1)}, bf16[128,1024]{1,0:T(8,128)(2,1)S(1)}, u32[]{:S(2)}, u32[]{:S(2)}) collective-permute-start(bf16[128,1024]{1,0:T(8,128)(2,1)S(1)} %collective-permute-done.5.refs_0_), channel_id=1, source_target_pairs={{0,1},{1,0},{2,3},{3,2},{4,5},{5,4},{6,7},{7,6},{8,9},{9,8},{10,11... | collective-permute-start | bytes 786440 | tf_op jit(solution)/shard_map/ppermute | solution.py:155
  43.0 7.1 %shard_map.75.refs_4_ = f32[1024,1024]{1,0:T(8,128)S(1)} custom-call(bf16[3,1024,1024]{2,1,0:T(8,128)(2,1)S(1)} %copy-done.1, bf16[128,1024]{1,0:T(8,128)(2,1)S(1)} %collective-permute-done.2.refs_0_, bf16[128,1024]{1,0:T(8,128)(2,1)S(1)} %collective-permute-done.10.refs_1_, ...), custom_call_target="tpu_custom_call", output_to_operand_aliasing={{}: (5, {})} | custom-call | flops 6442450944 | bytes 15728640 | tf_op jit(solution)/shard_map/pallas_call | solution.py:113
  50.7 5.0 %collective-permute-done.13.refs_1_ = bf16[128,1024]{1,0:T(8,128)(2,1)S(1)} collective-permute-done((bf16[128,1024]{1,0:T(8,128)(2,1)S(1)}, bf16[128,1024]{1,0:T(8,128)(2,1)S(1)}, u32[]{:S(2)}, u32[]{:S(2)}) %collective-permute-start.13) | collective-permute-done | bytes 262176 | tf_op jit(solution)/shard_map/ppermute | solution.py:155
  55.8 6.9 %shard_map.76.refs_2_ = f32[1024,1024]{1,0:T(8,128)S(1)} custom-call(bf16[3,1024,1024]{2,1,0:T(8,128)(2,1)S(1)} %copy-done.1, bf16[128,1024]{1,0:T(8,128)(2,1)S(1)} %collective-permute-done.5.refs_0_, bf16[128,1024]{1,0:T(8,128)(2,1)S(1)} %collective-permute-done.13.refs_1_, ...), custom_call_target="tpu_custom_call", output_to_operand_aliasing={{}: (5, {})} | custom-call | flops 6442450944 | bytes 15728640 | tf_op jit(solution)/shard_map/pallas_call | solution.py:113
  62.8 3.5 %shard_map.77 = (bf16[4,128,512]{2,1,0:T(8,128)(2,1)S(1)}, bf16[2,256,512]{2,1,0:T(8,128)(2,1)S(1)}, f32[4,128,512]{2,1,0:T(8,128)S(1)}, f32[2,256,512]{2,1,0:T(8,128)S(1)}) custom-call(bf16[3,1024,1024]{2,1,0:T(8,128)(2,1)S(1)} %copy-done.1, bf16[128,1024]{1,0:T(8,128)(2,1)S(1)} %collective-permute-done.9.refs_0_, ...), custom_call_target="tpu_custom_call" | custom-call | flops 3221225472 | bytes 15204352 | tf_op jit(solution)/shard_map/pallas_call | solution.py:113
  67.0 1.5 %collective-permute-start.18 = (bf16[2,256,512]{2,1,0:T(8,128)(2,1)S(1)}, bf16[2,256,512]{2,1,0:T(8,128)(2,1)}, u32[]{:S(2)}, u32[]{:S(2)}) collective-permute-start(bf16[2,256,512]{2,1,0:T(8,128)(2,1)S(1)} %get-tuple-element.28), channel_id=1, source_target_pairs={{0,2},{1,3},{2,0},{3,1},{4,6},{5,7},{6,4},{7,5},{8,10},{9,11},{10,... | collective-permute-start | bytes 1572872 | tf_op jit(solution)/shard_map/ppermute | solution.py:147
  68.9 6.8 %collective-permute-done.15 = bf16[4,128,512]{2,1,0:T(8,128)(2,1)} collective-permute-done((bf16[4,128,512]{2,1,0:T(8,128)(2,1)S(1)}, bf16[4,128,512]{2,1,0:T(8,128)(2,1)}, u32[]{:S(2)}, u32[]{:S(2)}) %collective-permute-start.15) | collective-permute-done | bytes 524320 | tf_op jit(solution)/shard_map/ppermute | solution.py:155
  76.7 2.7 %collective-permute-start.16 = (bf16[2,128,512]{2,1,0:T(8,128)(2,1)S(1)}, bf16[2,128,512]{2,1,0:T(8,128)(2,1)S(1)}, u32[]{:S(2)}, u32[]{:S(2)}) collective-permute-start(bf16[2,128,512]{2,1,0:T(8,128)(2,1)S(1)} %fusion.9), channel_id=1, source_target_pairs={{0,2},{1,3},{2,0},{3,1},{4,6},{5,7},{6,4},{7,5},{8,10},{9,11},{10,... | collective-permute-start | bytes 786440 | tf_op jit(solution)/shard_map/ppermute | solution.py:147
  80.5 1.2 collective-permute-start.19
  81.7 2.0 %collective-permute-done.16 = bf16[2,128,512]{2,1,0:T(8,128)(2,1)S(1)} collective-permute-done((bf16[2,128,512]{2,1,0:T(8,128)(2,1)S(1)}, bf16[2,128,512]{2,1,0:T(8,128)(2,1)S(1)}, u32[]{:S(2)}, u32[]{:S(2)}) %collective-permute-start.16) | collective-permute-done | bytes 262176 | tf_op jit(solution)/shard_map/ppermute | solution.py:147
  84.8 6.1 %collective-permute-start.17 = (bf16[128,512]{1,0:T(8,128)(2,1)S(1)}, bf16[128,512]{1,0:T(8,128)(2,1)S(1)}, u32[]{:S(2)}, u32[]{:S(2)}) collective-permute-start(bf16[128,512]{1,0:T(8,128)(2,1)S(1)} %fusion.15), channel_id=1, source_target_pairs={{0,4},{1,5},{2,6},{3,7},{4,0},{5,1},{6,2},{7,3},{8,12},{9,13},{10,... | collective-permute-start | bytes 393224 | tf_op jit(solution)/shard_map/ppermute | solution.py:147
  92.1 2.1 %collective-permute-done.17 = bf16[128,512]{1,0:T(8,128)(2,1)S(1)} collective-permute-done((bf16[128,512]{1,0:T(8,128)(2,1)S(1)}, bf16[128,512]{1,0:T(8,128)(2,1)S(1)}, u32[]{:S(2)}, u32[]{:S(2)}) %collective-permute-start.17) | collective-permute-done | bytes 131104 | tf_op jit(solution)/shard_map/ppermute | solution.py:147
  94.4 3.9 %collective-permute-done.20 = bf16[128,512]{1,0:T(8,128)(2,1)S(1)} collective-permute-done((bf16[128,512]{1,0:T(8,128)(2,1)S(1)}, bf16[128,512]{1,0:T(8,128)(2,1)S(1)}, u32[]{:S(2)}, u32[]{:S(2)}) %collective-permute-start.20) | collective-permute-done | bytes 131104 | tf_op jit(solution)/shard_map/ppermute | solution.py:147
  98.7 4.9 %collective-permute-done.21 = bf16[4,128,128]{2,1,0:T(8,128)(2,1)S(1)} collective-permute-done((bf16[4,128,128]{2,1,0:T(8,128)(2,1)S(1)}, bf16[4,128,128]{2,1,0:T(8,128)(2,1)S(1)}, u32[]{:S(2)}, u32[]{:S(2)}) %collective-permute-start.21) | collective-permute-done | bytes 131104 | tf_op jit(solution)/shard_map/ppermute | solution.py:155
  104.5 3.1 %collective-permute-start.24 = (bf16[128,256]{1,0:T(8,128)(2,1)S(1)}, bf16[128,256]{1,0:T(8,128)(2,1)S(1)}, u32[]{:S(2)}, u32[]{:S(2)}) collective-permute-start(bf16[128,256]{1,0:T(8,128)(2,1)S(1)} %get-tuple-element.45), channel_id=1, source_target_pairs={{0,20},{1,21},{2,22},{3,23},{4,16},{5,17},{6,18},{7,19},{8,28},{9,... | collective-permute-start | bytes 196616 | tf_op jit(solution)/shard_map/ppermute | solution.py:245
  107.6 3.0 %collective-permute-start.25 = (bf16[128,256]{1,0:T(8,128)(2,1)S(1)}, bf16[128,256]{1,0:T(8,128)(2,1)S(1)}, u32[]{:S(2)}, u32[]{:S(2)}) collective-permute-start(bf16[128,256]{1,0:T(8,128)(2,1)S(1)} %get-tuple-element.44), channel_id=1, source_target_pairs={{0,22},{1,23},{2,20},{3,21},{4,18},{5,19},{6,16},{7,17},{8,30},{9,... | collective-permute-start | bytes 196616 | tf_op jit(solution)/shard_map/ppermute | solution.py:245
  110.8 3.7 %collective-permute-done.25 = bf16[128,256]{1,0:T(8,128)(2,1)S(1)} collective-permute-done((bf16[128,256]{1,0:T(8,128)(2,1)S(1)}, bf16[128,256]{1,0:T(8,128)(2,1)S(1)}, u32[]{:S(2)}, u32[]{:S(2)}) %collective-permute-start.25) | collective-permute-done | bytes 65568 | tf_op jit(solution)/shard_map/ppermute | solution.py:245
  115.5 1.3 %fusion = f32[2,128,1024]{2,1,0:T(8,128)} fusion(f32[1,128,1024]{2,1,0:T(8,128)S(1)} %get-tuple-element.34, f32[1,128,1024]{2,1,0:T(8,128)S(1)} %get-tuple-element.33, f32[2]{0:T(128)S(1)} %add.140, f32[128,1024]{1,0:T(8,128)S(1)} %broadcast_add_fusion, s32[1024]{0:T(1024)S(1)} %copy-done.3, s32[2,128]{1,0:T(2,128)S(1)} %broadcast_xor_fusion), kind=kLoop, calls=%fused_computation.1 | loop fusion | flops 1572864 | bytes 2626568 | tf_op jit(solution)/shard_map/jit(_where)/select_n | solution.py:276
  (73 shorter events, 12.0 us)
Async XLA Ops:
  0.0 66.9 %copy-start = (s32[8,2]{0,1:T(2,128)S(1)}, s32[8,2]{0,1:T(2,128)}, u32[]{:S(2)}) copy-start(s32[8,2]{0,1:T(2,128)} %param.13) | copy-start | bytes 196
  1.1 9.3 %collective-permute-start = (bf16[128,1024]{1,0:T(8,128)(2,1)S(1)}, bf16[128,1024]{1,0:T(8,128)(2,1)S(1)}, u32[]{:S(2)}, u32[]{:S(2)}) collective-permute-start(bf16[128,1024]{1,0:T(8,128)(2,1)S(1)} %get-tuple-element.40), channel_id=1, source_target_pairs={{0,16},{8,24},{16,0},{24,8},{1,17},{9,25},{17,1},{25,9},{2,18},{10... | collective-permute-start | bytes 786440 | tf_op jit(solution)/shard_map/ppermute | solution.py:150
  4.1 9.6 %collective-permute-start.4 = (bf16[128,1024]{1,0:T(8,128)(2,1)S(1)}, bf16[128,1024]{1,0:T(8,128)(2,1)S(1)}, u32[]{:S(2)}, u32[]{:S(2)}) collective-permute-start(bf16[128,1024]{1,0:T(8,128)(2,1)S(1)} %get-tuple-element.39.refs_0_), channel_id=1, source_target_pairs={{0,1},{1,0},{2,3},{3,2},{4,5},{5,4},{6,7},{7,6},{8,9},{9,8},{10,11... | collective-permute-start | bytes 786440 | tf_op jit(solution)/shard_map/ppermute | solution.py:155
  5.6 16.0 %collective-permute-start.6 = (bf16[128,1024]{1,0:T(8,128)(2,1)S(1)}, bf16[128,1024]{1,0:T(8,128)(2,1)S(1)}, u32[]{:S(2)}, u32[]{:S(2)}) collective-permute-start(bf16[128,1024]{1,0:T(8,128)(2,1)S(1)} %get-tuple-element.39.refs_0_), channel_id=1, source_target_pairs={{0,2},{1,3},{2,0},{3,1},{4,6},{5,7},{6,4},{7,5},{8,10},{9,11},{10,... | collective-permute-start | bytes 786440 | tf_op jit(solution)/shard_map/ppermute | solution.py:147
  7.2 21.2 %collective-permute-start.2 = (bf16[128,1024]{1,0:T(8,128)(2,1)S(1)}, bf16[128,1024]{1,0:T(8,128)(2,1)S(1)}, u32[]{:S(2)}, u32[]{:S(2)}) collective-permute-start(bf16[128,1024]{1,0:T(8,128)(2,1)S(1)} %get-tuple-element.39.refs_0_), channel_id=1, source_target_pairs={{0,4},{1,5},{2,6},{3,7},{4,0},{5,1},{6,2},{7,3},{8,12},{9,13},{10,... | collective-permute-start | bytes 786440 | tf_op jit(solution)/shard_map/ppermute | solution.py:147
  10.4 19.4 %collective-permute-start.3 = (bf16[128,1024]{1,0:T(8,128)(2,1)S(1)}, bf16[128,1024]{1,0:T(8,128)(2,1)S(1)}, u32[]{:S(2)}, u32[]{:S(2)}) collective-permute-start(bf16[128,1024]{1,0:T(8,128)(2,1)S(1)} %collective-permute-done.refs_2_), channel_id=1, source_target_pairs={{0,2},{1,3},{2,0},{3,1},{4,6},{5,7},{6,4},{7,5},{8,10},{9,11},{10,... | collective-permute-start | bytes 786440 | tf_op jit(solution)/shard_map/ppermute | solution.py:147
  12.2 19.6 %collective-permute-start.8 = (bf16[128,1024]{1,0:T(8,128)(2,1)S(1)}, bf16[128,1024]{1,0:T(8,128)(2,1)S(1)}, u32[]{:S(2)}, u32[]{:S(2)}) collective-permute-start(bf16[128,1024]{1,0:T(8,128)(2,1)S(1)} %collective-permute-done.refs_2_), channel_id=1, source_target_pairs={{0,1},{1,0},{2,3},{3,2},{4,5},{5,4},{6,7},{7,6},{8,9},{9,8},{10,11... | collective-permute-start | bytes 786440 | tf_op jit(solution)/shard_map/ppermute | solution.py:155
  13.7 25.1 %collective-permute-start.1 = (bf16[128,1024]{1,0:T(8,128)(2,1)S(1)}, bf16[128,1024]{1,0:T(8,128)(2,1)S(1)}, u32[]{:S(2)}, u32[]{:S(2)}) collective-permute-start(bf16[128,1024]{1,0:T(8,128)(2,1)S(1)} %collective-permute-done.refs_2_), channel_id=1, source_target_pairs={{0,4},{1,5},{2,6},{3,7},{4,0},{5,1},{6,2},{7,3},{8,12},{9,13},{10,... | collective-permute-start | bytes 786440 | tf_op jit(solution)/shard_map/ppermute | solution.py:147
  21.6 8.8 %collective-permute-start.7 = (bf16[128,1024]{1,0:T(8,128)(2,1)S(1)}, bf16[128,1024]{1,0:T(8,128)(2,1)S(1)}, u32[]{:S(2)}, u32[]{:S(2)}) collective-permute-start(bf16[128,1024]{1,0:T(8,128)(2,1)S(1)} %collective-permute-done.6.refs_0_), channel_id=1, source_target_pairs={{0,1},{1,0},{2,3},{3,2},{4,5},{5,4},{6,7},{7,6},{8,9},{9,8},{10,11... | collective-permute-start | bytes 786440 | tf_op jit(solution)/shard_map/ppermute | solution.py:155
  22.1 2.8 %copy-start.1 = (bf16[3,1024,1024]{2,1,0:T(8,128)(2,1)S(1)}, bf16[3,1024,1024]{2,1,0:T(8,128)(2,1)}, u32[]{:S(2)}) copy-start(bf16[3,1024,1024]{2,1,0:T(8,128)(2,1)} %factor_ref.9) | copy-start | bytes 18874372
  29.8 9.0 %collective-permute-start.5 = (bf16[128,1024]{1,0:T(8,128)(2,1)S(1)}, bf16[128,1024]{1,0:T(8,128)(2,1)S(1)}, u32[]{:S(2)}, u32[]{:S(2)}) collective-permute-start(bf16[128,1024]{1,0:T(8,128)(2,1)S(1)} %collective-permute-done.2.refs_0_), channel_id=1, source_target_pairs={{0,2},{1,3},{2,0},{3,1},{4,6},{5,7},{6,4},{7,5},{8,10},{9,11},{10,... | collective-permute-start | bytes 786440 | tf_op jit(solution)/shard_map/ppermute | solution.py:147
  29.8 13.1 %collective-permute-start.10 = (bf16[128,1024]{1,0:T(8,128)(2,1)S(1)}, bf16[128,1024]{1,0:T(8,128)(2,1)S(1)}, u32[]{:S(2)}, u32[]{:S(2)}) collective-permute-start(bf16[128,1024]{1,0:T(8,128)(2,1)S(1)} %collective-permute-done.2.refs_0_), channel_id=1, source_target_pairs={{0,1},{1,0},{2,3},{3,2},{4,5},{5,4},{6,7},{7,6},{8,9},{9,8},{10,11... | collective-permute-start | bytes 786440 | tf_op jit(solution)/shard_map/ppermute | solution.py:155
  30.4 12.6 %collective-permute-start.11 = (bf16[128,1024]{1,0:T(8,128)(2,1)S(1)}, bf16[128,1024]{1,0:T(8,128)(2,1)S(1)}, u32[]{:S(2)}, u32[]{:S(2)}) collective-permute-start(bf16[128,1024]{1,0:T(8,128)(2,1)S(1)} %collective-permute-done.3.refs_2_), channel_id=1, source_target_pairs={{0,1},{1,0},{2,3},{3,2},{4,5},{5,4},{6,7},{7,6},{8,9},{9,8},{10,11... | collective-permute-start | bytes 786440 | tf_op jit(solution)/shard_map/ppermute | solution.py:155
  38.8 11.3 %collective-permute-start.9 = (bf16[128,1024]{1,0:T(8,128)(2,1)S(1)}, bf16[128,1024]{1,0:T(8,128)(2,1)S(1)}, u32[]{:S(2)}, u32[]{:S(2)}) collective-permute-start(bf16[128,1024]{1,0:T(8,128)(2,1)S(1)} %collective-permute-done.1.refs_2_), channel_id=1, source_target_pairs={{0,2},{1,3},{2,0},{3,1},{4,6},{5,7},{6,4},{7,5},{8,10},{9,11},{10,... | collective-permute-start | bytes 786440 | tf_op jit(solution)/shard_map/ppermute | solution.py:147
  40.9 14.8 %collective-permute-start.14 = (bf16[128,1024]{1,0:T(8,128)(2,1)S(1)}, bf16[128,1024]{1,0:T(8,128)(2,1)S(1)}, u32[]{:S(2)}, u32[]{:S(2)}) collective-permute-start(bf16[128,1024]{1,0:T(8,128)(2,1)S(1)} %collective-permute-done.1.refs_2_), channel_id=1, source_target_pairs={{0,1},{1,0},{2,3},{3,2},{4,5},{5,4},{6,7},{7,6},{8,9},{9,8},{10,11... | collective-permute-start | bytes 786440 | tf_op jit(solution)/shard_map/ppermute | solution.py:155
  41.5 14.3 %collective-permute-start.13 = (bf16[128,1024]{1,0:T(8,128)(2,1)S(1)}, bf16[128,1024]{1,0:T(8,128)(2,1)S(1)}, u32[]{:S(2)}, u32[]{:S(2)}) collective-permute-start(bf16[128,1024]{1,0:T(8,128)(2,1)S(1)} %collective-permute-done.5.refs_0_), channel_id=1, source_target_pairs={{0,1},{1,0},{2,3},{3,2},{4,5},{5,4},{6,7},{7,6},{8,9},{9,8},{10,11... | collective-permute-start | bytes 786440 | tf_op jit(solution)/shard_map/ppermute | solution.py:155
  50.1 12.6 %collective-permute-start.12 = (bf16[128,1024]{1,0:T(8,128)(2,1)S(1)}, bf16[128,1024]{1,0:T(8,128)(2,1)S(1)}, u32[]{:S(2)}, u32[]{:S(2)}) collective-permute-start(bf16[128,1024]{1,0:T(8,128)(2,1)S(1)} %collective-permute-done.9.refs_0_), channel_id=1, source_target_pairs={{0,1},{1,0},{2,3},{3,2},{4,5},{5,4},{6,7},{7,6},{8,9},{9,8},{10,11... | collective-permute-start | bytes 786440 | tf_op jit(solution)/shard_map/ppermute | solution.py:155
  62.7 5.8 %copy-start.3 = (s32[1024]{0:T(1024)S(1)}, s32[1024]{0:T(1024)}, u32[]{:S(2)}) copy-start(s32[1024]{0:T(1024)} %param.12) | copy-start | bytes 12292
  62.7 5.8 %copy-start.2 = (f32[1024]{0:T(1024)S(1)}, f32[1024]{0:T(1024)}, u32[]{:S(2)}) copy-start(f32[1024]{0:T(1024)} %param.10) | copy-start | bytes 12292
  62.7 5.9 %copy-start.4 = (s32[100]{0:T(128)S(1)}, s32[100]{0:T(128)}, u32[]{:S(2)}) copy-start(s32[100]{0:T(128)} %param.11) | copy-start | bytes 1204
  66.3 9.4 %collective-permute-start.15 = (bf16[4,128,512]{2,1,0:T(8,128)(2,1)S(1)}, bf16[4,128,512]{2,1,0:T(8,128)(2,1)}, u32[]{:S(2)}, u32[]{:S(2)}) collective-permute-start(bf16[4,128,512]{2,1,0:T(8,128)(2,1)S(1)} %get-tuple-element.26), channel_id=1, source_target_pairs={{0,1},{1,0},{2,3},{3,2},{4,5},{5,4},{6,7},{7,6},{8,9},{9,8},{10,11... | collective-permute-start | bytes 1572872 | tf_op jit(solution)/shard_map/ppermute | solution.py:155
  67.0 12.5 %collective-permute-start.18 = (bf16[2,256,512]{2,1,0:T(8,128)(2,1)S(1)}, bf16[2,256,512]{2,1,0:T(8,128)(2,1)}, u32[]{:S(2)}, u32[]{:S(2)}) collective-permute-start(bf16[2,256,512]{2,1,0:T(8,128)(2,1)S(1)} %get-tuple-element.28), channel_id=1, source_target_pairs={{0,2},{1,3},{2,0},{3,1},{4,6},{5,7},{6,4},{7,5},{8,10},{9,11},{10,... | collective-permute-start | bytes 1572872 | tf_op jit(solution)/shard_map/ppermute | solution.py:147
  76.7 7.0 %collective-permute-start.16 = (bf16[2,128,512]{2,1,0:T(8,128)(2,1)S(1)}, bf16[2,128,512]{2,1,0:T(8,128)(2,1)S(1)}, u32[]{:S(2)}, u32[]{:S(2)}) collective-permute-start(bf16[2,128,512]{2,1,0:T(8,128)(2,1)S(1)} %fusion.9), channel_id=1, source_target_pairs={{0,2},{1,3},{2,0},{3,1},{4,6},{5,7},{6,4},{7,5},{8,10},{9,11},{10,... | collective-permute-start | bytes 786440 | tf_op jit(solution)/shard_map/ppermute | solution.py:147
  80.5 10.4 %collective-permute-start.19 = (bf16[2,128,512]{2,1,0:T(8,128)(2,1)S(1)}, bf16[2,128,512]{2,1,0:T(8,128)(2,1)S(1)}, u32[]{:S(2)}, u32[]{:S(2)}) collective-permute-start(bf16[2,128,512]{2,1,0:T(8,128)(2,1)S(1)} %fusion.10), channel_id=1, source_target_pairs={{0,1},{1,0},{2,3},{3,2},{4,5},{5,4},{6,7},{7,6},{8,9},{9,8},{10,11... | collective-permute-start | bytes 786440 | tf_op jit(solution)/shard_map/ppermute | solution.py:155
  84.7 25.8 %copy-start.5 = (f32[100]{0:T(128)S(1)}, f32[100]{0:T(128)}, u32[]{:S(2)}) copy-start(f32[100]{0:T(128)} %param.9) | copy-start | bytes 1204
  84.8 9.4 %collective-permute-start.17 = (bf16[128,512]{1,0:T(8,128)(2,1)S(1)}, bf16[128,512]{1,0:T(8,128)(2,1)S(1)}, u32[]{:S(2)}, u32[]{:S(2)}) collective-permute-start(bf16[128,512]{1,0:T(8,128)(2,1)S(1)} %fusion.15), channel_id=1, source_target_pairs={{0,4},{1,5},{2,6},{3,7},{4,0},{5,1},{6,2},{7,3},{8,12},{9,13},{10,... | collective-permute-start | bytes 393224 | tf_op jit(solution)/shard_map/ppermute | solution.py:147
  92.0 6.3 %collective-permute-start.20 = (bf16[128,512]{1,0:T(8,128)(2,1)S(1)}, bf16[128,512]{1,0:T(8,128)(2,1)S(1)}, u32[]{:S(2)}, u32[]{:S(2)}) collective-permute-start(bf16[128,512]{1,0:T(8,128)(2,1)S(1)} %fusion.16), channel_id=1, source_target_pairs={{0,4},{1,5},{2,6},{3,7},{4,0},{5,1},{6,2},{7,3},{8,12},{9,13},{10,... | collective-permute-start | bytes 393224 | tf_op jit(solution)/shard_map/ppermute | solution.py:147
  98.5 5.0 %collective-permute-start.21 = (bf16[4,128,128]{2,1,0:T(8,128)(2,1)S(1)}, bf16[4,128,128]{2,1,0:T(8,128)(2,1)S(1)}, u32[]{:S(2)}, u32[]{:S(2)}) collective-permute-start(bf16[4,128,128]{2,1,0:T(8,128)(2,1)S(1)} %dynamic-slice_bitcast_fusion.2), channel_id=1, source_target_pairs={{0,1},{1,0},{2,3},{3,2},{4,5},{5,4},{6,7},{7,6},{8,9},{9,8},{10,11... | collective-permute-start | bytes 393224 | tf_op jit(solution)/shard_map/ppermute | solution.py:155
  103.8 7.0 %collective-permute-start.22 = (bf16[128,256]{1,0:T(8,128)(2,1)S(1)}, bf16[128,256]{1,0:T(8,128)(2,1)S(1)}, u32[]{:S(2)}, u32[]{:S(2)}) collective-permute-start(bf16[128,256]{1,0:T(8,128)(2,1)S(1)} %get-tuple-element.43), channel_id=1, source_target_pairs={{0,16},{1,17},{2,18},{3,19},{4,20},{5,21},{6,22},{7,23},{8,24},{9,... | collective-permute-start | bytes 196616 | tf_op jit(solution)/shard_map/ppermute | solution.py:245
  104.3 6.6 %collective-permute-start.23 = (bf16[128,256]{1,0:T(8,128)(2,1)S(1)}, bf16[128,256]{1,0:T(8,128)(2,1)S(1)}, u32[]{:S(2)}, u32[]{:S(2)}) collective-permute-start(bf16[128,256]{1,0:T(8,128)(2,1)S(1)} %get-tuple-element.46), channel_id=1, source_target_pairs={{0,18},{1,19},{2,16},{3,17},{4,22},{5,23},{6,20},{7,21},{8,26},{9,... | collective-permute-start | bytes 196616 | tf_op jit(solution)/shard_map/ppermute | solution.py:245
  104.5 6.3 %collective-permute-start.24 = (bf16[128,256]{1,0:T(8,128)(2,1)S(1)}, bf16[128,256]{1,0:T(8,128)(2,1)S(1)}, u32[]{:S(2)}, u32[]{:S(2)}) collective-permute-start(bf16[128,256]{1,0:T(8,128)(2,1)S(1)} %get-tuple-element.45), channel_id=1, source_target_pairs={{0,20},{1,21},{2,22},{3,23},{4,16},{5,17},{6,18},{7,19},{8,28},{9,... | collective-permute-start | bytes 196616 | tf_op jit(solution)/shard_map/ppermute | solution.py:245
  107.6 7.0 %collective-permute-start.25 = (bf16[128,256]{1,0:T(8,128)(2,1)S(1)}, bf16[128,256]{1,0:T(8,128)(2,1)S(1)}, u32[]{:S(2)}, u32[]{:S(2)}) collective-permute-start(bf16[128,256]{1,0:T(8,128)(2,1)S(1)} %get-tuple-element.44), channel_id=1, source_target_pairs={{0,22},{1,23},{2,20},{3,21},{4,18},{5,19},{6,16},{7,17},{8,30},{9,... | collective-permute-start | bytes 196616 | tf_op jit(solution)/shard_map/ppermute | solution.py:245
where the time goes:
time: 117 us
  starting transfers between devices  40.9 us (35%)
  waiting for transfers between devices  35.9 us (31%)
  Pallas kernels  28 us (24%)
  other arithmetic  6.57 us (6%)
  local copies, waits for them, and re-layouts  5.06 us (4%)
    pallas_call x5, Pallas kernels, ladder(): pl.pallas_call(functools.partial(ladder_kernel, distances, inner, len(kep...  28 us
    ppermute x10, starting transfers between devices, z_swap(): return lax.ppermute(block, 'vir', route)  21 us
    ppermute x11, waiting for transfers between devices, x_swap(): return lax.ppermute(block, 'vir', [(i, i ^ 1) for i in range(vir_devices)])  16.7 us
    ppermute x10, waiting for transfers between devices, z_swap(): return lax.ppermute(block, 'vir', route)  14.8 us
    ppermute x11, starting transfers between devices, x_swap(): return lax.ppermute(block, 'vir', [(i, i ^ 1) for i in range(vir_devices)])  10 us
    ppermute x4, starting transfers between devices, per_device(): came.append(lax.ppermute(turned[step], ('occ', 'vir'), route))  6.81 us
    ppermute x4, waiting for transfers between devices, per_device(): came.append(lax.ppermute(turned[step], ('occ', 'vir'), route))  3.71 us
    ppermute x1, starting transfers between devices, y_swap(): lax.ppermute(block, 'occ', [(i, (i + across) % occ_devices) for i in rang...  3.03 us
  transfers between devices with their start and end apart: 26, of which 10 were waited for; matrix products, arithmetic and copies ran while one was open for 4% of the time, Pallas kernels for 21%

commit v1 on v0

--- a/solution.py
+++ b/solution.py
@@ -14,7 +14,7 @@
     return lax.dot_general(left, right, (((1,), (1,)), ((), ())), preferred_element_type=jnp.float32)
 
 
-def ladder_kernel(distances, inner, kept_count, has_total, splits, factor_ref, *refs):
+def ladder_kernel(distances, inner, kept_count, has_total, splits, loads, factor_ref, *refs):
     block_count = len(distances)
     vir_index = lax.axis_index("vir")
     z_index = vir_index // inner
@@ -27,6 +27,13 @@
     out_count = 4 if splits else 1
     out_refs, refs = refs[:out_count], refs[out_count:]
     rows_ref, left_ref, right_ref = refs[:3]
+    loading = []
+    if loads:
+        source_ref, factor_ref, factor_sem = factor_ref, refs[0], refs[4]
+        out_refs, (rows_ref, left_ref, right_ref) = out_refs, refs[1:4]
+        for q in range(factor_ref.shape[0]):
+            loading.append(pltpu.make_async_copy(source_ref.at[q], factor_ref.at[q], factor_sem.at[q]))
+            loading[q].start()
     factor_count, size, _ = factor_ref.shape
     half = pair_refs[0].shape[0]
     width = block_count * GROUP_ROWS
@@ -41,6 +48,8 @@
     if splits:
         other_left_ref = refs[3]
     for q in range(factor_count):
+        if loads:
+            loading[q].wait()
         if block_count == 1:
             halves = dot_nt(rows_ref[...], factor_ref[q]).T.astype(jnp.bfloat16)
         else:
@@ -88,7 +97,7 @@
                 target[part, :, :] = value.astype(target.dtype)
 
 
-def ladder(distances, inner, factors, kept, swapped, total, splits=False):
+def ladder(distances, inner, factors, kept, swapped, total, splits=False, loads=False):
     factor_count, size, _ = factors.shape
     pairs = list(kept) + list(swapped)
     width = len(pairs) * GROUP_ROWS
@@ -110,8 +119,13 @@
         kinds = [(shape, kind) for kind in (jnp.bfloat16, jnp.float32) for shape in shapes]
         scratch.append(pltpu.VMEM((size, factor_count * width), jnp.bfloat16))
         out_shape = [jax.ShapeDtypeStruct(shape, kind) for shape, kind in kinds]
+    if loads:
+        factors = pltpu.with_memory_space_constraint(factors, pltpu.HBM)
+        in_specs[0] = pl.BlockSpec(memory_space=pl.ANY)
+        out_shape.append(jax.ShapeDtypeStruct(factors.shape, factors.dtype))
+        scratch.append(pltpu.SemaphoreType.DMA((factor_count,)))
     out = pl.pallas_call(
-        functools.partial(ladder_kernel, distances, inner, len(kept), total is not None, splits),
+        functools.partial(ladder_kernel, distances, inner, len(kept), total is not None, splits, loads),
         out_shape=out_shape,
         in_specs=in_specs,
         out_specs=[whole] * len(out_shape),
@@ -124,7 +138,7 @@
             transcendentals=0,
         ),
     )(factors, *operands)
-    return out if splits else out[0]
+    return out if splits or loads else out[0]
 
 
 def per_device(amplitudes, factors, occ_energy, vir_energy, occ_irrep, vir_irrep, pair_orbitals):
@@ -184,6 +198,10 @@
     kept_0 = lax.dynamic_index_in_dim(amplitudes, side, 0, keepdims=False)
     given = lax.dynamic_index_in_dim(amplitudes, 1 - side, 0, keepdims=False)
     swapped_0 = y_swap(given)
+    def step(distance, kept, swapped, total):
+        return ladder((distance,), inner, factors, kept, swapped, total)
+
+    after = lax.optimization_barrier
     kept_2 = z_swap(kept_0, 2)
     kept_1 = z_swap(kept_0, 1)
     kept_pair_0 = x_gather(kept_0)
@@ -191,18 +209,18 @@
     swapped_1 = z_swap(swapped_0, 1)
     swapped_pair_0 = x_gather(swapped_0)
     kept_pair_1 = x_gather(kept_1)
-    total = ladder((0,), inner, factors, [kept_pair_0], [], None)
-    kept_2, swapped_1, total = lax.optimization_barrier((kept_2, swapped_1, total))
+    total, factors = ladder((0,), inner, factors, [kept_pair_0], [], None, loads=True)
+    kept_2, swapped_1, total = after((kept_2, swapped_1, total))
     kept_3 = z_swap(kept_2, 1)
     kept_pair_2 = x_gather(kept_2)
     swapped_pair_1 = x_gather(swapped_1)
     total = ladder((1, 0), inner, factors, [kept_pair_1], [swapped_pair_0], total)
-    swapped_2, kept_3, total = lax.optimization_barrier((swapped_2, kept_3, total))
+    swapped_2, kept_3, total = after((swapped_2, kept_3, total))
     swapped_3 = z_swap(swapped_2, 1)
     swapped_pair_2 = x_gather(swapped_2)
-    kept_pair_3 = x_gather(kept_3)
+    kept_pair_3 = (kept_3, z_swap(kept_pair_2[1], 1)) if inner == 2 else x_gather(kept_3)
     total = ladder((2, 1), inner, factors, [kept_pair_2], [swapped_pair_1], total)
-    swapped_3, total = lax.optimization_barrier((swapped_3, total))
+    swapped_3, total = after((swapped_3, total))
     swapped_pair_3 = x_gather(swapped_3)
     total = ladder((3, 2), inner, factors, [kept_pair_3], [swapped_pair_2], total)
 

time: 117 us -> 112 us (0.957)
  waiting for transfers between devices: 35.9 us -> 27.2 us
  starting transfers between devices: 40.9 us -> 45.3 us
  local copies, waits for them, and re-layouts: 5.06 us -> 2.28 us
  Pallas kernels: 28 us -> 30.3 us
    ppermute x11 -> x10, waiting for transfers between devices: 16.7 us -> 9.39 us  [x_swap(): return lax.ppermute(block, 'vir', [(i, i ^ 1) for i in range(vir_devices)])]
    unnamed x12 -> x10, local copies, waits for them, and re-layouts: 2.81 us -> 0.03 us
    ppermute x10 -> x11, starting transfers between devices: 21 us -> 23.6 us  [z_swap(): return lax.ppermute(block, 'vir', route)]
    pallas_call x5, Pallas kernels: 28 us -> 30.3 us  [ladder(): pl.pallas_call(functools.partial(ladder_kernel, distances, inner, len(kep...]
    ppermute x11 -> x10, starting transfers between devices: 10 us -> 11.8 us  [x_swap(): return lax.ppermute(block, 'vir', [(i, i ^ 1) for i in range(vir_devices)])]
    ppermute x10 -> x11, waiting for transfers between devices: 14.8 us -> 13.4 us  [z_swap(): return lax.ppermute(block, 'vir', route)]
  transfers between devices with their start and end apart: 26 -> 26, of which waited for: 10 -> 11; matrix products, arithmetic and copies ran while one was open for 4% -> 5% of each run, Pallas kernels for 21% -> 24%
where the time goes in v1:
time: 112 us
  starting transfers between devices  45.3 us (40%)
  Pallas kernels  30.3 us (27%)
  waiting for transfers between devices  27.2 us (24%)
  other arithmetic  6.56 us (6%)
  local copies, waits for them, and re-layouts  2.28 us (2%)
    pallas_call x5, Pallas kernels, ladder(): pl.pallas_call(functools.partial(ladder_kernel, distances, inner, len(kep...  30.3 us
    ppermute x11, starting transfers between devices, z_swap(): return lax.ppermute(block, 'vir', route)  23.6 us
    ppermute x11, waiting for transfers between devices, z_swap(): return lax.ppermute(block, 'vir', route)  13.4 us
    ppermute x10, starting transfers between devices, x_swap(): return lax.ppermute(block, 'vir', [(i, i ^ 1) for i in range(vir_devices)])  11.8 us
    ppermute x10, waiting for transfers between devices, x_swap(): return lax.ppermute(block, 'vir', [(i, i ^ 1) for i in range(vir_devices)])  9.39 us
    ppermute x4, starting transfers between devices, per_device(): came.append(lax.ppermute(turned[step], ('occ', 'vir'), route))  6.81 us
    ppermute x4, waiting for transfers between devices, per_device(): came.append(lax.ppermute(turned[step], ('occ', 'vir'), route))  3.81 us
    ppermute x1, starting transfers between devices, y_swap(): lax.ppermute(block, 'occ', [(i, (i + across) % occ_devices) for i in rang...  3.03 us
  transfers between devices with their start and end apart: 26, of which 11 were waited for; matrix products, arithmetic and copies ran while one was open for 5% of the time, Pallas kernels for 24%

profile of v1, /device:TPU:0, one launch (start us, length us, event | category | flops | bytes accessed | tf_op | source)
XLA Modules:
  0.0 112.0 jit_solution(17884682964117860336)
XLA Ops:
  1.1 3.0 %collective-permute-start.1 = (bf16[128,1024]{1,0:T(8,128)(2,1)S(1)}, bf16[128,1024]{1,0:T(8,128)(2,1)S(1)}, u32[]{:S(2)}, u32[]{:S(2)}) collective-permute-start(bf16[128,1024]{1,0:T(8,128)(2,1)S(1)} %get-tuple-element.43), channel_id=1, source_target_pairs={{0,16},{8,24},{16,0},{24,8},{1,17},{9,25},{17,1},{25,9},{2,18},{10... | collective-permute-start | bytes 786440 | tf_op jit(solution)/shard_map/ppermute | solution.py:164
  4.1 1.5 %collective-permute-start = (bf16[128,1024]{1,0:T(8,128)(2,1)S(1)}, bf16[128,1024]{1,0:T(8,128)(2,1)S(1)}, u32[]{:S(2)}, u32[]{:S(2)}) collective-permute-start(bf16[128,1024]{1,0:T(8,128)(2,1)S(1)} %get-tuple-element.44.refs_0_), channel_id=1, source_target_pairs={{0,1},{1,0},{2,3},{3,2},{4,5},{5,4},{6,7},{7,6},{8,9},{9,8},{10,11... | collective-permute-start | bytes 786440 | tf_op jit(solution)/shard_map/ppermute | solution.py:169
  5.6 1.6 %collective-permute-start.6 = (bf16[128,1024]{1,0:T(8,128)(2,1)S(1)}, bf16[128,1024]{1,0:T(8,128)(2,1)S(1)}, u32[]{:S(2)}, u32[]{:S(2)}) collective-permute-start(bf16[128,1024]{1,0:T(8,128)(2,1)S(1)} %get-tuple-element.44.refs_0_), channel_id=1, source_target_pairs={{0,2},{1,3},{2,0},{3,1},{4,6},{5,7},{6,4},{7,5},{8,10},{9,11},{10,... | collective-permute-start | bytes 786440 | tf_op jit(solution)/shard_map/ppermute | solution.py:161
  7.2 2.6 %collective-permute-start.3 = (bf16[128,1024]{1,0:T(8,128)(2,1)S(1)}, bf16[128,1024]{1,0:T(8,128)(2,1)S(1)}, u32[]{:S(2)}, u32[]{:S(2)}) collective-permute-start(bf16[128,1024]{1,0:T(8,128)(2,1)S(1)} %get-tuple-element.44.refs_0_), channel_id=1, source_target_pairs={{0,4},{1,5},{2,6},{3,7},{4,0},{5,1},{6,2},{7,3},{8,12},{9,13},{10,... | collective-permute-start | bytes 786440 | tf_op jit(solution)/shard_map/ppermute | solution.py:161
  10.4 1.8 %collective-permute-start.4 = (bf16[128,1024]{1,0:T(8,128)(2,1)S(1)}, bf16[128,1024]{1,0:T(8,128)(2,1)S(1)}, u32[]{:S(2)}, u32[]{:S(2)}) collective-permute-start(bf16[128,1024]{1,0:T(8,128)(2,1)S(1)} %collective-permute-done.1.refs_2_), channel_id=1, source_target_pairs={{0,2},{1,3},{2,0},{3,1},{4,6},{5,7},{6,4},{7,5},{8,10},{9,11},{10,... | collective-permute-start | bytes 786440 | tf_op jit(solution)/shard_map/ppermute | solution.py:161
  12.2 1.5 %collective-permute-start.8 = (bf16[128,1024]{1,0:T(8,128)(2,1)S(1)}, bf16[128,1024]{1,0:T(8,128)(2,1)S(1)}, u32[]{:S(2)}, u32[]{:S(2)}) collective-permute-start(bf16[128,1024]{1,0:T(8,128)(2,1)S(1)} %collective-permute-done.1.refs_2_), channel_id=1, source_target_pairs={{0,1},{1,0},{2,3},{3,2},{4,5},{5,4},{6,7},{7,6},{8,9},{9,8},{10,11... | collective-permute-start | bytes 786440 | tf_op jit(solution)/shard_map/ppermute | solution.py:169
  13.7 2.6 %collective-permute-start.2 = (bf16[128,1024]{1,0:T(8,128)(2,1)S(1)}, bf16[128,1024]{1,0:T(8,128)(2,1)S(1)}, u32[]{:S(2)}, u32[]{:S(2)}) collective-permute-start(bf16[128,1024]{1,0:T(8,128)(2,1)S(1)} %collective-permute-done.1.refs_2_), channel_id=1, source_target_pairs={{0,4},{1,5},{2,6},{3,7},{4,0},{5,1},{6,2},{7,3},{8,12},{9,13},{10,... | collective-permute-start | bytes 786440 | tf_op jit(solution)/shard_map/ppermute | solution.py:161
  16.3 5.3 %collective-permute-done.6.refs_0_ = bf16[128,1024]{1,0:T(8,128)(2,1)S(1)} collective-permute-done((bf16[128,1024]{1,0:T(8,128)(2,1)S(1)}, bf16[128,1024]{1,0:T(8,128)(2,1)S(1)}, u32[]{:S(2)}, u32[]{:S(2)}) %collective-permute-start.6) | collective-permute-done | bytes 262176 | tf_op jit(solution)/shard_map/ppermute | solution.py:161
  22.1 5.7 %shard_map.73 = (f32[1024,1024]{1,0:T(8,128)S(1)}, bf16[3,1024,1024]{2,1,0:T(8,128)(2,1)S(1)}) custom-call(bf16[3,1024,1024]{2,1,0:T(8,128)(2,1)} %factor_ref.1, bf16[128,1024]{1,0:T(8,128)(2,1)S(1)} %get-tuple-element.44.refs_0_, bf16[128,1024]{1,0:T(8,128)(2,1)S(1)} %collective-permute-done.refs_1_), custom_call_target="tpu_custom_call" | custom-call | flops 3221225472 | bytes 15204352 | tf_op jit(solution)/shard_map/pallas_call | solution.py:127
  27.9 1.9 %collective-permute-done.4.refs_2_ = bf16[128,1024]{1,0:T(8,128)(2,1)S(1)} collective-permute-done((bf16[128,1024]{1,0:T(8,128)(2,1)S(1)}, bf16[128,1024]{1,0:T(8,128)(2,1)S(1)}, u32[]{:S(2)}, u32[]{:S(2)}) %collective-permute-start.4) | collective-permute-done | bytes 262176 | tf_op jit(solution)/shard_map/ppermute | solution.py:161
  30.4 1.5 %collective-permute-start.11 = (bf16[128,1024]{1,0:T(8,128)(2,1)S(1)}, bf16[128,1024]{1,0:T(8,128)(2,1)S(1)}, u32[]{:S(2)}, u32[]{:S(2)}) collective-permute-start(bf16[128,1024]{1,0:T(8,128)(2,1)S(1)} %collective-permute-done.4.refs_2_), channel_id=1, source_target_pairs={{0,1},{1,0},{2,3},{3,2},{4,5},{5,4},{6,7},{7,6},{8,9},{9,8},{10,11... | collective-permute-start | bytes 786440 | tf_op jit(solution)/shard_map/ppermute | solution.py:169
  31.9 6.9 %shard_map.74.refs_4_ = f32[1024,1024]{1,0:T(8,128)S(1)} custom-call(bf16[3,1024,1024]{2,1,0:T(8,128)(2,1)S(1)} %get-tuple-element.19.factor_ref, bf16[128,1024]{1,0:T(8,128)(2,1)S(1)} %collective-permute-done.6.refs_0_, bf16[128,1024]{1,0:T(8,128)(2,1)S(1)} %collective-permute-done.7.refs_1_, ...), custom_call_target="tpu_custom_call", output_to_operand_aliasing={{}: (5, {})} | custom-call | flops 6442450944 | bytes 15728640 | tf_op jit(solution)/shard_map/pallas_call | solution.py:127
  38.8 2.1 %collective-permute-start.9 = (bf16[128,1024]{1,0:T(8,128)(2,1)S(1)}, bf16[128,1024]{1,0:T(8,128)(2,1)S(1)}, u32[]{:S(2)}, u32[]{:S(2)}) collective-permute-start(bf16[128,1024]{1,0:T(8,128)(2,1)S(1)} %collective-permute-done.2.refs_2_), channel_id=1, source_target_pairs={{0,2},{1,3},{2,0},{3,1},{4,6},{5,7},{6,4},{7,5},{8,10},{9,11},{10,... | collective-permute-start | bytes 786440 | tf_op jit(solution)/shard_map/ppermute | solution.py:161
  41.6 1.3 %collective-permute-done.11.refs_3_ = bf16[128,1024]{1,0:T(8,128)(2,1)S(1)} collective-permute-done((bf16[128,1024]{1,0:T(8,128)(2,1)S(1)}, bf16[128,1024]{1,0:T(8,128)(2,1)S(1)}, u32[]{:S(2)}, u32[]{:S(2)}) %collective-permute-start.11) | collective-permute-done | bytes 262176 | tf_op jit(solution)/shard_map/ppermute | solution.py:169
  42.9 7.1 %shard_map.75.refs_4_ = f32[1024,1024]{1,0:T(8,128)S(1)} custom-call(bf16[3,1024,1024]{2,1,0:T(8,128)(2,1)S(1)} %get-tuple-element.19.factor_ref, bf16[128,1024]{1,0:T(8,128)(2,1)S(1)} %collective-permute-done.3.refs_0_, bf16[128,1024]{1,0:T(8,128)(2,1)S(1)} %collective-permute-done.10.refs_1_, ...), custom_call_target="tpu_custom_call", output_to_operand_aliasing={{}: (5, {})} | custom-call | flops 6442450944 | bytes 15728640 | tf_op jit(solution)/shard_map/pallas_call | solution.py:127
  50.7 6.9 %shard_map.76.refs_2_ = f32[1024,1024]{1,0:T(8,128)S(1)} custom-call(bf16[3,1024,1024]{2,1,0:T(8,128)(2,1)S(1)} %get-tuple-element.19.factor_ref, bf16[128,1024]{1,0:T(8,128)(2,1)S(1)} %collective-permute-done.5.refs_0_, bf16[128,1024]{1,0:T(8,128)(2,1)S(1)} %collective-permute-done.13.refs_1_, ...), custom_call_target="tpu_custom_call", output_to_operand_aliasing={{}: (5, {})} | custom-call | flops 6442450944 | bytes 15728640 | tf_op jit(solution)/shard_map/pallas_call | solution.py:127
  57.7 3.5 %shard_map.77 = (bf16[4,128,512]{2,1,0:T(8,128)(2,1)S(1)}, bf16[2,256,512]{2,1,0:T(8,128)(2,1)S(1)}, f32[4,128,512]{2,1,0:T(8,128)S(1)}, f32[2,256,512]{2,1,0:T(8,128)S(1)}) custom-call(bf16[3,1024,1024]{2,1,0:T(8,128)(2,1)S(1)} %get-tuple-element.19.factor_ref, bf16[128,1024]{1,0:T(8,128)(2,1)S(1)} %collective-permute-done.9.refs_0_, ...), custom_call_target="tpu_custom_call" | custom-call | flops 3221225472 | bytes 15204352 | tf_op jit(solution)/shard_map/pallas_call | solution.py:127
  61.2 1.6 %collective-permute-start.15 = (bf16[4,128,512]{2,1,0:T(8,128)(2,1)S(1)}, bf16[4,128,512]{2,1,0:T(8,128)(2,1)}, u32[]{:S(2)}, u32[]{:S(2)}) collective-permute-start(bf16[4,128,512]{2,1,0:T(8,128)(2,1)S(1)} %get-tuple-element.30), channel_id=1, source_target_pairs={{0,1},{1,0},{2,3},{3,2},{4,5},{5,4},{6,7},{7,6},{8,9},{9,8},{10,11... | collective-permute-start | bytes 1572872 | tf_op jit(solution)/shard_map/ppermute | solution.py:169
  62.8 3.1 %collective-permute-start.18 = (bf16[2,256,512]{2,1,0:T(8,128)(2,1)S(1)}, bf16[2,256,512]{2,1,0:T(8,128)(2,1)}, u32[]{:S(2)}, u32[]{:S(2)}) collective-permute-start(bf16[2,256,512]{2,1,0:T(8,128)(2,1)S(1)} %get-tuple-element.32), channel_id=1, source_target_pairs={{0,2},{1,3},{2,0},{3,1},{4,6},{5,7},{6,4},{7,5},{8,10},{9,11},{10,... | collective-permute-start | bytes 1572872 | tf_op jit(solution)/shard_map/ppermute | solution.py:161
  66.4 5.0 %collective-permute-done.15 = bf16[4,128,512]{2,1,0:T(8,128)(2,1)} collective-permute-done((bf16[4,128,512]{2,1,0:T(8,128)(2,1)S(1)}, bf16[4,128,512]{2,1,0:T(8,128)(2,1)}, u32[]{:S(2)}, u32[]{:S(2)}) %collective-permute-start.15) | collective-permute-done | bytes 524320 | tf_op jit(solution)/shard_map/ppermute | solution.py:169
  72.4 2.8 %collective-permute-start.16 = (bf16[2,128,512]{2,1,0:T(8,128)(2,1)S(1)}, bf16[2,128,512]{2,1,0:T(8,128)(2,1)S(1)}, u32[]{:S(2)}, u32[]{:S(2)}) collective-permute-start(bf16[2,128,512]{2,1,0:T(8,128)(2,1)S(1)} %fusion.9), channel_id=1, source_target_pairs={{0,2},{1,3},{2,0},{3,1},{4,6},{5,7},{6,4},{7,5},{8,10},{9,11},{10,... | collective-permute-start | bytes 786440 | tf_op jit(solution)/shard_map/ppermute | solution.py:161
  77.1 1.7 %collective-permute-start.19 = (bf16[2,128,512]{2,1,0:T(8,128)(2,1)S(1)}, bf16[2,128,512]{2,1,0:T(8,128)(2,1)S(1)}, u32[]{:S(2)}, u32[]{:S(2)}) collective-permute-start(bf16[2,128,512]{2,1,0:T(8,128)(2,1)S(1)} %fusion.10), channel_id=1, source_target_pairs={{0,1},{1,0},{2,3},{3,2},{4,5},{5,4},{6,7},{7,6},{8,9},{9,8},{10,11... | collective-permute-start | bytes 786440 | tf_op jit(solution)/shard_map/ppermute | solution.py:169
  80.6 4.8 %collective-permute-start.17 = (bf16[128,512]{1,0:T(8,128)(2,1)S(1)}, bf16[128,512]{1,0:T(8,128)(2,1)S(1)}, u32[]{:S(2)}, u32[]{:S(2)}) collective-permute-start(bf16[128,512]{1,0:T(8,128)(2,1)S(1)} %fusion.15), channel_id=1, source_target_pairs={{0,4},{1,5},{2,6},{3,7},{4,0},{5,1},{6,2},{7,3},{8,12},{9,13},{10,... | collective-permute-start | bytes 393224 | tf_op jit(solution)/shard_map/ppermute | solution.py:161
  86.5 2.1 %collective-permute-start.20 = (bf16[128,512]{1,0:T(8,128)(2,1)S(1)}, bf16[128,512]{1,0:T(8,128)(2,1)S(1)}, u32[]{:S(2)}, u32[]{:S(2)}) collective-permute-start(bf16[128,512]{1,0:T(8,128)(2,1)S(1)} %fusion.16), channel_id=1, source_target_pairs={{0,4},{1,5},{2,6},{3,7},{4,0},{5,1},{6,2},{7,3},{8,12},{9,13},{10,... | collective-permute-start | bytes 393224 | tf_op jit(solution)/shard_map/ppermute | solution.py:161
  88.6 1.7 %collective-permute-done.17 = bf16[128,512]{1,0:T(8,128)(2,1)S(1)} collective-permute-done((bf16[128,512]{1,0:T(8,128)(2,1)S(1)}, bf16[128,512]{1,0:T(8,128)(2,1)S(1)}, u32[]{:S(2)}, u32[]{:S(2)}) %collective-permute-start.17) | collective-permute-done | bytes 131104 | tf_op jit(solution)/shard_map/ppermute | solution.py:161
  90.5 2.9 %collective-permute-done.20 = bf16[128,512]{1,0:T(8,128)(2,1)S(1)} collective-permute-done((bf16[128,512]{1,0:T(8,128)(2,1)S(1)}, bf16[128,512]{1,0:T(8,128)(2,1)S(1)}, u32[]{:S(2)}, u32[]{:S(2)}) %collective-permute-start.20) | collective-permute-done | bytes 131104 | tf_op jit(solution)/shard_map/ppermute | solution.py:161
  93.6 1.9 %collective-permute-start.21 = (bf16[4,128,128]{2,1,0:T(8,128)(2,1)S(1)}, bf16[4,128,128]{2,1,0:T(8,128)(2,1)S(1)}, u32[]{:S(2)}, u32[]{:S(2)}) collective-permute-start(bf16[4,128,128]{2,1,0:T(8,128)(2,1)S(1)} %dynamic-slice_bitcast_fusion.2), channel_id=1, source_target_pairs={{0,1},{1,0},{2,3},{3,2},{4,5},{5,4},{6,7},{7,6},{8,9},{9,8},{10,11... | collective-permute-start | bytes 393224 | tf_op jit(solution)/shard_map/ppermute | solution.py:169
  95.6 3.1 %collective-permute-done.21 = bf16[4,128,128]{2,1,0:T(8,128)(2,1)S(1)} collective-permute-done((bf16[4,128,128]{2,1,0:T(8,128)(2,1)S(1)}, bf16[4,128,128]{2,1,0:T(8,128)(2,1)S(1)}, u32[]{:S(2)}, u32[]{:S(2)}) %collective-permute-start.21) | collective-permute-done | bytes 131104 | tf_op jit(solution)/shard_map/ppermute | solution.py:169
  99.7 3.1 %collective-permute-start.24 = (bf16[128,256]{1,0:T(8,128)(2,1)S(1)}, bf16[128,256]{1,0:T(8,128)(2,1)S(1)}, u32[]{:S(2)}, u32[]{:S(2)}) collective-permute-start(bf16[128,256]{1,0:T(8,128)(2,1)S(1)} %get-tuple-element.49), channel_id=1, source_target_pairs={{0,20},{1,21},{2,22},{3,23},{4,16},{5,17},{6,18},{7,19},{8,28},{9,... | collective-permute-start | bytes 196616 | tf_op jit(solution)/shard_map/ppermute | solution.py:263
  102.8 2.9 %collective-permute-start.25 = (bf16[128,256]{1,0:T(8,128)(2,1)S(1)}, bf16[128,256]{1,0:T(8,128)(2,1)S(1)}, u32[]{:S(2)}, u32[]{:S(2)}) collective-permute-start(bf16[128,256]{1,0:T(8,128)(2,1)S(1)} %get-tuple-element.48), channel_id=1, source_target_pairs={{0,22},{1,23},{2,20},{3,21},{4,18},{5,19},{6,16},{7,17},{8,30},{9,... | collective-permute-start | bytes 196616 | tf_op jit(solution)/shard_map/ppermute | solution.py:263
  106.0 3.8 %collective-permute-done.25 = bf16[128,256]{1,0:T(8,128)(2,1)S(1)} collective-permute-done((bf16[128,256]{1,0:T(8,128)(2,1)S(1)}, bf16[128,256]{1,0:T(8,128)(2,1)S(1)}, u32[]{:S(2)}, u32[]{:S(2)}) %collective-permute-start.25) | collective-permute-done | bytes 65568 | tf_op jit(solution)/shard_map/ppermute | solution.py:263
  110.7 1.3 %fusion = f32[2,128,1024]{2,1,0:T(8,128)} fusion(f32[1,128,1024]{2,1,0:T(8,128)S(1)} %get-tuple-element.38, f32[1,128,1024]{2,1,0:T(8,128)S(1)} %get-tuple-element.37, f32[2]{0:T(128)S(1)} %add.140, f32[128,1024]{1,0:T(8,128)S(1)} %broadcast_add_fusion, s32[1024]{0:T(1024)S(1)} %copy-done.2, s32[2,128]{1,0:T(2,128)S(1)} %broadcast_xor_fusion), kind=kLoop, calls=%fused_computation.1 | loop fusion | flops 1572864 | bytes 2626568 | tf_op jit(solution)/shard_map/jit(_where)/select_n | solution.py:294
  (71 shorter events, 12.9 us)
Async XLA Ops:
  0.0 62.8 %copy-start = (s32[8,2]{0,1:T(2,128)S(1)}, s32[8,2]{0,1:T(2,128)}, u32[]{:S(2)}) copy-start(s32[8,2]{0,1:T(2,128)} %param.13) | copy-start | bytes 196
  1.1 9.3 %collective-permute-start.1 = (bf16[128,1024]{1,0:T(8,128)(2,1)S(1)}, bf16[128,1024]{1,0:T(8,128)(2,1)S(1)}, u32[]{:S(2)}, u32[]{:S(2)}) collective-permute-start(bf16[128,1024]{1,0:T(8,128)(2,1)S(1)} %get-tuple-element.43), channel_id=1, source_target_pairs={{0,16},{8,24},{16,0},{24,8},{1,17},{9,25},{17,1},{25,9},{2,18},{10... | collective-permute-start | bytes 786440 | tf_op jit(solution)/shard_map/ppermute | solution.py:164
  4.1 9.6 %collective-permute-start = (bf16[128,1024]{1,0:T(8,128)(2,1)S(1)}, bf16[128,1024]{1,0:T(8,128)(2,1)S(1)}, u32[]{:S(2)}, u32[]{:S(2)}) collective-permute-start(bf16[128,1024]{1,0:T(8,128)(2,1)S(1)} %get-tuple-element.44.refs_0_), channel_id=1, source_target_pairs={{0,1},{1,0},{2,3},{3,2},{4,5},{5,4},{6,7},{7,6},{8,9},{9,8},{10,11... | collective-permute-start | bytes 786440 | tf_op jit(solution)/shard_map/ppermute | solution.py:169
  5.6 16.0 %collective-permute-start.6 = (bf16[128,1024]{1,0:T(8,128)(2,1)S(1)}, bf16[128,1024]{1,0:T(8,128)(2,1)S(1)}, u32[]{:S(2)}, u32[]{:S(2)}) collective-permute-start(bf16[128,1024]{1,0:T(8,128)(2,1)S(1)} %get-tuple-element.44.refs_0_), channel_id=1, source_target_pairs={{0,2},{1,3},{2,0},{3,1},{4,6},{5,7},{6,4},{7,5},{8,10},{9,11},{10,... | collective-permute-start | bytes 786440 | tf_op jit(solution)/shard_map/ppermute | solution.py:161
  7.2 20.7 %collective-permute-start.3 = (bf16[128,1024]{1,0:T(8,128)(2,1)S(1)}, bf16[128,1024]{1,0:T(8,128)(2,1)S(1)}, u32[]{:S(2)}, u32[]{:S(2)}) collective-permute-start(bf16[128,1024]{1,0:T(8,128)(2,1)S(1)} %get-tuple-element.44.refs_0_), channel_id=1, source_target_pairs={{0,4},{1,5},{2,6},{3,7},{4,0},{5,1},{6,2},{7,3},{8,12},{9,13},{10,... | collective-permute-start | bytes 786440 | tf_op jit(solution)/shard_map/ppermute | solution.py:161
  10.4 19.4 %collective-permute-start.4 = (bf16[128,1024]{1,0:T(8,128)(2,1)S(1)}, bf16[128,1024]{1,0:T(8,128)(2,1)S(1)}, u32[]{:S(2)}, u32[]{:S(2)}) collective-permute-start(bf16[128,1024]{1,0:T(8,128)(2,1)S(1)} %collective-permute-done.1.refs_2_), channel_id=1, source_target_pairs={{0,2},{1,3},{2,0},{3,1},{4,6},{5,7},{6,4},{7,5},{8,10},{9,11},{10,... | collective-permute-start | bytes 786440 | tf_op jit(solution)/shard_map/ppermute | solution.py:161
  12.2 19.6 %collective-permute-start.8 = (bf16[128,1024]{1,0:T(8,128)(2,1)S(1)}, bf16[128,1024]{1,0:T(8,128)(2,1)S(1)}, u32[]{:S(2)}, u32[]{:S(2)}) collective-permute-start(bf16[128,1024]{1,0:T(8,128)(2,1)S(1)} %collective-permute-done.1.refs_2_), channel_id=1, source_target_pairs={{0,1},{1,0},{2,3},{3,2},{4,5},{5,4},{6,7},{7,6},{8,9},{9,8},{10,11... | collective-permute-start | bytes 786440 | tf_op jit(solution)/shard_map/ppermute | solution.py:169
  13.7 25.1 %collective-permute-start.2 = (bf16[128,1024]{1,0:T(8,128)(2,1)S(1)}, bf16[128,1024]{1,0:T(8,128)(2,1)S(1)}, u32[]{:S(2)}, u32[]{:S(2)}) collective-permute-start(bf16[128,1024]{1,0:T(8,128)(2,1)S(1)} %collective-permute-done.1.refs_2_), channel_id=1, source_target_pairs={{0,4},{1,5},{2,6},{3,7},{4,0},{5,1},{6,2},{7,3},{8,12},{9,13},{10,... | collective-permute-start | bytes 786440 | tf_op jit(solution)/shard_map/ppermute | solution.py:161
  21.6 8.8 %collective-permute-start.7 = (bf16[128,1024]{1,0:T(8,128)(2,1)S(1)}, bf16[128,1024]{1,0:T(8,128)(2,1)S(1)}, u32[]{:S(2)}, u32[]{:S(2)}) collective-permute-start(bf16[128,1024]{1,0:T(8,128)(2,1)S(1)} %collective-permute-done.6.refs_0_), channel_id=1, source_target_pairs={{0,1},{1,0},{2,3},{3,2},{4,5},{5,4},{6,7},{7,6},{8,9},{9,8},{10,11... | collective-permute-start | bytes 786440 | tf_op jit(solution)/shard_map/ppermute | solution.py:169
  29.8 9.0 %collective-permute-start.5 = (bf16[128,1024]{1,0:T(8,128)(2,1)S(1)}, bf16[128,1024]{1,0:T(8,128)(2,1)S(1)}, u32[]{:S(2)}, u32[]{:S(2)}) collective-permute-start(bf16[128,1024]{1,0:T(8,128)(2,1)S(1)} %collective-permute-done.3.refs_0_), channel_id=1, source_target_pairs={{0,2},{1,3},{2,0},{3,1},{4,6},{5,7},{6,4},{7,5},{8,10},{9,11},{10,... | collective-permute-start | bytes 786440 | tf_op jit(solution)/shard_map/ppermute | solution.py:161
  29.8 11.6 %collective-permute-start.10 = (bf16[128,1024]{1,0:T(8,128)(2,1)S(1)}, bf16[128,1024]{1,0:T(8,128)(2,1)S(1)}, u32[]{:S(2)}, u32[]{:S(2)}) collective-permute-start(bf16[128,1024]{1,0:T(8,128)(2,1)S(1)} %collective-permute-done.3.refs_0_), channel_id=1, source_target_pairs={{0,1},{1,0},{2,3},{3,2},{4,5},{5,4},{6,7},{7,6},{8,9},{9,8},{10,11... | collective-permute-start | bytes 786440 | tf_op jit(solution)/shard_map/ppermute | solution.py:169
  30.4 12.5 %collective-permute-start.11 = (bf16[128,1024]{1,0:T(8,128)(2,1)S(1)}, bf16[128,1024]{1,0:T(8,128)(2,1)S(1)}, u32[]{:S(2)}, u32[]{:S(2)}) collective-permute-start(bf16[128,1024]{1,0:T(8,128)(2,1)S(1)} %collective-permute-done.4.refs_2_), channel_id=1, source_target_pairs={{0,1},{1,0},{2,3},{3,2},{4,5},{5,4},{6,7},{7,6},{8,9},{9,8},{10,11... | collective-permute-start | bytes 786440 | tf_op jit(solution)/shard_map/ppermute | solution.py:169
  38.8 11.2 %collective-permute-start.9 = (bf16[128,1024]{1,0:T(8,128)(2,1)S(1)}, bf16[128,1024]{1,0:T(8,128)(2,1)S(1)}, u32[]{:S(2)}, u32[]{:S(2)}) collective-permute-start(bf16[128,1024]{1,0:T(8,128)(2,1)S(1)} %collective-permute-done.2.refs_2_), channel_id=1, source_target_pairs={{0,2},{1,3},{2,0},{3,1},{4,6},{5,7},{6,4},{7,5},{8,10},{9,11},{10,... | collective-permute-start | bytes 786440 | tf_op jit(solution)/shard_map/ppermute | solution.py:161
  40.9 9.7 %collective-permute-start.14 = (bf16[128,1024]{1,0:T(8,128)(2,1)S(1)}, bf16[128,1024]{1,0:T(8,128)(2,1)S(1)}, u32[]{:S(2)}, u32[]{:S(2)}) collective-permute-start(bf16[128,1024]{1,0:T(8,128)(2,1)S(1)} %collective-permute-done.2.refs_2_), channel_id=1, source_target_pairs={{0,1},{1,0},{2,3},{3,2},{4,5},{5,4},{6,7},{7,6},{8,9},{9,8},{10,11... | collective-permute-start | bytes 786440 | tf_op jit(solution)/shard_map/ppermute | solution.py:169
  41.5 9.2 %collective-permute-start.13 = (bf16[128,1024]{1,0:T(8,128)(2,1)S(1)}, bf16[128,1024]{1,0:T(8,128)(2,1)S(1)}, u32[]{:S(2)}, u32[]{:S(2)}) collective-permute-start(bf16[128,1024]{1,0:T(8,128)(2,1)S(1)} %collective-permute-done.10.refs_1_), channel_id=1, source_target_pairs={{0,2},{1,3},{2,0},{3,1},{4,6},{5,7},{6,4},{7,5},{8,10},{9,11},{10,... | collective-permute-start | bytes 786440 | tf_op jit(solution)/shard_map/ppermute | solution.py:161
  50.1 7.6 %collective-permute-start.12 = (bf16[128,1024]{1,0:T(8,128)(2,1)S(1)}, bf16[128,1024]{1,0:T(8,128)(2,1)S(1)}, u32[]{:S(2)}, u32[]{:S(2)}) collective-permute-start(bf16[128,1024]{1,0:T(8,128)(2,1)S(1)} %collective-permute-done.9.refs_0_), channel_id=1, source_target_pairs={{0,1},{1,0},{2,3},{3,2},{4,5},{5,4},{6,7},{7,6},{8,9},{9,8},{10,11... | collective-permute-start | bytes 786440 | tf_op jit(solution)/shard_map/ppermute | solution.py:169
  57.6 8.4 %copy-start.2 = (s32[1024]{0:T(1024)S(1)}, s32[1024]{0:T(1024)}, u32[]{:S(2)}) copy-start(s32[1024]{0:T(1024)} %param.12) | copy-start | bytes 12292
  57.6 8.4 %copy-start.1 = (f32[1024]{0:T(1024)S(1)}, f32[1024]{0:T(1024)}, u32[]{:S(2)}) copy-start(f32[1024]{0:T(1024)} %param.10) | copy-start | bytes 12292
  57.6 8.5 %copy-start.3 = (s32[100]{0:T(128)S(1)}, s32[100]{0:T(128)}, u32[]{:S(2)}) copy-start(s32[100]{0:T(128)} %param.11) | copy-start | bytes 1204
  61.2 10.1 %collective-permute-start.15 = (bf16[4,128,512]{2,1,0:T(8,128)(2,1)S(1)}, bf16[4,128,512]{2,1,0:T(8,128)(2,1)}, u32[]{:S(2)}, u32[]{:S(2)}) collective-permute-start(bf16[4,128,512]{2,1,0:T(8,128)(2,1)S(1)} %get-tuple-element.30), channel_id=1, source_target_pairs={{0,1},{1,0},{2,3},{3,2},{4,5},{5,4},{6,7},{7,6},{8,9},{9,8},{10,11... | collective-permute-start | bytes 1572872 | tf_op jit(solution)/shard_map/ppermute | solution.py:169
  62.8 13.2 %collective-permute-start.18 = (bf16[2,256,512]{2,1,0:T(8,128)(2,1)S(1)}, bf16[2,256,512]{2,1,0:T(8,128)(2,1)}, u32[]{:S(2)}, u32[]{:S(2)}) collective-permute-start(bf16[2,256,512]{2,1,0:T(8,128)(2,1)S(1)} %get-tuple-element.32), channel_id=1, source_target_pairs={{0,2},{1,3},{2,0},{3,1},{4,6},{5,7},{6,4},{7,5},{8,10},{9,11},{10,... | collective-permute-start | bytes 1572872 | tf_op jit(solution)/shard_map/ppermute | solution.py:161
  72.4 7.1 %collective-permute-start.16 = (bf16[2,128,512]{2,1,0:T(8,128)(2,1)S(1)}, bf16[2,128,512]{2,1,0:T(8,128)(2,1)S(1)}, u32[]{:S(2)}, u32[]{:S(2)}) collective-permute-start(bf16[2,128,512]{2,1,0:T(8,128)(2,1)S(1)} %fusion.9), channel_id=1, source_target_pairs={{0,2},{1,3},{2,0},{3,1},{4,6},{5,7},{6,4},{7,5},{8,10},{9,11},{10,... | collective-permute-start | bytes 786440 | tf_op jit(solution)/shard_map/ppermute | solution.py:161
  77.1 8.3 %collective-permute-start.19 = (bf16[2,128,512]{2,1,0:T(8,128)(2,1)S(1)}, bf16[2,128,512]{2,1,0:T(8,128)(2,1)S(1)}, u32[]{:S(2)}, u32[]{:S(2)}) collective-permute-start(bf16[2,128,512]{2,1,0:T(8,128)(2,1)S(1)} %fusion.10), channel_id=1, source_target_pairs={{0,1},{1,0},{2,3},{3,2},{4,5},{5,4},{6,7},{7,6},{8,9},{9,8},{10,11... | collective-permute-start | bytes 786440 | tf_op jit(solution)/shard_map/ppermute | solution.py:169
  80.5 25.2 %copy-start.4 = (f32[100]{0:T(128)S(1)}, f32[100]{0:T(128)}, u32[]{:S(2)}) copy-start(f32[100]{0:T(128)} %param.9) | copy-start | bytes 1204
  80.6 9.7 %collective-permute-start.17 = (bf16[128,512]{1,0:T(8,128)(2,1)S(1)}, bf16[128,512]{1,0:T(8,128)(2,1)S(1)}, u32[]{:S(2)}, u32[]{:S(2)}) collective-permute-start(bf16[128,512]{1,0:T(8,128)(2,1)S(1)} %fusion.15), channel_id=1, source_target_pairs={{0,4},{1,5},{2,6},{3,7},{4,0},{5,1},{6,2},{7,3},{8,12},{9,13},{10,... | collective-permute-start | bytes 393224 | tf_op jit(solution)/shard_map/ppermute | solution.py:161
  86.5 6.9 %collective-permute-start.20 = (bf16[128,512]{1,0:T(8,128)(2,1)S(1)}, bf16[128,512]{1,0:T(8,128)(2,1)S(1)}, u32[]{:S(2)}, u32[]{:S(2)}) collective-permute-start(bf16[128,512]{1,0:T(8,128)(2,1)S(1)} %fusion.16), channel_id=1, source_target_pairs={{0,4},{1,5},{2,6},{3,7},{4,0},{5,1},{6,2},{7,3},{8,12},{9,13},{10,... | collective-permute-start | bytes 393224 | tf_op jit(solution)/shard_map/ppermute | solution.py:161
  93.6 5.0 %collective-permute-start.21 = (bf16[4,128,128]{2,1,0:T(8,128)(2,1)S(1)}, bf16[4,128,128]{2,1,0:T(8,128)(2,1)S(1)}, u32[]{:S(2)}, u32[]{:S(2)}) collective-permute-start(bf16[4,128,128]{2,1,0:T(8,128)(2,1)S(1)} %dynamic-slice_bitcast_fusion.2), channel_id=1, source_target_pairs={{0,1},{1,0},{2,3},{3,2},{4,5},{5,4},{6,7},{7,6},{8,9},{9,8},{10,11... | collective-permute-start | bytes 393224 | tf_op jit(solution)/shard_map/ppermute | solution.py:169
  98.9 7.0 %collective-permute-start.22 = (bf16[128,256]{1,0:T(8,128)(2,1)S(1)}, bf16[128,256]{1,0:T(8,128)(2,1)S(1)}, u32[]{:S(2)}, u32[]{:S(2)}) collective-permute-start(bf16[128,256]{1,0:T(8,128)(2,1)S(1)} %get-tuple-element.47), channel_id=1, source_target_pairs={{0,16},{1,17},{2,18},{3,19},{4,20},{5,21},{6,22},{7,23},{8,24},{9,... | collective-permute-start | bytes 196616 | tf_op jit(solution)/shard_map/ppermute | solution.py:263
  99.5 6.5 %collective-permute-start.23 = (bf16[128,256]{1,0:T(8,128)(2,1)S(1)}, bf16[128,256]{1,0:T(8,128)(2,1)S(1)}, u32[]{:S(2)}, u32[]{:S(2)}) collective-permute-start(bf16[128,256]{1,0:T(8,128)(2,1)S(1)} %get-tuple-element.50), channel_id=1, source_target_pairs={{0,18},{1,19},{2,16},{3,17},{4,22},{5,23},{6,20},{7,21},{8,26},{9,... | collective-permute-start | bytes 196616 | tf_op jit(solution)/shard_map/ppermute | solution.py:263
  99.7 6.3 %collective-permute-start.24 = (bf16[128,256]{1,0:T(8,128)(2,1)S(1)}, bf16[128,256]{1,0:T(8,128)(2,1)S(1)}, u32[]{:S(2)}, u32[]{:S(2)}) collective-permute-start(bf16[128,256]{1,0:T(8,128)(2,1)S(1)} %get-tuple-element.49), channel_id=1, source_target_pairs={{0,20},{1,21},{2,22},{3,23},{4,16},{5,17},{6,18},{7,19},{8,28},{9,... | collective-permute-start | bytes 196616 | tf_op jit(solution)/shard_map/ppermute | solution.py:263
  102.8 7.0 %collective-permute-start.25 = (bf16[128,256]{1,0:T(8,128)(2,1)S(1)}, bf16[128,256]{1,0:T(8,128)(2,1)S(1)}, u32[]{:S(2)}, u32[]{:S(2)}) collective-permute-start(bf16[128,256]{1,0:T(8,128)(2,1)S(1)} %get-tuple-element.48), channel_id=1, source_target_pairs={{0,22},{1,23},{2,20},{3,21},{4,18},{5,19},{6,16},{7,17},{8,30},{9,... | collective-permute-start | bytes 196616 | tf_op jit(solution)/shard_map/ppermute | solution.py:263

commit v2 on v1

v2 whole, which is shorter than its diff:
```python
import functools

import jax
import jax.numpy as jnp
from jax import lax
from jax.experimental import pallas as pl
from jax.experimental.pallas import tpu as pltpu
from jax.sharding import PartitionSpec as P

GROUP_ROWS = 256
VMEM_MIB = 16


def dot_nt(left, right):
    return lax.dot_general(left, right, (((1,), (1,)), ((), ())), preferred_element_type=jnp.float32)


def ladder_kernel(distances, kept_count, has_sums, loads, factor_ref, *refs):
    block_count = len(distances)
    vir_index = lax.axis_index("vir")
    z_index = vir_index // 2
    x_index = vir_index % 2
    z_low = z_index % 2
    pair_refs, refs = refs[: 2 * block_count], refs[2 * block_count :]
    before_refs = ()
    if has_sums:
        before_refs, refs = refs[:2], refs[2:]
    sent_x_ref, sent_z_ref, keep_x_ref, keep_z_ref, right_ref = refs[:5]
    refs = refs[5:]
    loading = []
    if loads:
        source_ref, factor_ref, factor_sem, refs = factor_ref, refs[0], refs[4], refs[1:4]
        for q in range(factor_ref.shape[0]):
            loading.append(pltpu.make_async_copy(source_ref.at[q], factor_ref.at[q], factor_sem.at[q]))
            loading[q].start()
    rows_ref, left_x_ref, left_z_ref = refs
    factor_count, size, _ = factor_ref.shape
    half = pair_refs[0].shape[0]
    width = block_count * GROUP_ROWS
    middle = size // 2

    for block in range(block_count):
        first = block * GROUP_ROWS + x_index * half
        second = block * GROUP_ROWS + (1 - x_index) * half
        rows_ref[pl.ds(pl.multiple_of(first, half), half), :] = pair_refs[2 * block][...]
        rows_ref[pl.ds(pl.multiple_of(second, half), half), :] = pair_refs[2 * block + 1][...]

    for q in range(factor_count):
        if loads:
            loading[q].wait()
        if block_count == 1:
            halves = dot_nt(rows_ref[...], factor_ref[q]).T.astype(jnp.bfloat16)
        else:
            halves = dot_nt(factor_ref[q], rows_ref[...]).astype(jnp.bfloat16)
        for block in range(block_count):
            column = pl.multiple_of((z_index ^ distances[block]) * GROUP_ROWS, GROUP_ROWS)
            taken = factor_ref[q, :, pl.ds(column, GROUP_ROWS)]
            made = halves[:, block * GROUP_ROWS : (block + 1) * GROUP_ROWS]
            target = pl.ds(q * width + block * GROUP_ROWS, GROUP_ROWS)
            left, right = (taken, made) if block < kept_count else (made, taken)
            right_ref[:, target] = right
            for start in range(0, size, 2 * half):
                low, high = left[start : start + half], left[start + half : start + 2 * half]
                here = pl.ds(start // 2, half)
                left_x_ref[here, target] = jnp.where(x_index == 0, high, low)
                keep_x_ref[here, target] = jnp.where(x_index == 0, low, high)
            for start in range(0, size, 2 * GROUP_ROWS):
                low = left[start : start + GROUP_ROWS]
                high = left[start + GROUP_ROWS : start + 2 * GROUP_ROWS]
                here = pl.ds(start // 2, GROUP_ROWS)
                left_z_ref[here, target] = jnp.where(z_low == 0, high, low)
                keep_z_ref[here, target] = jnp.where(z_low == 0, low, high)

    for number, (left_ref, out_ref) in enumerate(((left_x_ref, sent_x_ref), (left_z_ref, sent_z_ref))):
        product = dot_nt(left_ref[...], right_ref[pl.ds(number * middle, middle), :])
        if has_sums:
            product = product + before_refs[number][...]
        out_ref[...] = product.astype(out_ref.dtype)


def ladder(distances, factors, kept, swapped, sums=None, loads=False, last=False):
    factor_count, size, _ = factors.shape
    pairs = list(kept) + list(swapped)
    width = len(pairs) * GROUP_ROWS
    depth = factor_count * width
    middle = size // 2
    whole = pl.BlockSpec(memory_space=pltpu.VMEM)
    operands = [factors] + [half_block for pair in pairs for half_block in pair]
    aliases = {}
    if sums is not None:
        if not last:
            aliases = {len(operands): 0, len(operands) + 1: 1}
        operands += list(sums)
    in_specs = [whole] * len(operands)
    kind = jnp.bfloat16 if last else jnp.float32
    out_shape = [jax.ShapeDtypeStruct((middle, middle), kind)] * 2
    out_shape += [jax.ShapeDtypeStruct((rows, depth), jnp.bfloat16) for rows in (middle, middle, size)]
    scratch = [
        pltpu.VMEM((width, size), jnp.bfloat16),
        pltpu.VMEM((middle, depth), jnp.bfloat16),
        pltpu.VMEM((middle, depth), jnp.bfloat16),
    ]
    if loads:
        operands[0] = pltpu.with_memory_space_constraint(factors, pltpu.HBM)
        in_specs[0] = pl.BlockSpec(memory_space=pl.ANY)
        out_shape.append(jax.ShapeDtypeStruct(factors.shape, factors.dtype))
        scratch.append(pltpu.SemaphoreType.DMA((factor_count,)))
    out = pl.pallas_call(
        functools.partial(ladder_kernel, distances, len(kept), sums is not None, loads),
        out_shape=out_shape,
        in_specs=in_specs,
        out_specs=[whole] * len(out_shape),
        scratch_shapes=scratch,
        input_output_aliases=aliases,
        compiler_params=pltpu.CompilerParams(vmem_limit_bytes=VMEM_MIB * 1024 * 1024),
        cost_estimate=pl.CostEstimate(
            flops=(0 if loads else 3) * factor_count * width * size * size,
            bytes_accessed=2 * factor_count * size * size + 4 * size * size + 2 * width * size,
            transcendentals=0,
        ),
    )(*operands)
    return out[:2], tuple(out[2:5]), out[5:]


def keep_kernel(count, *refs):
    factors_refs, out_refs = refs[: 3 * count], refs[3 * count :]
    middle = out_refs[0].shape[0]
    for number, out_ref in enumerate(out_refs):
        total = None
        for part in range(count):
            left_ref, right_ref = factors_refs[3 * part + number], factors_refs[3 * part + 2]
            product = dot_nt(left_ref[...], right_ref[pl.ds(number * middle, middle), :])
            total = product if total is None else total + product
        out_ref[...] = total


def keep_sums(parts):
    middle = parts[0][0].shape[0]
    operands = [array for part in parts for array in part]
    whole = pl.BlockSpec(memory_space=pltpu.VMEM)
    return pl.pallas_call(
        functools.partial(keep_kernel, len(parts)),
        out_shape=[jax.ShapeDtypeStruct((middle, middle), jnp.float32)] * 2,
        in_specs=[whole] * len(operands),
        out_specs=[whole] * 2,
        compiler_params=pltpu.CompilerParams(vmem_limit_bytes=VMEM_MIB * 1024 * 1024),
        cost_estimate=pl.CostEstimate(
            flops=4 * middle * middle * sum(part[0].shape[1] for part in parts),
            bytes_accessed=2 * sum(array.size for array in operands) + 8 * middle * middle,
            transcendentals=0,
        ),
    )(*operands)


def per_device(amplitudes, factors, occ_energy, vir_energy, occ_irrep, vir_irrep, pair_orbitals):
    local_pairs, row_count, size = amplitudes.shape
    occ_total = occ_energy.shape[0]
    occ_devices = lax.axis_size("occ")
    vir_devices = lax.axis_size("vir")
    inner = GROUP_ROWS // row_count
    outer = vir_devices // inner
    assert local_pairs == 2 and outer == 4 and inner * row_count == GROUP_ROWS
    occ_index = lax.axis_index("occ")
    vir_index = lax.axis_index("vir")
    z_index = vir_index // inner
    x_index = vir_index % inner
    side = occ_index // (occ_devices // 2)
    across = occ_devices // 2

    def z_swap(block, distance):
        route = [(i, (i // inner ^ distance) * inner + i % inner) for i in range(vir_devices)]
        return lax.ppermute(block, "vir", route)

    def y_swap(block):
        return lax.ppermute(block, "occ", [(i, (i + across) % occ_devices) for i in range(occ_devices)])

    inner_groups = [[g * inner + i for i in range(inner)] for g in range(outer)]

    def x_swap(block):
        return lax.ppermute(block, "vir", [(i, i ^ 1) for i in range(vir_devices)])

    def x_pair(block):
        return block, x_swap(block)

    def x_scatter(sums):
        return lax.psum_scatter(sums, "vir", scatter_dimension=1, axis_index_groups=inner_groups)

    def z_scatter(sums, axis, distance, bit):
        sent = lax.dynamic_index_in_dim(sums, 1 - bit, axis, keepdims=False).astype(jnp.bfloat16)
        own = lax.dynamic_index_in_dim(sums, bit, axis, keepdims=False)
        return own + z_swap(sent, distance).astype(jnp.float32)

    def halved(own, came, bit, swap):
        came = came.reshape(own.shape)

        def half(index):
            mine = lax.dynamic_index_in_dim(own, index, 1, keepdims=False)
            theirs = lax.dynamic_index_in_dim(came, index, 1, keepdims=False)
            return mine + theirs.astype(jnp.float32)

        return half(bit) + swap(half(1 - bit).astype(jnp.bfloat16)).astype(jnp.float32)

    z_high = z_index // 2
    z_low = z_index % 2

    kept_0 = lax.dynamic_index_in_dim(amplitudes, side, 0, keepdims=False)
    given = lax.dynamic_index_in_dim(amplitudes, 1 - side, 0, keepdims=False)
    swapped_0 = y_swap(given)
    def step(distance, kept, swapped, total):
        return ladder((distance,), inner, factors, kept, swapped, total)

    after = lax.optimization_barrier
    middle = size // 2
    if inner == 2:
        kept_2 = z_swap(kept_0, 2)
        kept_1 = z_swap(kept_0, 1)
        kept_pair_0 = x_pair(kept_0)
        swapped_2 = z_swap(swapped_0, 2)
        swapped_1 = z_swap(swapped_0, 1)
        swapped_pair_0 = x_pair(swapped_0)
        kept_pair_1 = x_pair(kept_1)
        sums, part_0, (factors,) = ladder((0,), factors, [kept_pair_0], [], loads=True)
        kept_2, swapped_1, sums = after((kept_2, swapped_1, sums))
        kept_3 = z_swap(kept_2, 1)
        kept_pair_2 = x_pair(kept_2)
        swapped_pair_1 = x_pair(swapped_1)
        sums, part_1, _ = ladder((1, 0), factors, [kept_pair_1], [swapped_pair_0], sums)
        swapped_2, kept_3, sums = after((swapped_2, kept_3, sums))
        swapped_3 = z_swap(swapped_2, 1)
        swapped_pair_2 = x_pair(swapped_2)
        kept_pair_3 = (kept_3, z_swap(kept_pair_2[1], 1))
        sums, part_2, _ = ladder((2, 1), factors, [kept_pair_2], [swapped_pair_1], sums)
        swapped_3, sums = after((swapped_3, sums))
        swapped_pair_3 = x_pair(swapped_3)
        sums, part_3, _ = ladder((3, 2), factors, [kept_pair_3], [swapped_pair_2], sums)
        sent, part_4, _ = ladder((3,), factors, [], [swapped_pair_3], sums, last=True)
        own_x, own_z = keep_sums([part_0, part_1, part_2, part_3, part_4])
        shape = (2, 2, row_count, middle)
        left = halved(own_x.reshape(shape), x_swap(sent[0]), z_low, lambda b: z_swap(b, 1))
        right = halved(own_z.reshape(shape), z_swap(sent[1], 1), x_index, x_swap)
    else:
        kept_all = lax.all_gather(kept_0, "vir", axis=0, tiled=True)
        swapped_all = lax.all_gather(swapped_0, "vir", axis=0, tiled=True)
        kept_halves = jnp.einsum("cd,qbd->qcb", kept_all, factors, preferred_element_type=jnp.float32)
        swapped_halves = jnp.einsum("cd,qad->qca", swapped_all, factors, preferred_element_type=jnp.float32)
        total = jnp.einsum(
            "qac,qcb->ab", factors, kept_halves.astype(jnp.bfloat16), preferred_element_type=jnp.float32
        ) + jnp.einsum(
            "qca,qbc->ab", swapped_halves.astype(jnp.bfloat16), factors, preferred_element_type=jnp.float32
        )
        left = x_scatter(total[:, :middle].reshape(4, inner, row_count, middle))
        left = z_scatter(left.reshape(2, 2, row_count, middle), 1, 1, z_low)
        right = z_scatter(total[:, middle:].reshape(2, 2, GROUP_ROWS, middle), 1, 1, z_low)
        right = x_scatter(right.reshape(2, inner, row_count, middle))
    own_rows = jnp.concatenate([z_scatter(left, 0, 2, z_high), z_scatter(right, 0, 2, z_high)], axis=1)

    packed = own_rows.astype(jnp.bfloat16).reshape(row_count, vir_devices, row_count)
    packed = jnp.transpose(packed, (1, 2, 0))
    if inner == 2:
        def flipped(blocks):
            blocks = blocks.reshape(2, 2, *blocks.shape[1:])
            blocks = jnp.where(z_high == 1, jnp.flip(blocks, 0), blocks)
            blocks = jnp.where(z_low == 1, jnp.flip(blocks, 1), blocks)
            return blocks.reshape(4, *blocks.shape[2:])

        packed = packed.reshape(4, 2, row_count, row_count)
        stays = lax.dynamic_index_in_dim(packed, x_index, 1, keepdims=False)
        leaves = lax.dynamic_index_in_dim(packed, 1 - x_index, 1, keepdims=False)
        came = x_swap(leaves)
        first = jnp.where(x_index == 0, stays, came)
        second = jnp.where(x_index == 0, came, stays)
        turned = flipped(jnp.concatenate([first, second], axis=2))
        came = []
        for step in range(4):
            route = [
                (o * vir_devices + i, ((o + across) % occ_devices) * vir_devices + (i ^ 2 * step))
                for o in range(occ_devices)
                for i in range(vir_devices)
            ]
            came.append(lax.ppermute(turned[step], ("occ", "vir"), route))
        partner = flipped(jnp.stack(came))
    else:
        partner = y_swap(lax.all_to_all(packed, "vir", 0, 0))
    partner = jnp.transpose(partner, (1, 0, 2)).reshape(row_count, size).astype(jnp.float32)

    first = jnp.where(side == 0, own_rows, partner)
    second = jnp.where(side == 0, partner, own_rows)
    numerator = jnp.stack([first, second])

    pair_ids = lax.dynamic_slice_in_dim(pair_orbitals, occ_index * local_pairs, local_pairs, 0)
    row_start = vir_index * row_count
    energy_rows = lax.dynamic_slice_in_dim(vir_energy, row_start, row_count, 0)
    irrep_rows = lax.dynamic_slice_in_dim(vir_irrep, row_start, row_count, 0)
    positions = jnp.arange(occ_total, dtype=jnp.int32)
    first_hot = positions[None, :] == pair_ids[:, 0:1]
    second_hot = positions[None, :] == pair_ids[:, 1:2]
    pair_energy = jnp.sum(jnp.where(first_hot, occ_energy[None, :], 0.0), axis=1) + jnp.sum(
        jnp.where(second_hot, occ_energy[None, :], 0.0), axis=1
    )
    first_irrep = jnp.sum(jnp.where(first_hot, occ_irrep[None, :], 0), axis=1)
    second_irrep = jnp.sum(jnp.where(second_hot, occ_irrep[None, :], 0), axis=1)
    pair_sym = jnp.bitwise_xor(first_irrep, second_irrep)
    combined = jnp.bitwise_xor(
        jnp.bitwise_xor(pair_sym[:, None, None], irrep_rows[None, :, None]),
        vir_irrep[None, None, :],
    )
    allowed = combined == 0
    denominator = (
        energy_rows[None, :, None] + vir_energy[None, None, :] - pair_energy[:, None, None]
    )
    return jnp.where(allowed, numerator / denominator, jnp.float32(0.0))


def solution(mesh):
    return jax.shard_map(
        per_device,
        mesh=mesh,
        in_specs=(P("occ", "vir", None), P("vir", None, None), P(), P(), P(), P(), P()),
        out_specs=P("occ", "vir", None),
        check_vma=False,
    )
```

time: 112 us -> 106 us (0.946)
  waiting for transfers between devices: 27.2 us -> 22.4 us
  other arithmetic: 6.56 us -> 3.38 us
  local copies, waits for them, and re-layouts: 2.28 us -> 3.94 us
    ppermute x10, starting transfers between devices: 11.8 us -> 14.1 us  [x_swap(): return lax.ppermute(block, 'vir', [(i, i ^ 1) for i in range(vir_devices)])]
    ppermute x11, starting transfers between devices: 23.6 us -> 21.5 us  [z_swap(): return lax.ppermute(block, 'vir', route)]
    convert_element_type x2, other arithmetic: 2.06 us -> 0.14 us  [halved(): half(1 - bit).astype(jnp.bfloat16)]
    add x2, other arithmetic: 2.1 us -> 0.19 us  [halved(): half(bit) + swap(half(1 - bit).astype(jnp.bfloat16)).astype(jnp.float32)]
    ppermute x10, waiting for transfers between devices: 9.39 us -> 7.86 us  [x_swap(): return lax.ppermute(block, 'vir', [(i, i ^ 1) for i in range(vir_devices)])]
    ppermute x11, waiting for transfers between devices: 13.4 us -> 12 us  [z_swap(): return lax.ppermute(block, 'vir', route)]
    ppermute x4, waiting for transfers between devices: 3.81 us -> 2.51 us  [per_device(): came.append(lax.ppermute(turned[step], ('occ', 'vir'), route))]
    pallas_call x5 -> x6, Pallas kernels: 30.3 us -> 30.4 us  [the longest x5 23.7 us: ladder(): pl.pallas_call(functools.partial(ladder_kernel, distances, len(kept), sum...]
  transfers between devices with their start and end apart: 26 -> 26, of which waited for: 11 -> 10; matrix products, arithmetic and copies ran while one was open for 5% -> 3% of each run, Pallas kernels for 24% -> 26%
where the time goes in v2:
time: 106 us
  starting transfers between devices  45.4 us (43%)
  Pallas kernels  30.4 us (29%)
  waiting for transfers between devices  22.4 us (21%)
  local copies, waits for them, and re-layouts  3.94 us (4%)
  other arithmetic  3.38 us (3%)
    pallas_call x5, Pallas kernels, ladder(): pl.pallas_call(functools.partial(ladder_kernel, distances, len(kept), sum...  23.7 us
    ppermute x11, starting transfers between devices, z_swap(): return lax.ppermute(block, 'vir', route)  21.5 us
    ppermute x10, starting transfers between devices, x_swap(): return lax.ppermute(block, 'vir', [(i, i ^ 1) for i in range(vir_devices)])  14.1 us
    ppermute x11, waiting for transfers between devices, z_swap(): return lax.ppermute(block, 'vir', route)  12 us
    ppermute x10, waiting for transfers between devices, x_swap(): return lax.ppermute(block, 'vir', [(i, i ^ 1) for i in range(vir_devices)])  7.86 us
    ppermute x4, starting transfers between devices, per_device(): came.append(lax.ppermute(turned[step], ('occ', 'vir'), route))  6.81 us
    pallas_call x1, Pallas kernels, keep_sums(): pl.pallas_call(functools.partial(keep_kernel, len(parts)), out_shape=[jax...  6.67 us
    ppermute x1, starting transfers between devices, y_swap(): lax.ppermute(block, 'occ', [(i, (i + across) % occ_devices) for i in rang...  3.03 us
  transfers between devices with their start and end apart: 26, of which 10 were waited for; matrix products, arithmetic and copies ran while one was open for 3% of the time, Pallas kernels for 26%

profile of v2, /device:TPU:0, one launch (start us, length us, event | category | flops | bytes accessed | tf_op | source)
XLA Modules:
  0.0 105.8 jit_solution(5970378028178790214)
XLA Ops:
  1.1 3.0 %collective-permute-start.3 = (bf16[128,1024]{1,0:T(8,128)(2,1)S(1)}, bf16[128,1024]{1,0:T(8,128)(2,1)S(1)}, u32[]{:S(2)}, u32[]{:S(2)}) collective-permute-start(bf16[128,1024]{1,0:T(8,128)(2,1)S(1)} %get-tuple-element.93), channel_id=1, source_target_pairs={{0,16},{8,24},{16,0},{24,8},{1,17},{9,25},{17,1},{25,9},{2,18},{10... | collective-permute-start | bytes 786440 | tf_op jit(solution)/shard_map/ppermute | solution.py:175
  4.1 1.6 %collective-permute-start.1 = (bf16[128,1024]{1,0:T(8,128)(2,1)S(1)}, bf16[128,1024]{1,0:T(8,128)(2,1)S(1)}, u32[]{:S(2)}, u32[]{:S(2)}) collective-permute-start(bf16[128,1024]{1,0:T(8,128)(2,1)S(1)} %get-tuple-element.94.refs_0_), channel_id=1, source_target_pairs={{0,2},{1,3},{2,0},{3,1},{4,6},{5,7},{6,4},{7,5},{8,10},{9,11},{10,... | collective-permute-start | bytes 786440 | tf_op jit(solution)/shard_map/ppermute | solution.py:172
  5.7 1.5 %collective-permute-start = (bf16[128,1024]{1,0:T(8,128)(2,1)S(1)}, bf16[128,1024]{1,0:T(8,128)(2,1)S(1)}, u32[]{:S(2)}, u32[]{:S(2)}) collective-permute-start(bf16[128,1024]{1,0:T(8,128)(2,1)S(1)} %get-tuple-element.94.refs_0_), channel_id=1, source_target_pairs={{0,1},{1,0},{2,3},{3,2},{4,5},{5,4},{6,7},{7,6},{8,9},{9,8},{10,11... | collective-permute-start | bytes 786440 | tf_op jit(solution)/shard_map/ppermute | solution.py:180
  7.2 2.6 %collective-permute-start.5 = (bf16[128,1024]{1,0:T(8,128)(2,1)S(1)}, bf16[128,1024]{1,0:T(8,128)(2,1)S(1)}, u32[]{:S(2)}, u32[]{:S(2)}) collective-permute-start(bf16[128,1024]{1,0:T(8,128)(2,1)S(1)} %get-tuple-element.94.refs_0_), channel_id=1, source_target_pairs={{0,4},{1,5},{2,6},{3,7},{4,0},{5,1},{6,2},{7,3},{8,12},{9,13},{10,... | collective-permute-start | bytes 786440 | tf_op jit(solution)/shard_map/ppermute | solution.py:172
  12.1 1.6 %collective-permute-start.6 = (bf16[128,1024]{1,0:T(8,128)(2,1)S(1)}, bf16[128,1024]{1,0:T(8,128)(2,1)S(1)}, u32[]{:S(2)}, u32[]{:S(2)}) collective-permute-start(bf16[128,1024]{1,0:T(8,128)(2,1)S(1)} %collective-permute-done.3.refs_2_), channel_id=1, source_target_pairs={{0,2},{1,3},{2,0},{3,1},{4,6},{5,7},{6,4},{7,5},{8,10},{9,11},{10,... | collective-permute-start | bytes 786440 | tf_op jit(solution)/shard_map/ppermute | solution.py:172
  13.7 3.9 %collective-permute-done.1.refs_0_ = bf16[128,1024]{1,0:T(8,128)(2,1)S(1)} collective-permute-done((bf16[128,1024]{1,0:T(8,128)(2,1)S(1)}, bf16[128,1024]{1,0:T(8,128)(2,1)S(1)}, u32[]{:S(2)}, u32[]{:S(2)}) %collective-permute-start.1) | collective-permute-done | bytes 262176 | tf_op jit(solution)/shard_map/ppermute | solution.py:172
  17.6 2.8 %collective-permute-start.2 = (bf16[128,1024]{1,0:T(8,128)(2,1)S(1)}, bf16[128,1024]{1,0:T(8,128)(2,1)S(1)}, u32[]{:S(2)}, u32[]{:S(2)}) collective-permute-start(bf16[128,1024]{1,0:T(8,128)(2,1)S(1)} %collective-permute-done.1.refs_0_), channel_id=1, source_target_pairs={{0,1},{1,0},{2,3},{3,2},{4,5},{5,4},{6,7},{7,6},{8,9},{9,8},{10,11... | collective-permute-start | bytes 786440 | tf_op jit(solution)/shard_map/ppermute | solution.py:180
  21.3 1.2 %collective-permute-start.9 = (bf16[128,1024]{1,0:T(8,128)(2,1)S(1)}, bf16[128,1024]{1,0:T(8,128)(2,1)S(1)}, u32[]{:S(2)}, u32[]{:S(2)}) collective-permute-start(bf16[128,1024]{1,0:T(8,128)(2,1)S(1)} %collective-permute-done.3.refs_2_), channel_id=1, source_target_pairs={{0,4},{1,5},{2,6},{3,7},{4,0},{5,1},{6,2},{7,3},{8,12},{9,13},{10,... | collective-permute-start | bytes 786440 | tf_op jit(solution)/shard_map/ppermute | solution.py:172
  22.6 5.0 %shard_map.73 = (f32[512,512]{1,0:T(8,128)S(1)}, f32[512,512]{1,0:T(8,128)S(1)}, bf16[512,768]{1,0:T(8,128)(2,1)S(1)}, bf16[512,768]{1,0:T(8,128)(2,1)S(1)}, bf1...) custom-call(bf16[3,1024,1024]{2,1,0:T(8,128)(2,1)} %factor_ref.1, ...), custom_call_target="tpu_custom_call" | custom-call | bytes 11010048 | tf_op jit(solution)/shard_map/pallas_call | solution.py:108
  28.7 2.0 %collective-permute-start.10 = (bf16[128,1024]{1,0:T(8,128)(2,1)S(1)}, bf16[128,1024]{1,0:T(8,128)(2,1)S(1)}, u32[]{:S(2)}, u32[]{:S(2)}) collective-permute-start(bf16[128,1024]{1,0:T(8,128)(2,1)S(1)} %collective-permute-done.5.refs_0_), channel_id=1, source_target_pairs={{0,2},{1,3},{2,0},{3,1},{4,6},{5,7},{6,4},{7,5},{8,10},{9,11},{10,... | collective-permute-start | bytes 786440 | tf_op jit(solution)/shard_map/ppermute | solution.py:172
  30.7 2.0 %collective-permute-start.8 = (bf16[128,1024]{1,0:T(8,128)(2,1)S(1)}, bf16[128,1024]{1,0:T(8,128)(2,1)S(1)}, u32[]{:S(2)}, u32[]{:S(2)}) collective-permute-start(bf16[128,1024]{1,0:T(8,128)(2,1)S(1)} %collective-permute-done.6.refs_2_), channel_id=1, source_target_pairs={{0,1},{1,0},{2,3},{3,2},{4,5},{5,4},{6,7},{7,6},{8,9},{9,8},{10,11... | collective-permute-start | bytes 786440 | tf_op jit(solution)/shard_map/ppermute | solution.py:180
  32.6 5.3 %shard_map.74 = (f32[512,512]{1,0:T(8,128)S(1)}, f32[512,512]{1,0:T(8,128)S(1)}, bf16[512,1536]{1,0:T(8,128)(2,1)S(1)}, bf16[512,1536]{1,0:T(8,128)(2,1)S(1)}, bf16[1024,1536]{1,0:T(8,128)(2,1)S(1)}) custom-call(bf16[3,1024,1024]{2,1,0:T(8,128)(2,1)S(1)} %get-tuple-element.47.factor_ref, ...), custom_call_target="tpu_custom_call", output_to_operand_aliasing={{0}: (5, {}), {1}: (6, {})} | custom-call | flops 4831838208 | bytes 11534336 | tf_op jit(solution)/shard_map/pallas_call | solution.py:108
  38.1 1.3 %collective-permute-start.13 = (bf16[128,1024]{1,0:T(8,128)(2,1)S(1)}, bf16[128,1024]{1,0:T(8,128)(2,1)S(1)}, u32[]{:S(2)}, u32[]{:S(2)}) collective-permute-start(bf16[128,1024]{1,0:T(8,128)(2,1)S(1)} %collective-permute-done.9.refs_2_), channel_id=1, source_target_pairs={{0,2},{1,3},{2,0},{3,1},{4,6},{5,7},{6,4},{7,5},{8,10},{9,11},{10,... | collective-permute-start | bytes 786440 | tf_op jit(solution)/shard_map/ppermute | solution.py:172
  40.3 5.5 %shard_map.75 = (f32[512,512]{1,0:T(8,128)S(1)}, f32[512,512]{1,0:T(8,128)S(1)}, bf16[512,1536]{1,0:T(8,128)(2,1)S(1)}, bf16[512,1536]{1,0:T(8,128)(2,1)S(1)}, bf16[1024,1536]{1,0:T(8,128)(2,1)S(1)}) custom-call(bf16[3,1024,1024]{2,1,0:T(8,128)(2,1)S(1)} %get-tuple-element.47.factor_ref, ...), custom_call_target="tpu_custom_call", output_to_operand_aliasing={{0}: (5, {}), {1}: (6, {})} | custom-call | flops 4831838208 | bytes 11534336 | tf_op jit(solution)/shard_map/pallas_call | solution.py:108
  45.8 2.5 %collective-permute-start.14 = (bf16[128,1024]{1,0:T(8,128)(2,1)S(1)}, bf16[128,1024]{1,0:T(8,128)(2,1)S(1)}, u32[]{:S(2)}, u32[]{:S(2)}) collective-permute-start(bf16[128,1024]{1,0:T(8,128)(2,1)S(1)} %collective-permute-done.13.refs_0_), channel_id=1, source_target_pairs={{0,1},{1,0},{2,3},{3,2},{4,5},{5,4},{6,7},{7,6},{8,9},{9,8},{10,11... | collective-permute-start | bytes 786440 | tf_op jit(solution)/shard_map/ppermute | solution.py:180
  48.3 5.3 %shard_map.76 = (f32[512,512]{1,0:T(8,128)S(1)}, f32[512,512]{1,0:T(8,128)S(1)}, bf16[512,1536]{1,0:T(8,128)(2,1)S(1)}, bf16[512,1536]{1,0:T(8,128)(2,1)S(1)}, bf16[1024,1536]{1,0:T(8,128)(2,1)S(1)}) custom-call(bf16[3,1024,1024]{2,1,0:T(8,128)(2,1)S(1)} %get-tuple-element.47.factor_ref, ...), custom_call_target="tpu_custom_call", output_to_operand_aliasing={{0}: (5, {}), {1}: (6, {})} | custom-call | flops 4831838208 | bytes 11534336 | tf_op jit(solution)/shard_map/pallas_call | solution.py:108
  53.6 2.7 %shard_map.77 = (bf16[512,512]{1,0:T(8,128)(2,1)S(1)}, bf16[512,512]{1,0:T(8,128)(2,1)S(1)}, bf16[512,768]{1,0:T(8,128)(2,1)S(1)}, bf16[512,768]{1,0:T(8,128)(2,1)S(1)}, bf16[1024,768]{1,0:T(8,128)(2,1)S(1)}) custom-call(bf16[3,1024,1024]{2,1,0:T(8,128)(2,1)S(1)} %get-tuple-element.47.factor_ref, bf16[128,1024]{1,0:T(8,128)(2,1)S(1)} %collective-permute-done.13.refs_0_, ...), custom_call_target="tpu_custom_call" | custom-call | flops 2415919104 | bytes 11010048 | tf_op jit(solution)/shard_map/pallas_call | solution.py:108
  58.3 6.7 %shard_map.78 = (f32[512,512]{1,0:T(8,128)S(1)}, f32[512,512]{1,0:T(8,128)S(1)}) custom-call(bf16[512,768]{1,0:T(8,128)(2,1)S(1)} %get-tuple-element.44.refs_0_, bf16[512,768]{1,0:T(8,128)(2,1)S(1)} %get-tuple-element.45.refs_1_, bf16[1024,768]{1,0:T(8,128)(2,1)S(1)} %get-tuple-element.46.refs_2_, bf16[512,1536]{1,0:T(8,128)(2,1)S(1)} %get-tuple-element.52.refs_3_, ...), custom_call_target="tpu_custom_call" | custom-call | flops 6442450944 | bytes 27262976 | tf_op jit(solution)/shard_map/pallas_call | solution.py:141
  65.0 3.2 %collective-permute-done.18 = bf16[512,512]{1,0:T(8,128)(2,1)S(1)} collective-permute-done((bf16[512,512]{1,0:T(8,128)(2,1)S(1)}, bf16[512,512]{1,0:T(8,128)(2,1)S(1)}, u32[]{:S(2)}, u32[]{:S(2)}) %collective-permute-start.18) | collective-permute-done | bytes 524320 | tf_op jit(solution)/shard_map/ppermute | solution.py:172
  69.3 1.3 %collective-permute-start.16 = (bf16[2,128,512]{2,1,0:T(8,128)(2,1)S(1)}, bf16[2,128,512]{2,1,0:T(8,128)(2,1)S(1)}, u32[]{:S(2)}, u32[]{:S(2)}) collective-permute-start(bf16[2,128,512]{2,1,0:T(8,128)(2,1)S(1)} %fusion.9), channel_id=1, source_target_pairs={{0,2},{1,3},{2,0},{3,1},{4,6},{5,7},{6,4},{7,5},{8,10},{9,11},{10,... | collective-permute-start | bytes 786440 | tf_op jit(solution)/shard_map/ppermute | solution.py:172
  70.6 4.1 %collective-permute-done.19 = bf16[2,128,512]{2,1,0:T(8,128)(2,1)S(1)} collective-permute-done((bf16[2,128,512]{2,1,0:T(8,128)(2,1)S(1)}, bf16[2,128,512]{2,1,0:T(8,128)(2,1)S(1)}, u32[]{:S(2)}, u32[]{:S(2)}) %collective-permute-start.19) | collective-permute-done | bytes 262176 | tf_op jit(solution)/shard_map/ppermute | solution.py:180
  74.8 4.1 %collective-permute-start.20 = (bf16[128,512]{1,0:T(8,128)(2,1)S(1)}, bf16[128,512]{1,0:T(8,128)(2,1)S(1)}, u32[]{:S(2)}, u32[]{:S(2)}) collective-permute-start(bf16[128,512]{1,0:T(8,128)(2,1)S(1)} %fusion.16), channel_id=1, source_target_pairs={{0,4},{1,5},{2,6},{3,7},{4,0},{5,1},{6,2},{7,3},{8,12},{9,13},{10,... | collective-permute-start | bytes 393224 | tf_op jit(solution)/shard_map/ppermute | solution.py:172
  79.1 4.2 %collective-permute-start.17 = (bf16[128,512]{1,0:T(8,128)(2,1)S(1)}, bf16[128,512]{1,0:T(8,128)(2,1)S(1)}, u32[]{:S(2)}, u32[]{:S(2)}) collective-permute-start(bf16[128,512]{1,0:T(8,128)(2,1)S(1)} %fusion.15), channel_id=1, source_target_pairs={{0,4},{1,5},{2,6},{3,7},{4,0},{5,1},{6,2},{7,3},{8,12},{9,13},{10,... | collective-permute-start | bytes 393224 | tf_op jit(solution)/shard_map/ppermute | solution.py:172
  83.3 3.6 %collective-permute-done.20 = bf16[128,512]{1,0:T(8,128)(2,1)S(1)} collective-permute-done((bf16[128,512]{1,0:T(8,128)(2,1)S(1)}, bf16[128,512]{1,0:T(8,128)(2,1)S(1)}, u32[]{:S(2)}, u32[]{:S(2)}) %collective-permute-start.20) | collective-permute-done | bytes 131104 | tf_op jit(solution)/shard_map/ppermute | solution.py:172
  87.1 1.2 %collective-permute-done.17 = bf16[128,512]{1,0:T(8,128)(2,1)S(1)} collective-permute-done((bf16[128,512]{1,0:T(8,128)(2,1)S(1)}, bf16[128,512]{1,0:T(8,128)(2,1)S(1)}, u32[]{:S(2)}, u32[]{:S(2)}) %collective-permute-start.17) | collective-permute-done | bytes 131104 | tf_op jit(solution)/shard_map/ppermute | solution.py:172
  88.5 1.6 %collective-permute-start.21 = (bf16[4,128,128]{2,1,0:T(8,128)(2,1)S(1)}, bf16[4,128,128]{2,1,0:T(8,128)(2,1)S(1)}, u32[]{:S(2)}, u32[]{:S(2)}) collective-permute-start(bf16[4,128,128]{2,1,0:T(8,128)(2,1)S(1)} %dynamic-slice_bitcast_fusion.2), channel_id=1, source_target_pairs={{0,1},{1,0},{2,3},{3,2},{4,5},{5,4},{6,7},{7,6},{8,9},{9,8},{10,11... | collective-permute-start | bytes 393224 | tf_op jit(solution)/shard_map/ppermute | solution.py:180
  90.2 3.3 %collective-permute-done.21 = bf16[4,128,128]{2,1,0:T(8,128)(2,1)S(1)} collective-permute-done((bf16[4,128,128]{2,1,0:T(8,128)(2,1)S(1)}, bf16[4,128,128]{2,1,0:T(8,128)(2,1)S(1)}, u32[]{:S(2)}, u32[]{:S(2)}) %collective-permute-start.21) | collective-permute-done | bytes 131104 | tf_op jit(solution)/shard_map/ppermute | solution.py:180
  93.8 2.5 %collective-permute-start.25 = (bf16[128,256]{1,0:T(8,128)(2,1)S(1)}, bf16[128,256]{1,0:T(8,128)(2,1)S(1)}, u32[]{:S(2)}, u32[]{:S(2)}) collective-permute-start(bf16[128,256]{1,0:T(8,128)(2,1)S(1)} %get-tuple-element.98), channel_id=1, source_target_pairs={{0,22},{1,23},{2,20},{3,21},{4,18},{5,19},{6,16},{7,17},{8,30},{9,... | collective-permute-start | bytes 196616 | tf_op jit(solution)/shard_map/ppermute | solution.py:280
  96.3 2.8 %collective-permute-start.23 = (bf16[128,256]{1,0:T(8,128)(2,1)S(1)}, bf16[128,256]{1,0:T(8,128)(2,1)S(1)}, u32[]{:S(2)}, u32[]{:S(2)}) collective-permute-start(bf16[128,256]{1,0:T(8,128)(2,1)S(1)} %get-tuple-element.100), channel_id=1, source_target_pairs={{0,18},{1,19},{2,16},{3,17},{4,22},{5,23},{6,20},{7,21},{8,26},{9,... | collective-permute-start | bytes 196616 | tf_op jit(solution)/shard_map/ppermute | solution.py:280
  99.1 1.5 %collective-permute-start.22 = (bf16[128,256]{1,0:T(8,128)(2,1)S(1)}, bf16[128,256]{1,0:T(8,128)(2,1)S(1)}, u32[]{:S(2)}, u32[]{:S(2)}) collective-permute-start(bf16[128,256]{1,0:T(8,128)(2,1)S(1)} %get-tuple-element.97), channel_id=1, source_target_pairs={{0,16},{1,17},{2,18},{3,19},{4,20},{5,21},{6,22},{7,23},{8,24},{9,... | collective-permute-start | bytes 196616 | tf_op jit(solution)/shard_map/ppermute | solution.py:280
  100.8 1.5 %collective-permute-done.24 = bf16[128,256]{1,0:T(8,128)(2,1)S(1)} collective-permute-done((bf16[128,256]{1,0:T(8,128)(2,1)S(1)}, bf16[128,256]{1,0:T(8,128)(2,1)S(1)}, u32[]{:S(2)}, u32[]{:S(2)}) %collective-permute-start.24) | collective-permute-done | bytes 65568 | tf_op jit(solution)/shard_map/ppermute | solution.py:280
  104.6 1.3 %fusion = f32[2,128,1024]{2,1,0:T(8,128)} fusion(f32[1,128,1024]{2,1,0:T(8,128)S(1)} %get-tuple-element.88, f32[1,128,1024]{2,1,0:T(8,128)S(1)} %get-tuple-element.87, f32[2]{0:T(128)S(1)} %add.140, f32[128,1024]{1,0:T(8,128)S(1)} %broadcast_add_fusion, s32[1024]{0:T(1024)S(1)} %copy-done.2, s32[2,128]{1,0:T(2,128)S(1)} %broadcast_xor_fusion), kind=kLoop, calls=%fused_computation.1 | loop fusion | flops 1572864 | bytes 2626568 | tf_op jit(solution)/shard_map/jit(_where)/select_n | solution.py:311
  (70 shorter events, 12.7 us)
Async XLA Ops:
  0.0 11.3 %copy-start = (s32[8,2]{0,1:T(2,128)S(1)}, s32[8,2]{0,1:T(2,128)}, u32[]{:S(2)}) copy-start(s32[8,2]{0,1:T(2,128)} %param.13) | copy-start | bytes 196
  1.1 10.3 %collective-permute-start.3 = (bf16[128,1024]{1,0:T(8,128)(2,1)S(1)}, bf16[128,1024]{1,0:T(8,128)(2,1)S(1)}, u32[]{:S(2)}, u32[]{:S(2)}) collective-permute-start(bf16[128,1024]{1,0:T(8,128)(2,1)S(1)} %get-tuple-element.93), channel_id=1, source_target_pairs={{0,16},{8,24},{16,0},{24,8},{1,17},{9,25},{17,1},{25,9},{2,18},{10... | collective-permute-start | bytes 786440 | tf_op jit(solution)/shard_map/ppermute | solution.py:175
  4.1 13.5 %collective-permute-start.1 = (bf16[128,1024]{1,0:T(8,128)(2,1)S(1)}, bf16[128,1024]{1,0:T(8,128)(2,1)S(1)}, u32[]{:S(2)}, u32[]{:S(2)}) collective-permute-start(bf16[128,1024]{1,0:T(8,128)(2,1)S(1)} %get-tuple-element.94.refs_0_), channel_id=1, source_target_pairs={{0,2},{1,3},{2,0},{3,1},{4,6},{5,7},{6,4},{7,5},{8,10},{9,11},{10,... | collective-permute-start | bytes 786440 | tf_op jit(solution)/shard_map/ppermute | solution.py:172
  5.7 15.6 %collective-permute-start = (bf16[128,1024]{1,0:T(8,128)(2,1)S(1)}, bf16[128,1024]{1,0:T(8,128)(2,1)S(1)}, u32[]{:S(2)}, u32[]{:S(2)}) collective-permute-start(bf16[128,1024]{1,0:T(8,128)(2,1)S(1)} %get-tuple-element.94.refs_0_), channel_id=1, source_target_pairs={{0,1},{1,0},{2,3},{3,2},{4,5},{5,4},{6,7},{7,6},{8,9},{9,8},{10,11... | collective-permute-start | bytes 786440 | tf_op jit(solution)/shard_map/ppermute | solution.py:180
  7.2 20.4 %collective-permute-start.5 = (bf16[128,1024]{1,0:T(8,128)(2,1)S(1)}, bf16[128,1024]{1,0:T(8,128)(2,1)S(1)}, u32[]{:S(2)}, u32[]{:S(2)}) collective-permute-start(bf16[128,1024]{1,0:T(8,128)(2,1)S(1)} %get-tuple-element.94.refs_0_), channel_id=1, source_target_pairs={{0,4},{1,5},{2,6},{3,7},{4,0},{5,1},{6,2},{7,3},{8,12},{9,13},{10,... | collective-permute-start | bytes 786440 | tf_op jit(solution)/shard_map/ppermute | solution.py:172
  11.4 21.3 %collective-permute-start.4 = (bf16[128,1024]{1,0:T(8,128)(2,1)S(1)}, bf16[128,1024]{1,0:T(8,128)(2,1)S(1)}, u32[]{:S(2)}, u32[]{:S(2)}) collective-permute-start(bf16[128,1024]{1,0:T(8,128)(2,1)S(1)} %collective-permute-done.3.refs_2_), channel_id=1, source_target_pairs={{0,1},{1,0},{2,3},{3,2},{4,5},{5,4},{6,7},{7,6},{8,9},{9,8},{10,11... | collective-permute-start | bytes 786440 | tf_op jit(solution)/shard_map/ppermute | solution.py:180
  12.1 15.5 %collective-permute-start.6 = (bf16[128,1024]{1,0:T(8,128)(2,1)S(1)}, bf16[128,1024]{1,0:T(8,128)(2,1)S(1)}, u32[]{:S(2)}, u32[]{:S(2)}) collective-permute-start(bf16[128,1024]{1,0:T(8,128)(2,1)S(1)} %collective-permute-done.3.refs_2_), channel_id=1, source_target_pairs={{0,2},{1,3},{2,0},{3,1},{4,6},{5,7},{6,4},{7,5},{8,10},{9,11},{10,... | collective-permute-start | bytes 786440 | tf_op jit(solution)/shard_map/ppermute | solution.py:172
  17.6 13.0 %collective-permute-start.2 = (bf16[128,1024]{1,0:T(8,128)(2,1)S(1)}, bf16[128,1024]{1,0:T(8,128)(2,1)S(1)}, u32[]{:S(2)}, u32[]{:S(2)}) collective-permute-start(bf16[128,1024]{1,0:T(8,128)(2,1)S(1)} %collective-permute-done.1.refs_0_), channel_id=1, source_target_pairs={{0,1},{1,0},{2,3},{3,2},{4,5},{5,4},{6,7},{7,6},{8,9},{9,8},{10,11... | collective-permute-start | bytes 786440 | tf_op jit(solution)/shard_map/ppermute | solution.py:180
  21.3 16.6 %collective-permute-start.9 = (bf16[128,1024]{1,0:T(8,128)(2,1)S(1)}, bf16[128,1024]{1,0:T(8,128)(2,1)S(1)}, u32[]{:S(2)}, u32[]{:S(2)}) collective-permute-start(bf16[128,1024]{1,0:T(8,128)(2,1)S(1)} %collective-permute-done.3.refs_2_), channel_id=1, source_target_pairs={{0,4},{1,5},{2,6},{3,7},{4,0},{5,1},{6,2},{7,3},{8,12},{9,13},{10,... | collective-permute-start | bytes 786440 | tf_op jit(solution)/shard_map/ppermute | solution.py:172
  27.6 11.8 %collective-permute-start.7 = (bf16[128,1024]{1,0:T(8,128)(2,1)S(1)}, bf16[128,1024]{1,0:T(8,128)(2,1)S(1)}, u32[]{:S(2)}, u32[]{:S(2)}) collective-permute-start(bf16[128,1024]{1,0:T(8,128)(2,1)S(1)} %collective-permute-done.5.refs_0_), channel_id=1, source_target_pairs={{0,1},{1,0},{2,3},{3,2},{4,5},{5,4},{6,7},{7,6},{8,9},{9,8},{10,11... | collective-permute-start | bytes 786440 | tf_op jit(solution)/shard_map/ppermute | solution.py:180
  28.7 9.3 %collective-permute-start.10 = (bf16[128,1024]{1,0:T(8,128)(2,1)S(1)}, bf16[128,1024]{1,0:T(8,128)(2,1)S(1)}, u32[]{:S(2)}, u32[]{:S(2)}) collective-permute-start(bf16[128,1024]{1,0:T(8,128)(2,1)S(1)} %collective-permute-done.5.refs_0_), channel_id=1, source_target_pairs={{0,2},{1,3},{2,0},{3,1},{4,6},{5,7},{6,4},{7,5},{8,10},{9,11},{10,... | collective-permute-start | bytes 786440 | tf_op jit(solution)/shard_map/ppermute | solution.py:172
  30.7 9.6 %collective-permute-start.8 = (bf16[128,1024]{1,0:T(8,128)(2,1)S(1)}, bf16[128,1024]{1,0:T(8,128)(2,1)S(1)}, u32[]{:S(2)}, u32[]{:S(2)}) collective-permute-start(bf16[128,1024]{1,0:T(8,128)(2,1)S(1)} %collective-permute-done.6.refs_2_), channel_id=1, source_target_pairs={{0,1},{1,0},{2,3},{3,2},{4,5},{5,4},{6,7},{7,6},{8,9},{9,8},{10,11... | collective-permute-start | bytes 786440 | tf_op jit(solution)/shard_map/ppermute | solution.py:180
  37.9 10.4 %collective-permute-start.12 = (bf16[128,1024]{1,0:T(8,128)(2,1)S(1)}, bf16[128,1024]{1,0:T(8,128)(2,1)S(1)}, u32[]{:S(2)}, u32[]{:S(2)}) collective-permute-start(bf16[128,1024]{1,0:T(8,128)(2,1)S(1)} %collective-permute-done.9.refs_2_), channel_id=1, source_target_pairs={{0,1},{1,0},{2,3},{3,2},{4,5},{5,4},{6,7},{7,6},{8,9},{9,8},{10,11... | collective-permute-start | bytes 786440 | tf_op jit(solution)/shard_map/ppermute | solution.py:180
  38.1 7.7 %collective-permute-start.13 = (bf16[128,1024]{1,0:T(8,128)(2,1)S(1)}, bf16[128,1024]{1,0:T(8,128)(2,1)S(1)}, u32[]{:S(2)}, u32[]{:S(2)}) collective-permute-start(bf16[128,1024]{1,0:T(8,128)(2,1)S(1)} %collective-permute-done.9.refs_2_), channel_id=1, source_target_pairs={{0,2},{1,3},{2,0},{3,1},{4,6},{5,7},{6,4},{7,5},{8,10},{9,11},{10,... | collective-permute-start | bytes 786440 | tf_op jit(solution)/shard_map/ppermute | solution.py:172
  39.4 8.9 %collective-permute-start.11 = (bf16[128,1024]{1,0:T(8,128)(2,1)S(1)}, bf16[128,1024]{1,0:T(8,128)(2,1)S(1)}, u32[]{:S(2)}, u32[]{:S(2)}) collective-permute-start(bf16[128,1024]{1,0:T(8,128)(2,1)S(1)} %collective-permute-done.7.refs_1_), channel_id=1, source_target_pairs={{0,2},{1,3},{2,0},{3,1},{4,6},{5,7},{6,4},{7,5},{8,10},{9,11},{10,... | collective-permute-start | bytes 786440 | tf_op jit(solution)/shard_map/ppermute | solution.py:172
  45.8 7.9 %collective-permute-start.14 = (bf16[128,1024]{1,0:T(8,128)(2,1)S(1)}, bf16[128,1024]{1,0:T(8,128)(2,1)S(1)}, u32[]{:S(2)}, u32[]{:S(2)}) collective-permute-start(bf16[128,1024]{1,0:T(8,128)(2,1)S(1)} %collective-permute-done.13.refs_0_), channel_id=1, source_target_pairs={{0,1},{1,0},{2,3},{3,2},{4,5},{5,4},{6,7},{7,6},{8,9},{9,8},{10,11... | collective-permute-start | bytes 786440 | tf_op jit(solution)/shard_map/ppermute | solution.py:180
  56.3 11.8 %collective-permute-start.18 = (bf16[512,512]{1,0:T(8,128)(2,1)S(1)}, bf16[512,512]{1,0:T(8,128)(2,1)S(1)}, u32[]{:S(2)}, u32[]{:S(2)}) collective-permute-start(bf16[512,512]{1,0:T(8,128)(2,1)S(1)} %get-tuple-element.82), channel_id=1, source_target_pairs={{0,2},{1,3},{2,0},{3,1},{4,6},{5,7},{6,4},{7,5},{8,10},{9,11},{10,... | collective-permute-start | bytes 1572872 | tf_op jit(solution)/shard_map/ppermute | solution.py:172
  57.2 12.0 %collective-permute-start.15 = (bf16[512,512]{1,0:T(8,128)(2,1)S(1)}, bf16[512,512]{1,0:T(8,128)(2,1)S(1)}, u32[]{:S(2)}, u32[]{:S(2)}) collective-permute-start(bf16[512,512]{1,0:T(8,128)(2,1)S(1)} %get-tuple-element.80), channel_id=1, source_target_pairs={{0,1},{1,0},{2,3},{3,2},{4,5},{5,4},{6,7},{7,6},{8,9},{9,8},{10,11... | collective-permute-start | bytes 1572872 | tf_op jit(solution)/shard_map/ppermute | solution.py:180
  58.3 10.6 %copy-start.1 = (f32[1024]{0:T(1024)S(1)}, f32[1024]{0:T(1024)}, u32[]{:S(2)}) copy-start(f32[1024]{0:T(1024)} %param.10) | copy-start | bytes 12292
  68.3 6.4 %collective-permute-start.19 = (bf16[2,128,512]{2,1,0:T(8,128)(2,1)S(1)}, bf16[2,128,512]{2,1,0:T(8,128)(2,1)S(1)}, u32[]{:S(2)}, u32[]{:S(2)}) collective-permute-start(bf16[2,128,512]{2,1,0:T(8,128)(2,1)S(1)} %fusion.10), channel_id=1, source_target_pairs={{0,1},{1,0},{2,3},{3,2},{4,5},{5,4},{6,7},{7,6},{8,9},{9,8},{10,11... | collective-permute-start | bytes 786440 | tf_op jit(solution)/shard_map/ppermute | solution.py:180
  69.3 9.7 %collective-permute-start.16 = (bf16[2,128,512]{2,1,0:T(8,128)(2,1)S(1)}, bf16[2,128,512]{2,1,0:T(8,128)(2,1)S(1)}, u32[]{:S(2)}, u32[]{:S(2)}) collective-permute-start(bf16[2,128,512]{2,1,0:T(8,128)(2,1)S(1)} %fusion.9), channel_id=1, source_target_pairs={{0,2},{1,3},{2,0},{3,1},{4,6},{5,7},{6,4},{7,5},{8,10},{9,11},{10,... | collective-permute-start | bytes 786440 | tf_op jit(solution)/shard_map/ppermute | solution.py:172
  74.8 12.1 %collective-permute-start.20 = (bf16[128,512]{1,0:T(8,128)(2,1)S(1)}, bf16[128,512]{1,0:T(8,128)(2,1)S(1)}, u32[]{:S(2)}, u32[]{:S(2)}) collective-permute-start(bf16[128,512]{1,0:T(8,128)(2,1)S(1)} %fusion.16), channel_id=1, source_target_pairs={{0,4},{1,5},{2,6},{3,7},{4,0},{5,1},{6,2},{7,3},{8,12},{9,13},{10,... | collective-permute-start | bytes 393224 | tf_op jit(solution)/shard_map/ppermute | solution.py:172
  79.1 9.2 %collective-permute-start.17 = (bf16[128,512]{1,0:T(8,128)(2,1)S(1)}, bf16[128,512]{1,0:T(8,128)(2,1)S(1)}, u32[]{:S(2)}, u32[]{:S(2)}) collective-permute-start(bf16[128,512]{1,0:T(8,128)(2,1)S(1)} %fusion.15), channel_id=1, source_target_pairs={{0,4},{1,5},{2,6},{3,7},{4,0},{5,1},{6,2},{7,3},{8,12},{9,13},{10,... | collective-permute-start | bytes 393224 | tf_op jit(solution)/shard_map/ppermute | solution.py:172
  88.5 12.1 %copy-start.3 = (f32[100]{0:T(128)S(1)}, f32[100]{0:T(128)}, u32[]{:S(2)}) copy-start(f32[100]{0:T(128)} %param.9) | copy-start | bytes 1204
  88.5 5.0 %collective-permute-start.21 = (bf16[4,128,128]{2,1,0:T(8,128)(2,1)S(1)}, bf16[4,128,128]{2,1,0:T(8,128)(2,1)S(1)}, u32[]{:S(2)}, u32[]{:S(2)}) collective-permute-start(bf16[4,128,128]{2,1,0:T(8,128)(2,1)S(1)} %dynamic-slice_bitcast_fusion.2), channel_id=1, source_target_pairs={{0,1},{1,0},{2,3},{3,2},{4,5},{5,4},{6,7},{7,6},{8,9},{9,8},{10,11... | collective-permute-start | bytes 393224 | tf_op jit(solution)/shard_map/ppermute | solution.py:180
  93.8 7.0 %collective-permute-start.25 = (bf16[128,256]{1,0:T(8,128)(2,1)S(1)}, bf16[128,256]{1,0:T(8,128)(2,1)S(1)}, u32[]{:S(2)}, u32[]{:S(2)}) collective-permute-start(bf16[128,256]{1,0:T(8,128)(2,1)S(1)} %get-tuple-element.98), channel_id=1, source_target_pairs={{0,22},{1,23},{2,20},{3,21},{4,18},{5,19},{6,16},{7,17},{8,30},{9,... | collective-permute-start | bytes 196616 | tf_op jit(solution)/shard_map/ppermute | solution.py:280
  96.3 6.1 %collective-permute-start.24 = (bf16[128,256]{1,0:T(8,128)(2,1)S(1)}, bf16[128,256]{1,0:T(8,128)(2,1)S(1)}, u32[]{:S(2)}, u32[]{:S(2)}) collective-permute-start(bf16[128,256]{1,0:T(8,128)(2,1)S(1)} %get-tuple-element.99), channel_id=1, source_target_pairs={{0,20},{1,21},{2,22},{3,23},{4,16},{5,17},{6,18},{7,19},{8,28},{9,... | collective-permute-start | bytes 196616 | tf_op jit(solution)/shard_map/ppermute | solution.py:280
  96.3 6.1 %collective-permute-start.23 = (bf16[128,256]{1,0:T(8,128)(2,1)S(1)}, bf16[128,256]{1,0:T(8,128)(2,1)S(1)}, u32[]{:S(2)}, u32[]{:S(2)}) collective-permute-start(bf16[128,256]{1,0:T(8,128)(2,1)S(1)} %get-tuple-element.100), channel_id=1, source_target_pairs={{0,18},{1,19},{2,16},{3,17},{4,22},{5,23},{6,20},{7,21},{8,26},{9,... | collective-permute-start | bytes 196616 | tf_op jit(solution)/shard_map/ppermute | solution.py:280
  99.1 4.3 %collective-permute-start.22 = (bf16[128,256]{1,0:T(8,128)(2,1)S(1)}, bf16[128,256]{1,0:T(8,128)(2,1)S(1)}, u32[]{:S(2)}, u32[]{:S(2)}) collective-permute-start(bf16[128,256]{1,0:T(8,128)(2,1)S(1)} %get-tuple-element.97), channel_id=1, source_target_pairs={{0,16},{1,17},{2,18},{3,19},{4,20},{5,21},{6,22},{7,23},{8,24},{9,... | collective-permute-start | bytes 196616 | tf_op jit(solution)/shard_map/ppermute | solution.py:280
  103.9 0.7 copy-start.2

commit v3 on v2

--- a/solution.py
+++ b/solution.py
@@ -8,7 +8,7 @@
 from jax.sharding import PartitionSpec as P
 
 GROUP_ROWS = 256
-VMEM_MIB = 16
+VMEM_MIB = 8
 
 
 def dot_nt(left, right):
@@ -25,15 +25,15 @@
     before_refs = ()
     if has_sums:
         before_refs, refs = refs[:2], refs[2:]
-    sent_x_ref, sent_z_ref, keep_x_ref, keep_z_ref, right_ref = refs[:5]
-    refs = refs[5:]
+    sent_x_ref, sent_z_ref, left_ref, right_ref = refs[:4]
+    refs = refs[4:]
     loading = []
     if loads:
-        source_ref, factor_ref, factor_sem, refs = factor_ref, refs[0], refs[4], refs[1:4]
+        source_ref, factor_ref, factor_sem, refs = factor_ref, refs[0], refs[2], refs[1:2]
         for q in range(factor_ref.shape[0]):
             loading.append(pltpu.make_async_copy(source_ref.at[q], factor_ref.at[q], factor_sem.at[q]))
             loading[q].start()
-    rows_ref, left_x_ref, left_z_ref = refs
+    (rows_ref,) = refs
     factor_count, size, _ = factor_ref.shape
     half = pair_refs[0].shape[0]
     width = block_count * GROUP_ROWS
@@ -58,21 +58,23 @@
             made = halves[:, block * GROUP_ROWS : (block + 1) * GROUP_ROWS]
             target = pl.ds(q * width + block * GROUP_ROWS, GROUP_ROWS)
             left, right = (taken, made) if block < kept_count else (made, taken)
-            right_ref[:, target] = right
             for start in range(0, size, 2 * half):
-                low, high = left[start : start + half], left[start + half : start + 2 * half]
-                here = pl.ds(start // 2, half)
-                left_x_ref[here, target] = jnp.where(x_index == 0, high, low)
-                keep_x_ref[here, target] = jnp.where(x_index == 0, low, high)
+                low, high = right[start : start + half], right[start + half : start + 2 * half]
+                first = start // middle * middle + start % middle // 2
+                right_ref[pl.ds(first, half), target] = jnp.where(x_index == 0, low, high)
+                right_ref[pl.ds(first + GROUP_ROWS, half), target] = jnp.where(x_index == 0, high, low)
             for start in range(0, size, 2 * GROUP_ROWS):
                 low = left[start : start + GROUP_ROWS]
                 high = left[start + GROUP_ROWS : start + 2 * GROUP_ROWS]
-                here = pl.ds(start // 2, GROUP_ROWS)
-                left_z_ref[here, target] = jnp.where(z_low == 0, high, low)
-                keep_z_ref[here, target] = jnp.where(z_low == 0, low, high)
-
-    for number, (left_ref, out_ref) in enumerate(((left_x_ref, sent_x_ref), (left_z_ref, sent_z_ref))):
-        product = dot_nt(left_ref[...], right_ref[pl.ds(number * middle, middle), :])
+                left_ref[pl.ds(start // 2, GROUP_ROWS), target] = jnp.where(z_low == 0, low, high)
+                left_ref[pl.ds(middle + start // 2, GROUP_ROWS), target] = jnp.where(z_low == 0, high, low)
+
+    products = (
+        dot_nt(right_ref[pl.ds(GROUP_ROWS, GROUP_ROWS), :], left_ref[...]),
+        dot_nt(right_ref[pl.ds(middle, middle), :], left_ref[pl.ds(middle, middle), :]),
+    )
+    for number, out_ref in enumerate((sent_x_ref, sent_z_ref)):
+        product = products[number]
         if has_sums:
             product = product + before_refs[number][...]
         out_ref[...] = product.astype(out_ref.dtype)
@@ -93,12 +95,10 @@
         operands += list(sums)
     in_specs = [whole] * len(operands)
     kind = jnp.bfloat16 if last else jnp.float32
-    out_shape = [jax.ShapeDtypeStruct((middle, middle), kind)] * 2
-    out_shape += [jax.ShapeDtypeStruct((rows, depth), jnp.bfloat16) for rows in (middle, middle, size)]
+    out_shape = [jax.ShapeDtypeStruct(shape, kind) for shape in ((GROUP_ROWS, size), (middle, middle))]
+    out_shape += [jax.ShapeDtypeStruct((size, depth), jnp.bfloat16)] * 2
     scratch = [
         pltpu.VMEM((width, size), jnp.bfloat16),
-        pltpu.VMEM((middle, depth), jnp.bfloat16),
-        pltpu.VMEM((middle, depth), jnp.bfloat16),
     ]
     if loads:
         operands[0] = pltpu.with_memory_space_constraint(factors, pltpu.HBM)
@@ -114,33 +114,37 @@
         input_output_aliases=aliases,
         compiler_params=pltpu.CompilerParams(vmem_limit_bytes=VMEM_MIB * 1024 * 1024),
         cost_estimate=pl.CostEstimate(
-            flops=(0 if loads else 3) * factor_count * width * size * size,
+            flops=(0 if loads else 2) * factor_count * width * size * size,
             bytes_accessed=2 * factor_count * size * size + 4 * size * size + 2 * width * size,
             transcendentals=0,
         ),
     )(*operands)
-    return out[:2], tuple(out[2:5]), out[5:]
+    return out[:2], tuple(out[2:4]), out[4:]
 
 
 def keep_kernel(count, *refs):
-    factors_refs, out_refs = refs[: 3 * count], refs[3 * count :]
-    middle = out_refs[0].shape[0]
-    for number, out_ref in enumerate(out_refs):
-        total = None
-        for part in range(count):
-            left_ref, right_ref = factors_refs[3 * part + number], factors_refs[3 * part + 2]
-            product = dot_nt(left_ref[...], right_ref[pl.ds(number * middle, middle), :])
-            total = product if total is None else total + product
-        out_ref[...] = total
+    parts, (keep_x_ref, keep_z_ref) = refs[: 2 * count], refs[2 * count :]
+    middle = keep_z_ref.shape[0]
+    totals = [None, None]
+    for part in range(count):
+        left_ref, right_ref = parts[2 * part], parts[2 * part + 1]
+        products = (
+            dot_nt(right_ref[pl.ds(0, GROUP_ROWS), :], left_ref[...]),
+            dot_nt(right_ref[pl.ds(middle, middle), :], left_ref[pl.ds(0, middle), :]),
+        )
+        totals = [p if t is None else t + p for t, p in zip(totals, products)]
+    keep_x_ref[...] = totals[0]
+    keep_z_ref[...] = totals[1]
 
 
 def keep_sums(parts):
-    middle = parts[0][0].shape[0]
+    size = parts[0][0].shape[0]
+    middle = size // 2
     operands = [array for part in parts for array in part]
     whole = pl.BlockSpec(memory_space=pltpu.VMEM)
     return pl.pallas_call(
         functools.partial(keep_kernel, len(parts)),
-        out_shape=[jax.ShapeDtypeStruct((middle, middle), jnp.float32)] * 2,
+        out_shape=[jax.ShapeDtypeStruct(shape, jnp.float32) for shape in ((GROUP_ROWS, size), (middle, middle))],
         in_specs=[whole] * len(operands),
         out_specs=[whole] * 2,
         compiler_params=pltpu.CompilerParams(vmem_limit_bytes=VMEM_MIB * 1024 * 1024),
@@ -190,16 +194,6 @@
         own = lax.dynamic_index_in_dim(sums, bit, axis, keepdims=False)
         return own + z_swap(sent, distance).astype(jnp.float32)
 
-    def halved(own, came, bit, swap):
-        came = came.reshape(own.shape)
-
-        def half(index):
-            mine = lax.dynamic_index_in_dim(own, index, 1, keepdims=False)
-            theirs = lax.dynamic_index_in_dim(came, index, 1, keepdims=False)
-            return mine + theirs.astype(jnp.float32)
-
-        return half(bit) + swap(half(1 - bit).astype(jnp.bfloat16)).astype(jnp.float32)
-
     z_high = z_index // 2
     z_low = z_index % 2
 
@@ -210,11 +204,14 @@
         return ladder((distance,), inner, factors, kept, swapped, total)
 
     after = lax.optimization_barrier
+    def gated(block, part):
+        return after((block, part[0]))[0]
+
     middle = size // 2
     if inner == 2:
-        kept_2 = z_swap(kept_0, 2)
         kept_1 = z_swap(kept_0, 1)
         kept_pair_0 = x_pair(kept_0)
+        kept_2 = z_swap(kept_0, 2)
         swapped_2 = z_swap(swapped_0, 2)
         swapped_1 = z_swap(swapped_0, 1)
         swapped_pair_0 = x_pair(swapped_0)
@@ -225,19 +222,43 @@
         kept_pair_2 = x_pair(kept_2)
         swapped_pair_1 = x_pair(swapped_1)
         sums, part_1, _ = ladder((1, 0), factors, [kept_pair_1], [swapped_pair_0], sums)
-        swapped_2, kept_3, sums = after((swapped_2, kept_3, sums))
-        swapped_3 = z_swap(swapped_2, 1)
-        swapped_pair_2 = x_pair(swapped_2)
-        kept_pair_3 = (kept_3, z_swap(kept_pair_2[1], 1))
+        swapped_3 = z_swap(gated(swapped_2, part_0), 1)
+        swapped_pair_2 = x_pair(gated(swapped_2, part_1))
+        kept_pair_3 = (kept_3, z_swap(gated(kept_pair_2[1], part_1), 1))
         sums, part_2, _ = ladder((2, 1), factors, [kept_pair_2], [swapped_pair_1], sums)
-        swapped_3, sums = after((swapped_3, sums))
-        swapped_pair_3 = x_pair(swapped_3)
+        swapped_pair_3 = x_pair(gated(swapped_3, part_2))
         sums, part_3, _ = ladder((3, 2), factors, [kept_pair_3], [swapped_pair_2], sums)
         sent, part_4, _ = ladder((3,), factors, [], [swapped_pair_3], sums, last=True)
-        own_x, own_z = keep_sums([part_0, part_1, part_2, part_3, part_4])
-        shape = (2, 2, row_count, middle)
-        left = halved(own_x.reshape(shape), x_swap(sent[0]), z_low, lambda b: z_swap(b, 1))
-        right = halved(own_z.reshape(shape), z_swap(sent[1], 1), x_index, x_swap)
+        keep_x, keep_z = keep_sums([part_0, part_1, part_2, part_3, part_4])
+        came_x = x_swap(sent[0])
+        came_z = z_swap(sent[1], 1)
+
+        def added(own, came):
+            return own + came.astype(jnp.float32)
+
+        def high_half(block, index):
+            return jnp.where(index == 0, block[:, :GROUP_ROWS], block[:, GROUP_ROWS:])
+
+        first = added(keep_x[:, :middle], came_x[:, :middle])
+        leaving = added(keep_x[:, middle:], came_x[:, middle:]).astype(jnp.bfloat16)
+        left = added(first, z_swap(leaving, 1))
+        first = added(keep_z[:GROUP_ROWS], came_z[:GROUP_ROWS])
+        leaving = added(keep_z[GROUP_ROWS:], came_z[GROUP_ROWS:]).astype(jnp.bfloat16)
+        right = added(first, x_swap(leaving))
+        left = added(
+            high_half(left, z_high), z_swap(high_half(left, 1 - z_high).astype(jnp.bfloat16), 2)
+        )
+        right = added(
+            high_half(right, z_high), z_swap(high_half(right, 1 - z_high).astype(jnp.bfloat16), 2)
+        )
+        turned = jnp.concatenate([left, right], axis=0)
+        own_half = jnp.where(x_index == 0, turned[:, :row_count], turned[:, row_count:])
+        other_half = x_swap(jnp.where(x_index == 0, turned[:, row_count:], turned[:, :row_count]))
+        by_x = jnp.stack(
+            [jnp.where(x_index == 0, own_half, other_half), jnp.where(x_index == 0, other_half, own_half)]
+        ).reshape(2, 4, row_count, row_count)
+        own_rows = jnp.transpose(by_x, (3, 1, 0, 2)).reshape(row_count, size)
+        turned = turned.astype(jnp.bfloat16).reshape(4, row_count, GROUP_ROWS)
     else:
         kept_all = lax.all_gather(kept_0, "vir", axis=0, tiled=True)
         swapped_all = lax.all_gather(swapped_0, "vir", axis=0, tiled=True)
@@ -252,10 +273,9 @@
         left = z_scatter(left.reshape(2, 2, row_count, middle), 1, 1, z_low)
         right = z_scatter(total[:, middle:].reshape(2, 2, GROUP_ROWS, middle), 1, 1, z_low)
         right = x_scatter(right.reshape(2, inner, row_count, middle))
-    own_rows = jnp.concatenate([z_scatter(left, 0, 2, z_high), z_scatter(right, 0, 2, z_high)], axis=1)
-
-    packed = own_rows.astype(jnp.bfloat16).reshape(row_count, vir_devices, row_count)
-    packed = jnp.transpose(packed, (1, 2, 0))
+        own_rows = jnp.concatenate([z_scatter(left, 0, 2, z_high), z_scatter(right, 0, 2, z_high)], axis=1)
+        packed = own_rows.astype(jnp.bfloat16).reshape(row_count, vir_devices, row_count)
+        packed = jnp.transpose(packed, (1, 2, 0))
     if inner == 2:
         def flipped(blocks):
             blocks = blocks.reshape(2, 2, *blocks.shape[1:])
@@ -263,13 +283,7 @@
             blocks = jnp.where(z_low == 1, jnp.flip(blocks, 1), blocks)
             return blocks.reshape(4, *blocks.shape[2:])
 
-        packed = packed.reshape(4, 2, row_count, row_count)
-        stays = lax.dynamic_index_in_dim(packed, x_index, 1, keepdims=False)
-        leaves = lax.dynamic_index_in_dim(packed, 1 - x_index, 1, keepdims=False)
-        came = x_swap(leaves)
-        first = jnp.where(x_index == 0, stays, came)
-        second = jnp.where(x_index == 0, came, stays)
-        turned = flipped(jnp.concatenate([first, second], axis=2))
+        turned = flipped(turned)
         came = []
         for step in range(4):
             route = [
@@ -277,7 +291,10 @@
                 for o in range(occ_devices)
                 for i in range(vir_devices)
             ]
-            came.append(lax.ppermute(turned[step], ("occ", "vir"), route))
+            leaving = turned[step]
+            if step == 3:
+                leaving = after((leaving, other_half))[0]
+            came.append(lax.ppermute(leaving, ("occ", "vir"), route))
         partner = flipped(jnp.stack(came))
     else:
         partner = y_swap(lax.all_to_all(packed, "vir", 0, 0))
@@ -287,6 +304,10 @@
     second = jnp.where(side == 0, partner, own_rows)
     numerator = jnp.stack([first, second])
 
+    if inner == 2:
+        small = (occ_energy, vir_energy, occ_irrep, vir_irrep, pair_orbitals)
+        small = after((*small, part_4[0]))[:5]
+        occ_energy, vir_energy, occ_irrep, vir_irrep, pair_orbitals = small
     pair_ids = lax.dynamic_slice_in_dim(pair_orbitals, occ_index * local_pairs, local_pairs, 0)
     row_start = vir_index * row_count
     energy_rows = lax.dynamic_slice_in_dim(vir_energy, row_start, row_count, 0)

time: 106 us -> 103 us (0.972)
  starting transfers between devices: 45.4 us -> 34.5 us
  waiting for transfers between devices: 22.4 us -> 31.3 us
  local copies, waits for them, and re-layouts: 3.94 us -> 2.72 us
    ppermute x11, waiting for transfers between devices: 12 us -> 22.6 us  [z_swap(): return lax.ppermute(block, 'vir', route)]
    ppermute x11, starting transfers between devices: 21.5 us -> 14.3 us  [z_swap(): return lax.ppermute(block, 'vir', route)]
    ppermute x10, starting transfers between devices: 14.1 us -> 9.27 us  [x_swap(): return lax.ppermute(block, 'vir', [(i, i ^ 1) for i in range(vir_devices)])]
    ppermute x10, waiting for transfers between devices: 7.86 us -> 5.85 us  [x_swap(): return lax.ppermute(block, 'vir', [(i, i ^ 1) for i in range(vir_devices)])]
  transfers between devices with their start and end apart: 26 -> 26, of which waited for: 10 -> 13; matrix products, arithmetic and copies ran while one was open for 3% -> 2% of each run, Pallas kernels for 26% -> 28%
where the time goes in v3:
time: 103 us
  starting transfers between devices  34.5 us (33%)
  waiting for transfers between devices  31.3 us (30%)
  Pallas kernels  31.2 us (30%)
  other arithmetic  2.9 us (3%)
  local copies, waits for them, and re-layouts  2.72 us (3%)
    pallas_call x5, Pallas kernels, ladder(): pl.pallas_call(functools.partial(ladder_kernel, distances, len(kept), sum...  24.5 us
    ppermute x11, waiting for transfers between devices, z_swap(): return lax.ppermute(block, 'vir', route)  22.6 us
    ppermute x11, starting transfers between devices, z_swap(): return lax.ppermute(block, 'vir', route)  14.3 us
    ppermute x10, starting transfers between devices, x_swap(): return lax.ppermute(block, 'vir', [(i, i ^ 1) for i in range(vir_devices)])  9.27 us
    ppermute x4, starting transfers between devices, per_device(): came.append(lax.ppermute(leaving, ('occ', 'vir'), route))  7.83 us
    pallas_call x1, Pallas kernels, keep_sums(): pl.pallas_call(functools.partial(keep_kernel, len(parts)), out_shape=[jax...  6.67 us
    ppermute x10, waiting for transfers between devices, x_swap(): return lax.ppermute(block, 'vir', [(i, i ^ 1) for i in range(vir_devices)])  5.85 us
    ppermute x1, starting transfers between devices, y_swap(): lax.ppermute(block, 'occ', [(i, (i + across) % occ_devices) for i in rang...  3.03 us
  transfers between devices with their start and end apart: 26, of which 13 were waited for; matrix products, arithmetic and copies ran while one was open for 2% of the time, Pallas kernels for 28%

profile of v3, /device:TPU:0, one launch (start us, length us, event | category | flops | bytes accessed | tf_op | source)
XLA Modules:
  0.0 103.2 jit_solution(9745581435614720225)
XLA Ops:
  0.0 1.1 %dynamic-slice_bitcast_fusion = (bf16[128,1024]{1,0:T(8,128)(2,1)S(1)}, bf16[128,1024]{1,0:T(8,128)(2,1)S(1)}) fusion(bf16[2,128,1024]{2,1,0:T(8,128)(2,1)} %param.7, s32[]{:T(128)S(6)} %select_n.145, s32[]{:T(128)S(6)} %select_n.144), kind=kLoop, calls=%fused_computation.28 | loop fusion | bytes 1048584 | tf_op jit(solution)/shard_map/jit(dynamic_index_in_dim)/squeeze | solution.py:201
  1.1 3.0 %collective-permute-start.1 = (bf16[128,1024]{1,0:T(8,128)(2,1)S(1)}, bf16[128,1024]{1,0:T(8,128)(2,1)S(1)}, u32[]{:S(2)}, u32[]{:S(2)}) collective-permute-start(bf16[128,1024]{1,0:T(8,128)(2,1)S(1)} %get-tuple-element.87), channel_id=1, source_target_pairs={{0,16},{8,24},{16,0},{24,8},{1,17},{9,25},{17,1},{25,9},{2,18},{10... | collective-permute-start | bytes 786440 | tf_op jit(solution)/shard_map/ppermute | solution.py:179
  4.1 1.5 %collective-permute-start = (bf16[128,1024]{1,0:T(8,128)(2,1)S(1)}, bf16[128,1024]{1,0:T(8,128)(2,1)S(1)}, u32[]{:S(2)}, u32[]{:S(2)}) collective-permute-start(bf16[128,1024]{1,0:T(8,128)(2,1)S(1)} %get-tuple-element.88.refs_0_), channel_id=1, source_target_pairs={{0,1},{1,0},{2,3},{3,2},{4,5},{5,4},{6,7},{7,6},{8,9},{9,8},{10,11... | collective-permute-start | bytes 786440 | tf_op jit(solution)/shard_map/ppermute | solution.py:184
  5.6 1.6 %collective-permute-start.8 = (bf16[128,1024]{1,0:T(8,128)(2,1)S(1)}, bf16[128,1024]{1,0:T(8,128)(2,1)S(1)}, u32[]{:S(2)}, u32[]{:S(2)}) collective-permute-start(bf16[128,1024]{1,0:T(8,128)(2,1)S(1)} %get-tuple-element.88.refs_0_), channel_id=1, source_target_pairs={{0,2},{1,3},{2,0},{3,1},{4,6},{5,7},{6,4},{7,5},{8,10},{9,11},{10,... | collective-permute-start | bytes 786440 | tf_op jit(solution)/shard_map/ppermute | solution.py:176
  7.2 2.6 %collective-permute-start.4 = (bf16[128,1024]{1,0:T(8,128)(2,1)S(1)}, bf16[128,1024]{1,0:T(8,128)(2,1)S(1)}, u32[]{:S(2)}, u32[]{:S(2)}) collective-permute-start(bf16[128,1024]{1,0:T(8,128)(2,1)S(1)} %get-tuple-element.88.refs_0_), channel_id=1, source_target_pairs={{0,4},{1,5},{2,6},{3,7},{4,0},{5,1},{6,2},{7,3},{8,12},{9,13},{10,... | collective-permute-start | bytes 786440 | tf_op jit(solution)/shard_map/ppermute | solution.py:176
  10.4 1.8 %collective-permute-start.5 = (bf16[128,1024]{1,0:T(8,128)(2,1)S(1)}, bf16[128,1024]{1,0:T(8,128)(2,1)S(1)}, u32[]{:S(2)}, u32[]{:S(2)}) collective-permute-start(bf16[128,1024]{1,0:T(8,128)(2,1)S(1)} %collective-permute-done.1.refs_2_), channel_id=1, source_target_pairs={{0,2},{1,3},{2,0},{3,1},{4,6},{5,7},{6,4},{7,5},{8,10},{9,11},{10,... | collective-permute-start | bytes 786440 | tf_op jit(solution)/shard_map/ppermute | solution.py:176
  12.2 2.6 %collective-permute-start.2 = (bf16[128,1024]{1,0:T(8,128)(2,1)S(1)}, bf16[128,1024]{1,0:T(8,128)(2,1)S(1)}, u32[]{:S(2)}, u32[]{:S(2)}) collective-permute-start(bf16[128,1024]{1,0:T(8,128)(2,1)S(1)} %collective-permute-done.1.refs_2_), channel_id=1, source_target_pairs={{0,4},{1,5},{2,6},{3,7},{4,0},{5,1},{6,2},{7,3},{8,12},{9,13},{10,... | collective-permute-start | bytes 786440 | tf_op jit(solution)/shard_map/ppermute | solution.py:176
  14.8 1.5 %collective-permute-start.10 = (bf16[128,1024]{1,0:T(8,128)(2,1)S(1)}, bf16[128,1024]{1,0:T(8,128)(2,1)S(1)}, u32[]{:S(2)}, u32[]{:S(2)}) collective-permute-start(bf16[128,1024]{1,0:T(8,128)(2,1)S(1)} %collective-permute-done.1.refs_2_), channel_id=1, source_target_pairs={{0,1},{1,0},{2,3},{3,2},{4,5},{5,4},{6,7},{7,6},{8,9},{9,8},{10,11... | collective-permute-start | bytes 786440 | tf_op jit(solution)/shard_map/ppermute | solution.py:184
  16.3 5.3 %collective-permute-done.8.refs_0_ = bf16[128,1024]{1,0:T(8,128)(2,1)S(1)} collective-permute-done((bf16[128,1024]{1,0:T(8,128)(2,1)S(1)}, bf16[128,1024]{1,0:T(8,128)(2,1)S(1)}, u32[]{:S(2)}, u32[]{:S(2)}) %collective-permute-start.8) | collective-permute-done | bytes 262176 | tf_op jit(solution)/shard_map/ppermute | solution.py:176
  22.1 5.0 %shard_map.73 = (f32[256,1024]{1,0:T(8,128)S(1)}, f32[512,512]{1,0:T(8,128)S(1)}, bf16[1024,768]{1,0:T(8,128)(2,1)S(1)}, bf16[1024,768]{1,0:T(8,128)(2,1)S(1)}, bf16[3,1024,1024]{2,1,0:T(8,128)(2,1)S(1)}) custom-call(bf16[3,1024,1024]{2,1,0:T(8,128)(2,1)} %factor_ref.1, bf16[128,1024]{1,0:T(8,128)(2,1)S(1)} %get-tuple-element.88.refs_0_, ...), custom_call_target="tpu_custom_call" | custom-call | bytes 11010048 | tf_op jit(solution)/shard_map/pallas_call | solution.py:108
  27.1 2.7 %collective-permute-done.5.refs_2_ = bf16[128,1024]{1,0:T(8,128)(2,1)S(1)} collective-permute-done((bf16[128,1024]{1,0:T(8,128)(2,1)S(1)}, bf16[128,1024]{1,0:T(8,128)(2,1)S(1)}, u32[]{:S(2)}, u32[]{:S(2)}) %collective-permute-start.5) | collective-permute-done | bytes 262176 | tf_op jit(solution)/shard_map/ppermute | solution.py:176
  30.4 2.0 %collective-permute-done.2.refs_2_ = bf16[128,1024]{1,0:T(8,128)(2,1)S(1)} collective-permute-done((bf16[128,1024]{1,0:T(8,128)(2,1)S(1)}, bf16[128,1024]{1,0:T(8,128)(2,1)S(1)}, u32[]{:S(2)}, u32[]{:S(2)}) %collective-permute-start.2) | collective-permute-done | bytes 262176 | tf_op jit(solution)/shard_map/ppermute | solution.py:176
  33.9 5.5 %shard_map.74 = (f32[256,1024]{1,0:T(8,128)S(1)}, f32[512,512]{1,0:T(8,128)S(1)}, bf16[1024,1536]{1,0:T(8,128)(2,1)S(1)}, bf16[1024,1536]{1,0:T(8,128)(2,1)S(1)}) custom-call(bf16[3,1024,1024]{2,1,0:T(8,128)(2,1)S(1)} %get-tuple-element.42.factor_ref, ...), custom_call_target="tpu_custom_call", output_to_operand_aliasing={{0}: (5, {}), {1}: (6, {})} | custom-call | flops 3221225472 | bytes 11534336 | tf_op jit(solution)/shard_map/pallas_call | solution.py:108
  40.3 1.7 %collective-permute-start.13 = (bf16[128,1024]{1,0:T(8,128)(2,1)S(1)}, bf16[128,1024]{1,0:T(8,128)(2,1)S(1)}, u32[]{:S(2)}, u32[]{:S(2)}) collective-permute-start(bf16[128,1024]{1,0:T(8,128)(2,1)S(1)} %collective-permute-done.6.refs_1_), channel_id=1, source_target_pairs={{0,2},{1,3},{2,0},{3,1},{4,6},{5,7},{6,4},{7,5},{8,10},{9,11},{10,... | collective-permute-start | bytes 786440 | tf_op jit(solution)/shard_map/ppermute | solution.py:176
  42.0 2.2 %collective-permute-done.7.refs_3_ = bf16[128,1024]{1,0:T(8,128)(2,1)S(1)} collective-permute-done((bf16[128,1024]{1,0:T(8,128)(2,1)S(1)}, bf16[128,1024]{1,0:T(8,128)(2,1)S(1)}, u32[]{:S(2)}, u32[]{:S(2)}) %collective-permute-start.7) | collective-permute-done | bytes 262176 | tf_op jit(solution)/shard_map/ppermute | solution.py:184
  44.2 5.7 %shard_map.75 = (f32[256,1024]{1,0:T(8,128)S(1)}, f32[512,512]{1,0:T(8,128)S(1)}, bf16[1024,1536]{1,0:T(8,128)(2,1)S(1)}, bf16[1024,1536]{1,0:T(8,128)(2,1)S(1)}) custom-call(bf16[3,1024,1024]{2,1,0:T(8,128)(2,1)S(1)} %get-tuple-element.42.factor_ref, ...), custom_call_target="tpu_custom_call", output_to_operand_aliasing={{0}: (5, {}), {1}: (6, {})} | custom-call | flops 3221225472 | bytes 11534336 | tf_op jit(solution)/shard_map/pallas_call | solution.py:108
  50.0 5.5 %shard_map.76 = (f32[256,1024]{1,0:T(8,128)S(1)}, f32[512,512]{1,0:T(8,128)S(1)}, bf16[1024,1536]{1,0:T(8,128)(2,1)S(1)}, bf16[1024,1536]{1,0:T(8,128)(2,1)S(1)}) custom-call(bf16[3,1024,1024]{2,1,0:T(8,128)(2,1)S(1)} %get-tuple-element.42.factor_ref, ...), custom_call_target="tpu_custom_call", output_to_operand_aliasing={{0}: (5, {}), {1}: (6, {})} | custom-call | flops 3221225472 | bytes 11534336 | tf_op jit(solution)/shard_map/pallas_call | solution.py:108
  56.4 2.8 %shard_map.77 = (bf16[256,1024]{1,0:T(8,128)(2,1)S(1)}, bf16[512,512]{1,0:T(8,128)(2,1)S(1)}, bf16[1024,768]{1,0:T(8,128)(2,1)S(1)}, bf16[1024,768]{1,0:T(8,128)(2,1)S(1)}) custom-call(bf16[3,1024,1024]{2,1,0:T(8,128)(2,1)S(1)} %get-tuple-element.42.factor_ref, bf16[128,1024]{1,0:T(8,128)(2,1)S(1)} %collective-permute-done.3.refs_0_, ...), custom_call_target="tpu_custom_call" | custom-call | flops 1610612736 | bytes 11010048 | tf_op jit(solution)/shard_map/pallas_call | solution.py:108
  59.4 1.3 %collective-permute-start.15 = (bf16[256,1024]{1,0:T(8,128)(2,1)S(1)}, bf16[256,1024]{1,0:T(8,128)(2,1)S(1)}, u32[]{:S(2)}, u32[]{:S(2)}) collective-permute-start(bf16[256,1024]{1,0:T(8,128)(2,1)S(1)} %get-tuple-element.73), channel_id=1, source_target_pairs={{0,1},{1,0},{2,3},{3,2},{4,5},{5,4},{6,7},{7,6},{8,9},{9,8},{10,11... | collective-permute-start | bytes 1572872 | tf_op jit(solution)/shard_map/ppermute | solution.py:184
  60.7 6.7 %shard_map.78 = (f32[256,1024]{1,0:T(8,128)S(1)}, f32[512,512]{1,0:T(8,128)S(1)}) custom-call(bf16[1024,768]{1,0:T(8,128)(2,1)S(1)} %get-tuple-element.43.refs_0_, bf16[1024,768]{1,0:T(8,128)(2,1)S(1)} %get-tuple-element.66.refs_1_, bf16[1024,1536]{1,0:T(8,128)(2,1)S(1)} %get-tuple-element.55.refs_2_, bf16[1024,1536]{1,0:T(8,128)(2,1)S(1)} %get-tuple-element.67.refs_3_, ...), custom_call_target="tpu_custom_call" | custom-call | flops 6442450944 | bytes 27262976 | tf_op jit(solution)/shard_map/pallas_call | solution.py:145
  68.0 2.2 %collective-permute-done.15 = bf16[256,1024]{1,0:T(8,128)(2,1)S(1)} collective-permute-done((bf16[256,1024]{1,0:T(8,128)(2,1)S(1)}, bf16[256,1024]{1,0:T(8,128)(2,1)S(1)}, u32[]{:S(2)}, u32[]{:S(2)}) %collective-permute-start.15) | collective-permute-done | bytes 524320 | tf_op jit(solution)/shard_map/ppermute | solution.py:184
  70.5 2.1 %collective-permute-done.18 = bf16[512,512]{1,0:T(8,128)(2,1)S(1)} collective-permute-done((bf16[512,512]{1,0:T(8,128)(2,1)S(1)}, bf16[512,512]{1,0:T(8,128)(2,1)S(1)}, u32[]{:S(2)}, u32[]{:S(2)}) %collective-permute-start.18) | collective-permute-done | bytes 524320 | tf_op jit(solution)/shard_map/ppermute | solution.py:176
  73.6 4.7 %collective-permute-done.16 = bf16[256,512]{1,0:T(8,128)(2,1)S(1)} collective-permute-done((bf16[256,512]{1,0:T(8,128)(2,1)S(1)}, bf16[256,512]{1,0:T(8,128)(2,1)S(1)}, u32[]{:S(2)}, u32[]{:S(2)}) %collective-permute-start.16) | collective-permute-done | bytes 262176 | tf_op jit(solution)/shard_map/ppermute | solution.py:176
  78.5 1.1 %collective-permute-start.17 = (bf16[256,256]{1,0:T(8,128)(2,1)S(1)}, bf16[256,256]{1,0:T(8,128)(2,1)S(1)}, u32[]{:S(2)}, u32[]{:S(2)}) collective-permute-start(bf16[256,256]{1,0:T(8,128)(2,1)S(1)} %select_convert_fusion.1), channel_id=1, source_target_pairs={{0,4},{1,5},{2,6},{3,7},{4,0},{5,1},{6,2},{7,3},{8,12},{9,13},{10,... | collective-permute-start | bytes 393224 | tf_op jit(solution)/shard_map/ppermute | solution.py:176
  79.7 2.0 %collective-permute-start.20 = (bf16[256,256]{1,0:T(8,128)(2,1)S(1)}, bf16[256,256]{1,0:T(8,128)(2,1)S(1)}, u32[]{:S(2)}, u32[]{:S(2)}) collective-permute-start(bf16[256,256]{1,0:T(8,128)(2,1)S(1)} %select_convert_fusion), channel_id=1, source_target_pairs={{0,4},{1,5},{2,6},{3,7},{4,0},{5,1},{6,2},{7,3},{8,12},{9,13},{10,... | collective-permute-start | bytes 393224 | tf_op jit(solution)/shard_map/ppermute | solution.py:176
  81.7 4.4 %collective-permute-done.17 = bf16[256,256]{1,0:T(8,128)(2,1)S(1)} collective-permute-done((bf16[256,256]{1,0:T(8,128)(2,1)S(1)}, bf16[256,256]{1,0:T(8,128)(2,1)S(1)}, u32[]{:S(2)}, u32[]{:S(2)}) %collective-permute-start.17) | collective-permute-done | bytes 131104 | tf_op jit(solution)/shard_map/ppermute | solution.py:176
  86.1 1.4 %collective-permute-done.20 = bf16[256,256]{1,0:T(8,128)(2,1)S(1)} collective-permute-done((bf16[256,256]{1,0:T(8,128)(2,1)S(1)}, bf16[256,256]{1,0:T(8,128)(2,1)S(1)}, u32[]{:S(2)}, u32[]{:S(2)}) %collective-permute-start.20) | collective-permute-done | bytes 131104 | tf_op jit(solution)/shard_map/ppermute | solution.py:176
  87.6 1.6 %collective-permute-start.21 = (f32[512,128]{1,0:T(8,128)S(1)}, f32[512,128]{1,0:T(8,128)S(1)}, u32[]{:S(2)}, u32[]{:S(2)}) collective-permute-start(f32[512,128]{1,0:T(8,128)S(1)} %broadcast_select_fusion.4), channel_id=1, source_target_pairs={{0,1},{1,0},{2,3},{3,2},{4,5},{5,4},{6,7},{7,6},{8,9},{9,8},{10,11... | collective-permute-start | bytes 786440 | tf_op jit(solution)/shard_map/ppermute | solution.py:184
  90.1 3.2 %collective-permute-start.24 = (bf16[128,256]{1,0:T(8,128)(2,1)S(1)}, bf16[128,256]{1,0:T(8,128)(2,1)S(1)}, u32[]{:S(2)}, u32[]{:S(2)}) collective-permute-start(bf16[128,256]{1,0:T(8,128)(2,1)S(1)} %get-tuple-element.91), channel_id=1, source_target_pairs={{0,20},{1,21},{2,22},{3,23},{4,16},{5,17},{6,18},{7,19},{8,28},{9,... | collective-permute-start | bytes 196616 | tf_op jit(solution)/shard_map/ppermute | solution.py:297
  94.0 3.9 %collective-permute-start.25 = (bf16[128,256]{1,0:T(8,128)(2,1)S(1)}, bf16[128,256]{1,0:T(8,128)(2,1)S(1)}, u32[]{:S(2)}, u32[]{:S(2)}) collective-permute-start(bf16[128,256]{1,0:T(8,128)(2,1)S(1)} %get-tuple-element.76), channel_id=1, source_target_pairs={{0,22},{1,23},{2,20},{3,21},{4,18},{5,19},{6,16},{7,17},{8,30},{9,... | collective-permute-start | bytes 196616 | tf_op jit(solution)/shard_map/ppermute | solution.py:297
  98.8 2.2 %collective-permute-done.25 = bf16[128,256]{1,0:T(8,128)(2,1)S(1)} collective-permute-done((bf16[128,256]{1,0:T(8,128)(2,1)S(1)}, bf16[128,256]{1,0:T(8,128)(2,1)S(1)}, u32[]{:S(2)}, u32[]{:S(2)}) %collective-permute-start.25) | collective-permute-done | bytes 65568 | tf_op jit(solution)/shard_map/ppermute | solution.py:297
  101.9 1.3 %fusion = f32[2,128,1024]{2,1,0:T(8,128)} fusion(f32[1,128,1024]{2,1,0:T(8,128)S(1)} %get-tuple-element.84, f32[1,128,1024]{2,1,0:T(8,128)S(1)} %get-tuple-element.83, f32[2]{0:T(128)S(1)} %add.91, f32[128,1024]{1,0:T(8,128)S(1)} %broadcast_add_fusion, s32[1024]{0:T(1024)S(1)} %copy-done.2, s32[2,128]{1,0:T(2,128)S(1)} %broadcast_xor_fusion), kind=kLoop, calls=%fused_computation.1 | loop fusion | flops 1572864 | bytes 2626568 | tf_op jit(solution)/shard_map/jit(_where)/select_n | solution.py:332
  (72 shorter events, 10.6 us)
Async XLA Ops:
  0.0 59.2 %copy-start = (s32[8,2]{0,1:T(2,128)S(1)}, s32[8,2]{0,1:T(2,128)}, u32[]{:S(2)}) copy-start(s32[8,2]{0,1:T(2,128)} %param.13) | copy-start | bytes 196
  1.1 9.3 %collective-permute-start.1 = (bf16[128,1024]{1,0:T(8,128)(2,1)S(1)}, bf16[128,1024]{1,0:T(8,128)(2,1)S(1)}, u32[]{:S(2)}, u32[]{:S(2)}) collective-permute-start(bf16[128,1024]{1,0:T(8,128)(2,1)S(1)} %get-tuple-element.87), channel_id=1, source_target_pairs={{0,16},{8,24},{16,0},{24,8},{1,17},{9,25},{17,1},{25,9},{2,18},{10... | collective-permute-start | bytes 786440 | tf_op jit(solution)/shard_map/ppermute | solution.py:179
  4.1 10.7 %collective-permute-start = (bf16[128,1024]{1,0:T(8,128)(2,1)S(1)}, bf16[128,1024]{1,0:T(8,128)(2,1)S(1)}, u32[]{:S(2)}, u32[]{:S(2)}) collective-permute-start(bf16[128,1024]{1,0:T(8,128)(2,1)S(1)} %get-tuple-element.88.refs_0_), channel_id=1, source_target_pairs={{0,1},{1,0},{2,3},{3,2},{4,5},{5,4},{6,7},{7,6},{8,9},{9,8},{10,11... | collective-permute-start | bytes 786440 | tf_op jit(solution)/shard_map/ppermute | solution.py:184
  5.6 16.0 %collective-permute-start.8 = (bf16[128,1024]{1,0:T(8,128)(2,1)S(1)}, bf16[128,1024]{1,0:T(8,128)(2,1)S(1)}, u32[]{:S(2)}, u32[]{:S(2)}) collective-permute-start(bf16[128,1024]{1,0:T(8,128)(2,1)S(1)} %get-tuple-element.88.refs_0_), channel_id=1, source_target_pairs={{0,2},{1,3},{2,0},{3,1},{4,6},{5,7},{6,4},{7,5},{8,10},{9,11},{10,... | collective-permute-start | bytes 786440 | tf_op jit(solution)/shard_map/ppermute | solution.py:176
  7.2 19.9 %collective-permute-start.4 = (bf16[128,1024]{1,0:T(8,128)(2,1)S(1)}, bf16[128,1024]{1,0:T(8,128)(2,1)S(1)}, u32[]{:S(2)}, u32[]{:S(2)}) collective-permute-start(bf16[128,1024]{1,0:T(8,128)(2,1)S(1)} %get-tuple-element.88.refs_0_), channel_id=1, source_target_pairs={{0,4},{1,5},{2,6},{3,7},{4,0},{5,1},{6,2},{7,3},{8,12},{9,13},{10,... | collective-permute-start | bytes 786440 | tf_op jit(solution)/shard_map/ppermute | solution.py:176
  10.4 19.4 %collective-permute-start.5 = (bf16[128,1024]{1,0:T(8,128)(2,1)S(1)}, bf16[128,1024]{1,0:T(8,128)(2,1)S(1)}, u32[]{:S(2)}, u32[]{:S(2)}) collective-permute-start(bf16[128,1024]{1,0:T(8,128)(2,1)S(1)} %collective-permute-done.1.refs_2_), channel_id=1, source_target_pairs={{0,2},{1,3},{2,0},{3,1},{4,6},{5,7},{6,4},{7,5},{8,10},{9,11},{10,... | collective-permute-start | bytes 786440 | tf_op jit(solution)/shard_map/ppermute | solution.py:176
  12.2 20.1 %collective-permute-start.2 = (bf16[128,1024]{1,0:T(8,128)(2,1)S(1)}, bf16[128,1024]{1,0:T(8,128)(2,1)S(1)}, u32[]{:S(2)}, u32[]{:S(2)}) collective-permute-start(bf16[128,1024]{1,0:T(8,128)(2,1)S(1)} %collective-permute-done.1.refs_2_), channel_id=1, source_target_pairs={{0,4},{1,5},{2,6},{3,7},{4,0},{5,1},{6,2},{7,3},{8,12},{9,13},{10,... | collective-permute-start | bytes 786440 | tf_op jit(solution)/shard_map/ppermute | solution.py:176
  14.8 18.1 %collective-permute-start.10 = (bf16[128,1024]{1,0:T(8,128)(2,1)S(1)}, bf16[128,1024]{1,0:T(8,128)(2,1)S(1)}, u32[]{:S(2)}, u32[]{:S(2)}) collective-permute-start(bf16[128,1024]{1,0:T(8,128)(2,1)S(1)} %collective-permute-done.1.refs_2_), channel_id=1, source_target_pairs={{0,1},{1,0},{2,3},{3,2},{4,5},{5,4},{6,7},{7,6},{8,9},{9,8},{10,11... | collective-permute-start | bytes 786440 | tf_op jit(solution)/shard_map/ppermute | solution.py:184
  21.6 12.3 %collective-permute-start.9 = (bf16[128,1024]{1,0:T(8,128)(2,1)S(1)}, bf16[128,1024]{1,0:T(8,128)(2,1)S(1)}, u32[]{:S(2)}, u32[]{:S(2)}) collective-permute-start(bf16[128,1024]{1,0:T(8,128)(2,1)S(1)} %collective-permute-done.8.refs_0_), channel_id=1, source_target_pairs={{0,1},{1,0},{2,3},{3,2},{4,5},{5,4},{6,7},{7,6},{8,9},{9,8},{10,11... | collective-permute-start | bytes 786440 | tf_op jit(solution)/shard_map/ppermute | solution.py:184
  29.8 10.5 %collective-permute-start.6 = (bf16[128,1024]{1,0:T(8,128)(2,1)S(1)}, bf16[128,1024]{1,0:T(8,128)(2,1)S(1)}, u32[]{:S(2)}, u32[]{:S(2)}) collective-permute-start(bf16[128,1024]{1,0:T(8,128)(2,1)S(1)} %collective-permute-done.4.refs_0_), channel_id=1, source_target_pairs={{0,1},{1,0},{2,3},{3,2},{4,5},{5,4},{6,7},{7,6},{8,9},{9,8},{10,11... | collective-permute-start | bytes 786440 | tf_op jit(solution)/shard_map/ppermute | solution.py:184
  30.4 19.6 %collective-permute-start.12 = (bf16[128,1024]{1,0:T(8,128)(2,1)S(1)}, bf16[128,1024]{1,0:T(8,128)(2,1)S(1)}, u32[]{:S(2)}, u32[]{:S(2)}) collective-permute-start(bf16[128,1024]{1,0:T(8,128)(2,1)S(1)} %collective-permute-done.4.refs_0_), channel_id=1, source_target_pairs={{0,2},{1,3},{2,0},{3,1},{4,6},{5,7},{6,4},{7,5},{8,10},{9,11},{10,... | collective-permute-start | bytes 786440 | tf_op jit(solution)/shard_map/ppermute | solution.py:176
  32.3 11.9 %collective-permute-start.7 = (bf16[128,1024]{1,0:T(8,128)(2,1)S(1)}, bf16[128,1024]{1,0:T(8,128)(2,1)S(1)}, u32[]{:S(2)}, u32[]{:S(2)}) collective-permute-start(bf16[128,1024]{1,0:T(8,128)(2,1)S(1)} %collective-permute-done.5.refs_2_), channel_id=1, source_target_pairs={{0,1},{1,0},{2,3},{3,2},{4,5},{5,4},{6,7},{7,6},{8,9},{9,8},{10,11... | collective-permute-start | bytes 786440 | tf_op jit(solution)/shard_map/ppermute | solution.py:184
  32.9 17.0 %collective-permute-start.3 = (bf16[128,1024]{1,0:T(8,128)(2,1)S(1)}, bf16[128,1024]{1,0:T(8,128)(2,1)S(1)}, u32[]{:S(2)}, u32[]{:S(2)}) collective-permute-start(bf16[128,1024]{1,0:T(8,128)(2,1)S(1)} %collective-permute-done.2.refs_2_), channel_id=1, source_target_pairs={{0,2},{1,3},{2,0},{3,1},{4,6},{5,7},{6,4},{7,5},{8,10},{9,11},{10,... | collective-permute-start | bytes 786440 | tf_op jit(solution)/shard_map/ppermute | solution.py:176
  39.4 10.6 %collective-permute-start.14 = (bf16[128,1024]{1,0:T(8,128)(2,1)S(1)}, bf16[128,1024]{1,0:T(8,128)(2,1)S(1)}, u32[]{:S(2)}, u32[]{:S(2)}) collective-permute-start(bf16[128,1024]{1,0:T(8,128)(2,1)S(1)} %collective-permute-done.2.refs_2_), channel_id=1, source_target_pairs={{0,1},{1,0},{2,3},{3,2},{4,5},{5,4},{6,7},{7,6},{8,9},{9,8},{10,11... | collective-permute-start | bytes 786440 | tf_op jit(solution)/shard_map/ppermute | solution.py:184
  40.3 9.7 %collective-permute-start.13 = (bf16[128,1024]{1,0:T(8,128)(2,1)S(1)}, bf16[128,1024]{1,0:T(8,128)(2,1)S(1)}, u32[]{:S(2)}, u32[]{:S(2)}) collective-permute-start(bf16[128,1024]{1,0:T(8,128)(2,1)S(1)} %collective-permute-done.6.refs_1_), channel_id=1, source_target_pairs={{0,2},{1,3},{2,0},{3,1},{4,6},{5,7},{6,4},{7,5},{8,10},{9,11},{10,... | collective-permute-start | bytes 786440 | tf_op jit(solution)/shard_map/ppermute | solution.py:176
  49.9 6.4 %collective-permute-start.11 = (bf16[128,1024]{1,0:T(8,128)(2,1)S(1)}, bf16[128,1024]{1,0:T(8,128)(2,1)S(1)}, u32[]{:S(2)}, u32[]{:S(2)}) collective-permute-start(bf16[128,1024]{1,0:T(8,128)(2,1)S(1)} %collective-permute-done.3.refs_0_), channel_id=1, source_target_pairs={{0,1},{1,0},{2,3},{3,2},{4,5},{5,4},{6,7},{7,6},{8,9},{9,8},{10,11... | collective-permute-start | bytes 786440 | tf_op jit(solution)/shard_map/ppermute | solution.py:184
  56.3 2.9 %copy-start.2 = (s32[1024]{0:T(1024)S(1)}, s32[1024]{0:T(1024)}, u32[]{:S(2)}) copy-start(s32[1024]{0:T(1024)} %param.12) | copy-start | bytes 12292
  56.3 3.0 %copy-start.1 = (f32[1024]{0:T(1024)S(1)}, f32[1024]{0:T(1024)}, u32[]{:S(2)}) copy-start(f32[1024]{0:T(1024)} %param.10) | copy-start | bytes 12292
  59.4 10.7 %collective-permute-start.15 = (bf16[256,1024]{1,0:T(8,128)(2,1)S(1)}, bf16[256,1024]{1,0:T(8,128)(2,1)S(1)}, u32[]{:S(2)}, u32[]{:S(2)}) collective-permute-start(bf16[256,1024]{1,0:T(8,128)(2,1)S(1)} %get-tuple-element.73), channel_id=1, source_target_pairs={{0,1},{1,0},{2,3},{3,2},{4,5},{5,4},{6,7},{7,6},{8,9},{9,8},{10,11... | collective-permute-start | bytes 1572872 | tf_op jit(solution)/shard_map/ppermute | solution.py:184
  60.7 12.0 %collective-permute-start.18 = (bf16[512,512]{1,0:T(8,128)(2,1)S(1)}, bf16[512,512]{1,0:T(8,128)(2,1)S(1)}, u32[]{:S(2)}, u32[]{:S(2)}) collective-permute-start(bf16[512,512]{1,0:T(8,128)(2,1)S(1)} %get-tuple-element.75), channel_id=1, source_target_pairs={{0,2},{1,3},{2,0},{3,1},{4,6},{5,7},{6,4},{7,5},{8,10},{9,11},{10,... | collective-permute-start | bytes 1572872 | tf_op jit(solution)/shard_map/ppermute | solution.py:176
  60.7 6.7 %copy-start.3 = (s32[100]{0:T(128)S(1)}, s32[100]{0:T(128)}, u32[]{:S(2)}) copy-start(s32[100]{0:T(128)} %param.11) | copy-start | bytes 1204
  60.7 9.6 %copy-start.4 = (f32[100]{0:T(128)S(1)}, f32[100]{0:T(128)}, u32[]{:S(2)}) copy-start(f32[100]{0:T(128)} %param.9) | copy-start | bytes 1204
  70.2 8.1 %collective-permute-start.16 = (bf16[256,512]{1,0:T(8,128)(2,1)S(1)}, bf16[256,512]{1,0:T(8,128)(2,1)S(1)}, u32[]{:S(2)}, u32[]{:S(2)}) collective-permute-start(bf16[256,512]{1,0:T(8,128)(2,1)S(1)} %add_convert_fusion.1), channel_id=1, source_target_pairs={{0,2},{1,3},{2,0},{3,1},{4,6},{5,7},{6,4},{7,5},{8,10},{9,11},{10,... | collective-permute-start | bytes 786440 | tf_op jit(solution)/shard_map/ppermute | solution.py:176
  72.7 6.8 %collective-permute-start.19 = (bf16[256,512]{1,0:T(8,128)(2,1)S(1)}, bf16[256,512]{1,0:T(8,128)(2,1)S(1)}, u32[]{:S(2)}, u32[]{:S(2)}) collective-permute-start(bf16[256,512]{1,0:T(8,128)(2,1)S(1)} %add_convert_fusion), channel_id=1, source_target_pairs={{0,1},{1,0},{2,3},{3,2},{4,5},{5,4},{6,7},{7,6},{8,9},{9,8},{10,11... | collective-permute-start | bytes 786440 | tf_op jit(solution)/shard_map/ppermute | solution.py:184
  78.5 7.6 %collective-permute-start.17 = (bf16[256,256]{1,0:T(8,128)(2,1)S(1)}, bf16[256,256]{1,0:T(8,128)(2,1)S(1)}, u32[]{:S(2)}, u32[]{:S(2)}) collective-permute-start(bf16[256,256]{1,0:T(8,128)(2,1)S(1)} %select_convert_fusion.1), channel_id=1, source_target_pairs={{0,4},{1,5},{2,6},{3,7},{4,0},{5,1},{6,2},{7,3},{8,12},{9,13},{10,... | collective-permute-start | bytes 393224 | tf_op jit(solution)/shard_map/ppermute | solution.py:176
  79.7 7.8 %collective-permute-start.20 = (bf16[256,256]{1,0:T(8,128)(2,1)S(1)}, bf16[256,256]{1,0:T(8,128)(2,1)S(1)}, u32[]{:S(2)}, u32[]{:S(2)}) collective-permute-start(bf16[256,256]{1,0:T(8,128)(2,1)S(1)} %select_convert_fusion), channel_id=1, source_target_pairs={{0,4},{1,5},{2,6},{3,7},{4,0},{5,1},{6,2},{7,3},{8,12},{9,13},{10,... | collective-permute-start | bytes 393224 | tf_op jit(solution)/shard_map/ppermute | solution.py:176
  87.6 6.4 %collective-permute-start.21 = (f32[512,128]{1,0:T(8,128)S(1)}, f32[512,128]{1,0:T(8,128)S(1)}, u32[]{:S(2)}, u32[]{:S(2)}) collective-permute-start(f32[512,128]{1,0:T(8,128)S(1)} %broadcast_select_fusion.4), channel_id=1, source_target_pairs={{0,1},{1,0},{2,3},{3,2},{4,5},{5,4},{6,7},{7,6},{8,9},{9,8},{10,11... | collective-permute-start | bytes 786440 | tf_op jit(solution)/shard_map/ppermute | solution.py:184
  89.3 9.4 %collective-permute-start.22 = (bf16[128,256]{1,0:T(8,128)(2,1)S(1)}, bf16[128,256]{1,0:T(8,128)(2,1)S(1)}, u32[]{:S(2)}, u32[]{:S(2)}) collective-permute-start(bf16[128,256]{1,0:T(8,128)(2,1)S(1)} %get-tuple-element.89), channel_id=1, source_target_pairs={{0,16},{1,17},{2,18},{3,19},{4,20},{5,21},{6,22},{7,23},{8,24},{9,... | collective-permute-start | bytes 196616 | tf_op jit(solution)/shard_map/ppermute | solution.py:297
  89.4 9.3 %collective-permute-start.23 = (bf16[128,256]{1,0:T(8,128)(2,1)S(1)}, bf16[128,256]{1,0:T(8,128)(2,1)S(1)}, u32[]{:S(2)}, u32[]{:S(2)}) collective-permute-start(bf16[128,256]{1,0:T(8,128)(2,1)S(1)} %get-tuple-element.92), channel_id=1, source_target_pairs={{0,18},{1,19},{2,16},{3,17},{4,22},{5,23},{6,20},{7,21},{8,26},{9,... | collective-permute-start | bytes 196616 | tf_op jit(solution)/shard_map/ppermute | solution.py:297
  90.1 8.7 %collective-permute-start.24 = (bf16[128,256]{1,0:T(8,128)(2,1)S(1)}, bf16[128,256]{1,0:T(8,128)(2,1)S(1)}, u32[]{:S(2)}, u32[]{:S(2)}) collective-permute-start(bf16[128,256]{1,0:T(8,128)(2,1)S(1)} %get-tuple-element.91), channel_id=1, source_target_pairs={{0,20},{1,21},{2,22},{3,23},{4,16},{5,17},{6,18},{7,19},{8,28},{9,... | collective-permute-start | bytes 196616 | tf_op jit(solution)/shard_map/ppermute | solution.py:297
  94.0 7.0 %collective-permute-start.25 = (bf16[128,256]{1,0:T(8,128)(2,1)S(1)}, bf16[128,256]{1,0:T(8,128)(2,1)S(1)}, u32[]{:S(2)}, u32[]{:S(2)}) collective-permute-start(bf16[128,256]{1,0:T(8,128)(2,1)S(1)} %get-tuple-element.76), channel_id=1, source_target_pairs={{0,22},{1,23},{2,20},{3,21},{4,18},{5,19},{6,16},{7,17},{8,30},{9,... | collective-permute-start | bytes 196616 | tf_op jit(solution)/shard_map/ppermute | solution.py:297

commit v4 on v3

--- a/solution.py
+++ b/solution.py
@@ -114,7 +114,7 @@
         input_output_aliases=aliases,
         compiler_params=pltpu.CompilerParams(vmem_limit_bytes=VMEM_MIB * 1024 * 1024),
         cost_estimate=pl.CostEstimate(
-            flops=(0 if loads else 2) * factor_count * width * size * size,
+            flops=(1 if loads else 2) * factor_count * width * size * size,
             bytes_accessed=2 * factor_count * size * size + 4 * size * size + 2 * width * size,
             transcendentals=0,
         ),
@@ -253,7 +253,13 @@
         )
         turned = jnp.concatenate([left, right], axis=0)
         own_half = jnp.where(x_index == 0, turned[:, :row_count], turned[:, row_count:])
-        other_half = x_swap(jnp.where(x_index == 0, turned[:, row_count:], turned[:, :row_count]))
+        other_half = jnp.concatenate(
+            [
+                x_swap(jnp.where(x_index == 0, part[:, row_count:], part[:, :row_count]))
+                for part in (left, right)
+            ],
+            axis=0,
+        )
         by_x = jnp.stack(
             [jnp.where(x_index == 0, own_half, other_half), jnp.where(x_index == 0, other_half, own_half)]
         ).reshape(2, 4, row_count, row_count)
@@ -292,7 +298,7 @@
                 for i in range(vir_devices)
             ]
             leaving = turned[step]
-            if step == 3:
+            if step == 1:
                 leaving = after((leaving, other_half))[0]
             came.append(lax.ppermute(leaving, ("occ", "vir"), route))
         partner = flipped(jnp.stack(came))

time: 103 us -> 102 us (level)
  waiting for transfers between devices: 31.3 us -> 25 us
  starting transfers between devices: 34.5 us -> 39.1 us
    ppermute x10 -> x11, starting transfers between devices: 9.27 us -> 14.6 us  [x_swap(): return lax.ppermute(block, 'vir', [(i, i ^ 1) for i in range(vir_devices)])]
    ppermute x11, waiting for transfers between devices: 22.6 us -> 18.1 us  [z_swap(): return lax.ppermute(block, 'vir', route)]
    ppermute x4, starting transfers between devices: 7.83 us -> 6.04 us  [per_device(): came.append(lax.ppermute(leaving, ('occ', 'vir'), route))]
    ppermute x10 -> x11, waiting for transfers between devices: 5.85 us -> 4.52 us  [x_swap(): return lax.ppermute(block, 'vir', [(i, i ^ 1) for i in range(vir_devices)])]
    ppermute x11, starting transfers between devices: 14.3 us -> 15.4 us  [z_swap(): return lax.ppermute(block, 'vir', route)]
  transfers between devices with their start and end apart: 26 -> 27, of which waited for: 13 -> 13; matrix products, arithmetic and copies ran while one was open for 2% -> 2% of each run, Pallas kernels for 28% -> 28%
where the time goes in v4:
time: 102 us
  starting transfers between devices  39.1 us (38%)
  Pallas kernels  31.2 us (31%)
  waiting for transfers between devices  25 us (25%)
  other arithmetic  2.93 us (3%)
  local copies, waits for them, and re-layouts  2.74 us (3%)
    pallas_call x5, Pallas kernels, ladder(): pl.pallas_call(functools.partial(ladder_kernel, distances, len(kept), sum...  24.5 us
    ppermute x11, waiting for transfers between devices, z_swap(): return lax.ppermute(block, 'vir', route)  18.1 us
    ppermute x11, starting transfers between devices, z_swap(): return lax.ppermute(block, 'vir', route)  15.4 us
    ppermute x11, starting transfers between devices, x_swap(): return lax.ppermute(block, 'vir', [(i, i ^ 1) for i in range(vir_devices)])  14.6 us
    pallas_call x1, Pallas kernels, keep_sums(): pl.pallas_call(functools.partial(keep_kernel, len(parts)), out_shape=[jax...  6.67 us
    ppermute x4, starting transfers between devices, per_device(): came.append(lax.ppermute(leaving, ('occ', 'vir'), route))  6.04 us
    ppermute x11, waiting for transfers between devices, x_swap(): return lax.ppermute(block, 'vir', [(i, i ^ 1) for i in range(vir_devices)])  4.52 us
    ppermute x1, starting transfers between devices, y_swap(): lax.ppermute(block, 'occ', [(i, (i + across) % occ_devices) for i in rang...  3.03 us
  transfers between devices with their start and end apart: 27, of which 13 were waited for; matrix products, arithmetic and copies ran while one was open for 2% of the time, Pallas kernels for 28%

profile of v4, /device:TPU:0, one launch (start us, length us, event | category | flops | bytes accessed | tf_op | source)
XLA Modules:
  0.0 101.5 jit_solution(12262984930603187230)
XLA Ops:
  1.1 3.0 %collective-permute-start.1 = (bf16[128,1024]{1,0:T(8,128)(2,1)S(1)}, bf16[128,1024]{1,0:T(8,128)(2,1)S(1)}, u32[]{:S(2)}, u32[]{:S(2)}) collective-permute-start(bf16[128,1024]{1,0:T(8,128)(2,1)S(1)} %get-tuple-element.87), channel_id=1, source_target_pairs={{0,16},{8,24},{16,0},{24,8},{1,17},{9,25},{17,1},{25,9},{2,18},{10... | collective-permute-start | bytes 786440 | tf_op jit(solution)/shard_map/ppermute | solution.py:179
  4.1 1.6 %collective-permute-start.8 = (bf16[128,1024]{1,0:T(8,128)(2,1)S(1)}, bf16[128,1024]{1,0:T(8,128)(2,1)S(1)}, u32[]{:S(2)}, u32[]{:S(2)}) collective-permute-start(bf16[128,1024]{1,0:T(8,128)(2,1)S(1)} %get-tuple-element.88.refs_0_), channel_id=1, source_target_pairs={{0,2},{1,3},{2,0},{3,1},{4,6},{5,7},{6,4},{7,5},{8,10},{9,11},{10,... | collective-permute-start | bytes 786440 | tf_op jit(solution)/shard_map/ppermute | solution.py:176
  5.7 1.5 %collective-permute-start = (bf16[128,1024]{1,0:T(8,128)(2,1)S(1)}, bf16[128,1024]{1,0:T(8,128)(2,1)S(1)}, u32[]{:S(2)}, u32[]{:S(2)}) collective-permute-start(bf16[128,1024]{1,0:T(8,128)(2,1)S(1)} %get-tuple-element.88.refs_0_), channel_id=1, source_target_pairs={{0,1},{1,0},{2,3},{3,2},{4,5},{5,4},{6,7},{7,6},{8,9},{9,8},{10,11... | collective-permute-start | bytes 786440 | tf_op jit(solution)/shard_map/ppermute | solution.py:184
  7.2 2.6 %collective-permute-start.4 = (bf16[128,1024]{1,0:T(8,128)(2,1)S(1)}, bf16[128,1024]{1,0:T(8,128)(2,1)S(1)}, u32[]{:S(2)}, u32[]{:S(2)}) collective-permute-start(bf16[128,1024]{1,0:T(8,128)(2,1)S(1)} %get-tuple-element.88.refs_0_), channel_id=1, source_target_pairs={{0,4},{1,5},{2,6},{3,7},{4,0},{5,1},{6,2},{7,3},{8,12},{9,13},{10,... | collective-permute-start | bytes 786440 | tf_op jit(solution)/shard_map/ppermute | solution.py:176
  10.4 1.8 %collective-permute-start.5 = (bf16[128,1024]{1,0:T(8,128)(2,1)S(1)}, bf16[128,1024]{1,0:T(8,128)(2,1)S(1)}, u32[]{:S(2)}, u32[]{:S(2)}) collective-permute-start(bf16[128,1024]{1,0:T(8,128)(2,1)S(1)} %collective-permute-done.1.refs_2_), channel_id=1, source_target_pairs={{0,2},{1,3},{2,0},{3,1},{4,6},{5,7},{6,4},{7,5},{8,10},{9,11},{10,... | collective-permute-start | bytes 786440 | tf_op jit(solution)/shard_map/ppermute | solution.py:176
  12.2 5.4 %collective-permute-done.8.refs_0_ = bf16[128,1024]{1,0:T(8,128)(2,1)S(1)} collective-permute-done((bf16[128,1024]{1,0:T(8,128)(2,1)S(1)}, bf16[128,1024]{1,0:T(8,128)(2,1)S(1)}, u32[]{:S(2)}, u32[]{:S(2)}) %collective-permute-start.8) | collective-permute-done | bytes 262176 | tf_op jit(solution)/shard_map/ppermute | solution.py:176
  17.6 2.8 %collective-permute-start.9 = (bf16[128,1024]{1,0:T(8,128)(2,1)S(1)}, bf16[128,1024]{1,0:T(8,128)(2,1)S(1)}, u32[]{:S(2)}, u32[]{:S(2)}) collective-permute-start(bf16[128,1024]{1,0:T(8,128)(2,1)S(1)} %collective-permute-done.8.refs_0_), channel_id=1, source_target_pairs={{0,1},{1,0},{2,3},{3,2},{4,5},{5,4},{6,7},{7,6},{8,9},{9,8},{10,11... | collective-permute-start | bytes 786440 | tf_op jit(solution)/shard_map/ppermute | solution.py:184
  20.5 1.2 %collective-permute-start.2 = (bf16[128,1024]{1,0:T(8,128)(2,1)S(1)}, bf16[128,1024]{1,0:T(8,128)(2,1)S(1)}, u32[]{:S(2)}, u32[]{:S(2)}) collective-permute-start(bf16[128,1024]{1,0:T(8,128)(2,1)S(1)} %collective-permute-done.1.refs_2_), channel_id=1, source_target_pairs={{0,4},{1,5},{2,6},{3,7},{4,0},{5,1},{6,2},{7,3},{8,12},{9,13},{10,... | collective-permute-start | bytes 786440 | tf_op jit(solution)/shard_map/ppermute | solution.py:176
  21.7 5.0 %shard_map.73 = (f32[256,1024]{1,0:T(8,128)S(1)}, f32[512,512]{1,0:T(8,128)S(1)}, bf16[1024,768]{1,0:T(8,128)(2,1)S(1)}, bf16[1024,768]{1,0:T(8,128)(2,1)S(1)}, bf16[3,1024,1024]{2,1,0:T(8,128)(2,1)S(1)}) custom-call(bf16[3,1024,1024]{2,1,0:T(8,128)(2,1)} %factor_ref.1, bf16[128,1024]{1,0:T(8,128)(2,1)S(1)} %get-tuple-element.88.refs_0_, ...), custom_call_target="tpu_custom_call" | custom-call | flops 805306368 | bytes 11010048 | tf_op jit(solution)/shard_map/pallas_call | solution.py:108
  26.9 1.8 %collective-permute-start.6 = (bf16[128,1024]{1,0:T(8,128)(2,1)S(1)}, bf16[128,1024]{1,0:T(8,128)(2,1)S(1)}, u32[]{:S(2)}, u32[]{:S(2)}) collective-permute-start(bf16[128,1024]{1,0:T(8,128)(2,1)S(1)} %collective-permute-done.4.refs_0_), channel_id=1, source_target_pairs={{0,1},{1,0},{2,3},{3,2},{4,5},{5,4},{6,7},{7,6},{8,9},{9,8},{10,11... | collective-permute-start | bytes 786440 | tf_op jit(solution)/shard_map/ppermute | solution.py:184
  28.7 2.9 %collective-permute-start.12 = (bf16[128,1024]{1,0:T(8,128)(2,1)S(1)}, bf16[128,1024]{1,0:T(8,128)(2,1)S(1)}, u32[]{:S(2)}, u32[]{:S(2)}) collective-permute-start(bf16[128,1024]{1,0:T(8,128)(2,1)S(1)} %collective-permute-done.4.refs_0_), channel_id=1, source_target_pairs={{0,2},{1,3},{2,0},{3,1},{4,6},{5,7},{6,4},{7,5},{8,10},{9,11},{10,... | collective-permute-start | bytes 786440 | tf_op jit(solution)/shard_map/ppermute | solution.py:176
  31.7 5.5 %shard_map.74 = (f32[256,1024]{1,0:T(8,128)S(1)}, f32[512,512]{1,0:T(8,128)S(1)}, bf16[1024,1536]{1,0:T(8,128)(2,1)S(1)}, bf16[1024,1536]{1,0:T(8,128)(2,1)S(1)}) custom-call(bf16[3,1024,1024]{2,1,0:T(8,128)(2,1)S(1)} %get-tuple-element.42.factor_ref, ...), custom_call_target="tpu_custom_call", output_to_operand_aliasing={{0}: (5, {}), {1}: (6, {})} | custom-call | flops 3221225472 | bytes 11534336 | tf_op jit(solution)/shard_map/pallas_call | solution.py:108
  37.3 2.0 %collective-permute-start.14 = (bf16[128,1024]{1,0:T(8,128)(2,1)S(1)}, bf16[128,1024]{1,0:T(8,128)(2,1)S(1)}, u32[]{:S(2)}, u32[]{:S(2)}) collective-permute-start(bf16[128,1024]{1,0:T(8,128)(2,1)S(1)} %collective-permute-done.2.refs_2_), channel_id=1, source_target_pairs={{0,1},{1,0},{2,3},{3,2},{4,5},{5,4},{6,7},{7,6},{8,9},{9,8},{10,11... | collective-permute-start | bytes 786440 | tf_op jit(solution)/shard_map/ppermute | solution.py:184
  39.3 2.0 %collective-permute-start.13 = (bf16[128,1024]{1,0:T(8,128)(2,1)S(1)}, bf16[128,1024]{1,0:T(8,128)(2,1)S(1)}, u32[]{:S(2)}, u32[]{:S(2)}) collective-permute-start(bf16[128,1024]{1,0:T(8,128)(2,1)S(1)} %collective-permute-done.6.refs_1_), channel_id=1, source_target_pairs={{0,2},{1,3},{2,0},{3,1},{4,6},{5,7},{6,4},{7,5},{8,10},{9,11},{10,... | collective-permute-start | bytes 786440 | tf_op jit(solution)/shard_map/ppermute | solution.py:176
  41.3 1.4 %collective-permute-done.7.refs_3_ = bf16[128,1024]{1,0:T(8,128)(2,1)S(1)} collective-permute-done((bf16[128,1024]{1,0:T(8,128)(2,1)S(1)}, bf16[128,1024]{1,0:T(8,128)(2,1)S(1)}, u32[]{:S(2)}, u32[]{:S(2)}) %collective-permute-start.7) | collective-permute-done | bytes 262176 | tf_op jit(solution)/shard_map/ppermute | solution.py:184
  42.7 5.7 %shard_map.75 = (f32[256,1024]{1,0:T(8,128)S(1)}, f32[512,512]{1,0:T(8,128)S(1)}, bf16[1024,1536]{1,0:T(8,128)(2,1)S(1)}, bf16[1024,1536]{1,0:T(8,128)(2,1)S(1)}) custom-call(bf16[3,1024,1024]{2,1,0:T(8,128)(2,1)S(1)} %get-tuple-element.42.factor_ref, ...), custom_call_target="tpu_custom_call", output_to_operand_aliasing={{0}: (5, {}), {1}: (6, {})} | custom-call | flops 3221225472 | bytes 11534336 | tf_op jit(solution)/shard_map/pallas_call | solution.py:108
  48.4 2.1 %collective-permute-start.11 = (bf16[128,1024]{1,0:T(8,128)(2,1)S(1)}, bf16[128,1024]{1,0:T(8,128)(2,1)S(1)}, u32[]{:S(2)}, u32[]{:S(2)}) collective-permute-start(bf16[128,1024]{1,0:T(8,128)(2,1)S(1)} %collective-permute-done.3.refs_0_), channel_id=1, source_target_pairs={{0,1},{1,0},{2,3},{3,2},{4,5},{5,4},{6,7},{7,6},{8,9},{9,8},{10,11... | collective-permute-start | bytes 786440 | tf_op jit(solution)/shard_map/ppermute | solution.py:184
  50.5 5.5 %shard_map.76 = (f32[256,1024]{1,0:T(8,128)S(1)}, f32[512,512]{1,0:T(8,128)S(1)}, bf16[1024,1536]{1,0:T(8,128)(2,1)S(1)}, bf16[1024,1536]{1,0:T(8,128)(2,1)S(1)}) custom-call(bf16[3,1024,1024]{2,1,0:T(8,128)(2,1)S(1)} %get-tuple-element.42.factor_ref, ...), custom_call_target="tpu_custom_call", output_to_operand_aliasing={{0}: (5, {}), {1}: (6, {})} | custom-call | flops 3221225472 | bytes 11534336 | tf_op jit(solution)/shard_map/pallas_call | solution.py:108
  56.1 2.8 %shard_map.77 = (bf16[256,1024]{1,0:T(8,128)(2,1)S(1)}, bf16[512,512]{1,0:T(8,128)(2,1)S(1)}, bf16[1024,768]{1,0:T(8,128)(2,1)S(1)}, bf16[1024,768]{1,0:T(8,128)(2,1)S(1)}) custom-call(bf16[3,1024,1024]{2,1,0:T(8,128)(2,1)S(1)} %get-tuple-element.42.factor_ref, bf16[128,1024]{1,0:T(8,128)(2,1)S(1)} %collective-permute-done.3.refs_0_, ...), custom_call_target="tpu_custom_call" | custom-call | flops 1610612736 | bytes 11010048 | tf_op jit(solution)/shard_map/pallas_call | solution.py:108
  60.2 6.7 %shard_map.78 = (f32[256,1024]{1,0:T(8,128)S(1)}, f32[512,512]{1,0:T(8,128)S(1)}) custom-call(bf16[1024,768]{1,0:T(8,128)(2,1)S(1)} %get-tuple-element.43.refs_0_, bf16[1024,768]{1,0:T(8,128)(2,1)S(1)} %get-tuple-element.66.refs_1_, bf16[1024,1536]{1,0:T(8,128)(2,1)S(1)} %get-tuple-element.55.refs_2_, bf16[1024,1536]{1,0:T(8,128)(2,1)S(1)} %get-tuple-element.67.refs_3_, ...), custom_call_target="tpu_custom_call" | custom-call | flops 6442450944 | bytes 27262976 | tf_op jit(solution)/shard_map/pallas_call | solution.py:145
  67.5 2.3 %collective-permute-done.15 = bf16[256,1024]{1,0:T(8,128)(2,1)S(1)} collective-permute-done((bf16[256,1024]{1,0:T(8,128)(2,1)S(1)}, bf16[256,1024]{1,0:T(8,128)(2,1)S(1)}, u32[]{:S(2)}, u32[]{:S(2)}) %collective-permute-start.15) | collective-permute-done | bytes 524320 | tf_op jit(solution)/shard_map/ppermute | solution.py:184
  70.2 1.6 %collective-permute-done.18 = bf16[512,512]{1,0:T(8,128)(2,1)S(1)} collective-permute-done((bf16[512,512]{1,0:T(8,128)(2,1)S(1)}, bf16[512,512]{1,0:T(8,128)(2,1)S(1)}, u32[]{:S(2)}, u32[]{:S(2)}) %collective-permute-start.18) | collective-permute-done | bytes 524320 | tf_op jit(solution)/shard_map/ppermute | solution.py:176
  71.8 1.3 %collective-permute-start.19 = (bf16[256,512]{1,0:T(8,128)(2,1)S(1)}, bf16[256,512]{1,0:T(8,128)(2,1)S(1)}, u32[]{:S(2)}, u32[]{:S(2)}) collective-permute-start(bf16[256,512]{1,0:T(8,128)(2,1)S(1)} %add_convert_fusion), channel_id=1, source_target_pairs={{0,1},{1,0},{2,3},{3,2},{4,5},{5,4},{6,7},{7,6},{8,9},{9,8},{10,11... | collective-permute-start | bytes 786440 | tf_op jit(solution)/shard_map/ppermute | solution.py:184
  73.1 5.0 %collective-permute-done.16 = bf16[256,512]{1,0:T(8,128)(2,1)S(1)} collective-permute-done((bf16[256,512]{1,0:T(8,128)(2,1)S(1)}, bf16[256,512]{1,0:T(8,128)(2,1)S(1)}, u32[]{:S(2)}, u32[]{:S(2)}) %collective-permute-start.16) | collective-permute-done | bytes 262176 | tf_op jit(solution)/shard_map/ppermute | solution.py:176
  78.5 3.0 %collective-permute-start.20 = (bf16[256,256]{1,0:T(8,128)(2,1)S(1)}, bf16[256,256]{1,0:T(8,128)(2,1)S(1)}, u32[]{:S(2)}, u32[]{:S(2)}) collective-permute-start(bf16[256,256]{1,0:T(8,128)(2,1)S(1)} %select_convert_fusion), channel_id=1, source_target_pairs={{0,4},{1,5},{2,6},{3,7},{4,0},{5,1},{6,2},{7,3},{8,12},{9,13},{10,... | collective-permute-start | bytes 393224 | tf_op jit(solution)/shard_map/ppermute | solution.py:176
  81.5 4.5 %collective-permute-done.17 = bf16[256,256]{1,0:T(8,128)(2,1)S(1)} collective-permute-done((bf16[256,256]{1,0:T(8,128)(2,1)S(1)}, bf16[256,256]{1,0:T(8,128)(2,1)S(1)}, u32[]{:S(2)}, u32[]{:S(2)}) %collective-permute-start.17) | collective-permute-done | bytes 131104 | tf_op jit(solution)/shard_map/ppermute | solution.py:176
  86.1 1.3 %collective-permute-done.20 = bf16[256,256]{1,0:T(8,128)(2,1)S(1)} collective-permute-done((bf16[256,256]{1,0:T(8,128)(2,1)S(1)}, bf16[256,256]{1,0:T(8,128)(2,1)S(1)}, u32[]{:S(2)}, u32[]{:S(2)}) %collective-permute-start.20) | collective-permute-done | bytes 131104 | tf_op jit(solution)/shard_map/ppermute | solution.py:176
  88.1 1.5 %collective-permute-start.22 = (f32[256,128]{1,0:T(8,128)S(1)}, f32[256,128]{1,0:T(8,128)S(1)}, u32[]{:S(2)}, u32[]{:S(2)}) collective-permute-start(f32[256,128]{1,0:T(8,128)S(1)} %slice_select_fusion), channel_id=1, source_target_pairs={{0,1},{1,0},{2,3},{3,2},{4,5},{5,4},{6,7},{7,6},{8,9},{9,8},{10,11... | collective-permute-start | bytes 393224 | tf_op jit(solution)/shard_map/ppermute | solution.py:184
  89.8 1.8 %collective-permute-start.26 = (bf16[128,256]{1,0:T(8,128)(2,1)S(1)}, bf16[128,256]{1,0:T(8,128)(2,1)S(1)}, u32[]{:S(2)}, u32[]{:S(2)}) collective-permute-start(bf16[128,256]{1,0:T(8,128)(2,1)S(1)} %get-tuple-element.90), channel_id=1, source_target_pairs={{0,22},{1,23},{2,20},{3,21},{4,18},{5,19},{6,16},{7,17},{8,30},{9,... | collective-permute-start | bytes 196616 | tf_op jit(solution)/shard_map/ppermute | solution.py:303
  91.6 1.5 %collective-permute-start.23 = (bf16[128,256]{1,0:T(8,128)(2,1)S(1)}, bf16[128,256]{1,0:T(8,128)(2,1)S(1)}, u32[]{:S(2)}, u32[]{:S(2)}) collective-permute-start(bf16[128,256]{1,0:T(8,128)(2,1)S(1)} %get-tuple-element.89), channel_id=1, source_target_pairs={{0,16},{1,17},{2,18},{3,19},{4,20},{5,21},{6,22},{7,23},{8,24},{9,... | collective-permute-start | bytes 196616 | tf_op jit(solution)/shard_map/ppermute | solution.py:303
  94.1 2.7 %collective-permute-start.24 = (bf16[128,256]{1,0:T(8,128)(2,1)S(1)}, bf16[128,256]{1,0:T(8,128)(2,1)S(1)}, u32[]{:S(2)}, u32[]{:S(2)}) collective-permute-start(bf16[128,256]{1,0:T(8,128)(2,1)S(1)} %get-tuple-element.76), channel_id=1, source_target_pairs={{0,18},{1,19},{2,16},{3,17},{4,22},{5,23},{6,20},{7,21},{8,26},{9,... | collective-permute-start | bytes 196616 | tf_op jit(solution)/shard_map/ppermute | solution.py:303
  100.3 1.3 %fusion = f32[2,128,1024]{2,1,0:T(8,128)} fusion(f32[1,128,1024]{2,1,0:T(8,128)S(1)} %get-tuple-element.86, f32[1,128,1024]{2,1,0:T(8,128)S(1)} %get-tuple-element.85, f32[2]{0:T(128)S(1)} %add.91, f32[128,1024]{1,0:T(8,128)S(1)} %broadcast_add_fusion, s32[1024]{0:T(1024)S(1)} %copy-done.2, s32[2,128]{1,0:T(2,128)S(1)} %broadcast_xor_fusion), kind=kLoop, calls=%fused_computation.1 | loop fusion | flops 1572864 | bytes 2626568 | tf_op jit(solution)/shard_map/jit(_where)/select_n | solution.py:338
  (78 shorter events, 9.8 us)
Async XLA Ops:
  0.0 60.0 %copy-start = (s32[8,2]{0,1:T(2,128)S(1)}, s32[8,2]{0,1:T(2,128)}, u32[]{:S(2)}) copy-start(s32[8,2]{0,1:T(2,128)} %param.13) | copy-start | bytes 196
  1.1 9.3 %collective-permute-start.1 = (bf16[128,1024]{1,0:T(8,128)(2,1)S(1)}, bf16[128,1024]{1,0:T(8,128)(2,1)S(1)}, u32[]{:S(2)}, u32[]{:S(2)}) collective-permute-start(bf16[128,1024]{1,0:T(8,128)(2,1)S(1)} %get-tuple-element.87), channel_id=1, source_target_pairs={{0,16},{8,24},{16,0},{24,8},{1,17},{9,25},{17,1},{25,9},{2,18},{10... | collective-permute-start | bytes 786440 | tf_op jit(solution)/shard_map/ppermute | solution.py:179
  4.1 13.5 %collective-permute-start.8 = (bf16[128,1024]{1,0:T(8,128)(2,1)S(1)}, bf16[128,1024]{1,0:T(8,128)(2,1)S(1)}, u32[]{:S(2)}, u32[]{:S(2)}) collective-permute-start(bf16[128,1024]{1,0:T(8,128)(2,1)S(1)} %get-tuple-element.88.refs_0_), channel_id=1, source_target_pairs={{0,2},{1,3},{2,0},{3,1},{4,6},{5,7},{6,4},{7,5},{8,10},{9,11},{10,... | collective-permute-start | bytes 786440 | tf_op jit(solution)/shard_map/ppermute | solution.py:176
  5.7 14.8 %collective-permute-start = (bf16[128,1024]{1,0:T(8,128)(2,1)S(1)}, bf16[128,1024]{1,0:T(8,128)(2,1)S(1)}, u32[]{:S(2)}, u32[]{:S(2)}) collective-permute-start(bf16[128,1024]{1,0:T(8,128)(2,1)S(1)} %get-tuple-element.88.refs_0_), channel_id=1, source_target_pairs={{0,1},{1,0},{2,3},{3,2},{4,5},{5,4},{6,7},{7,6},{8,9},{9,8},{10,11... | collective-permute-start | bytes 786440 | tf_op jit(solution)/shard_map/ppermute | solution.py:184
  7.2 19.5 %collective-permute-start.4 = (bf16[128,1024]{1,0:T(8,128)(2,1)S(1)}, bf16[128,1024]{1,0:T(8,128)(2,1)S(1)}, u32[]{:S(2)}, u32[]{:S(2)}) collective-permute-start(bf16[128,1024]{1,0:T(8,128)(2,1)S(1)} %get-tuple-element.88.refs_0_), channel_id=1, source_target_pairs={{0,4},{1,5},{2,6},{3,7},{4,0},{5,1},{6,2},{7,3},{8,12},{9,13},{10,... | collective-permute-start | bytes 786440 | tf_op jit(solution)/shard_map/ppermute | solution.py:176
  10.4 16.5 %collective-permute-start.5 = (bf16[128,1024]{1,0:T(8,128)(2,1)S(1)}, bf16[128,1024]{1,0:T(8,128)(2,1)S(1)}, u32[]{:S(2)}, u32[]{:S(2)}) collective-permute-start(bf16[128,1024]{1,0:T(8,128)(2,1)S(1)} %collective-permute-done.1.refs_2_), channel_id=1, source_target_pairs={{0,2},{1,3},{2,0},{3,1},{4,6},{5,7},{6,4},{7,5},{8,10},{9,11},{10,... | collective-permute-start | bytes 786440 | tf_op jit(solution)/shard_map/ppermute | solution.py:176
  17.6 14.0 %collective-permute-start.9 = (bf16[128,1024]{1,0:T(8,128)(2,1)S(1)}, bf16[128,1024]{1,0:T(8,128)(2,1)S(1)}, u32[]{:S(2)}, u32[]{:S(2)}) collective-permute-start(bf16[128,1024]{1,0:T(8,128)(2,1)S(1)} %collective-permute-done.8.refs_0_), channel_id=1, source_target_pairs={{0,1},{1,0},{2,3},{3,2},{4,5},{5,4},{6,7},{7,6},{8,9},{9,8},{10,11... | collective-permute-start | bytes 786440 | tf_op jit(solution)/shard_map/ppermute | solution.py:184
  20.5 11.3 %collective-permute-start.10 = (bf16[128,1024]{1,0:T(8,128)(2,1)S(1)}, bf16[128,1024]{1,0:T(8,128)(2,1)S(1)}, u32[]{:S(2)}, u32[]{:S(2)}) collective-permute-start(bf16[128,1024]{1,0:T(8,128)(2,1)S(1)} %collective-permute-done.1.refs_2_), channel_id=1, source_target_pairs={{0,1},{1,0},{2,3},{3,2},{4,5},{5,4},{6,7},{7,6},{8,9},{9,8},{10,11... | collective-permute-start | bytes 786440 | tf_op jit(solution)/shard_map/ppermute | solution.py:184
  20.5 16.8 %collective-permute-start.2 = (bf16[128,1024]{1,0:T(8,128)(2,1)S(1)}, bf16[128,1024]{1,0:T(8,128)(2,1)S(1)}, u32[]{:S(2)}, u32[]{:S(2)}) collective-permute-start(bf16[128,1024]{1,0:T(8,128)(2,1)S(1)} %collective-permute-done.1.refs_2_), channel_id=1, source_target_pairs={{0,4},{1,5},{2,6},{3,7},{4,0},{5,1},{6,2},{7,3},{8,12},{9,13},{10,... | collective-permute-start | bytes 786440 | tf_op jit(solution)/shard_map/ppermute | solution.py:176
  26.9 12.4 %collective-permute-start.6 = (bf16[128,1024]{1,0:T(8,128)(2,1)S(1)}, bf16[128,1024]{1,0:T(8,128)(2,1)S(1)}, u32[]{:S(2)}, u32[]{:S(2)}) collective-permute-start(bf16[128,1024]{1,0:T(8,128)(2,1)S(1)} %collective-permute-done.4.refs_0_), channel_id=1, source_target_pairs={{0,1},{1,0},{2,3},{3,2},{4,5},{5,4},{6,7},{7,6},{8,9},{9,8},{10,11... | collective-permute-start | bytes 786440 | tf_op jit(solution)/shard_map/ppermute | solution.py:184
  28.7 21.8 %collective-permute-start.12 = (bf16[128,1024]{1,0:T(8,128)(2,1)S(1)}, bf16[128,1024]{1,0:T(8,128)(2,1)S(1)}, u32[]{:S(2)}, u32[]{:S(2)}) collective-permute-start(bf16[128,1024]{1,0:T(8,128)(2,1)S(1)} %collective-permute-done.4.refs_0_), channel_id=1, source_target_pairs={{0,2},{1,3},{2,0},{3,1},{4,6},{5,7},{6,4},{7,5},{8,10},{9,11},{10,... | collective-permute-start | bytes 786440 | tf_op jit(solution)/shard_map/ppermute | solution.py:176
  31.6 11.1 %collective-permute-start.7 = (bf16[128,1024]{1,0:T(8,128)(2,1)S(1)}, bf16[128,1024]{1,0:T(8,128)(2,1)S(1)}, u32[]{:S(2)}, u32[]{:S(2)}) collective-permute-start(bf16[128,1024]{1,0:T(8,128)(2,1)S(1)} %collective-permute-done.5.refs_2_), channel_id=1, source_target_pairs={{0,1},{1,0},{2,3},{3,2},{4,5},{5,4},{6,7},{7,6},{8,9},{9,8},{10,11... | collective-permute-start | bytes 786440 | tf_op jit(solution)/shard_map/ppermute | solution.py:184
  37.3 13.2 %collective-permute-start.14 = (bf16[128,1024]{1,0:T(8,128)(2,1)S(1)}, bf16[128,1024]{1,0:T(8,128)(2,1)S(1)}, u32[]{:S(2)}, u32[]{:S(2)}) collective-permute-start(bf16[128,1024]{1,0:T(8,128)(2,1)S(1)} %collective-permute-done.2.refs_2_), channel_id=1, source_target_pairs={{0,1},{1,0},{2,3},{3,2},{4,5},{5,4},{6,7},{7,6},{8,9},{9,8},{10,11... | collective-permute-start | bytes 786440 | tf_op jit(solution)/shard_map/ppermute | solution.py:184
  39.3 9.1 %collective-permute-start.3 = (bf16[128,1024]{1,0:T(8,128)(2,1)S(1)}, bf16[128,1024]{1,0:T(8,128)(2,1)S(1)}, u32[]{:S(2)}, u32[]{:S(2)}) collective-permute-start(bf16[128,1024]{1,0:T(8,128)(2,1)S(1)} %collective-permute-done.2.refs_2_), channel_id=1, source_target_pairs={{0,2},{1,3},{2,0},{3,1},{4,6},{5,7},{6,4},{7,5},{8,10},{9,11},{10,... | collective-permute-start | bytes 786440 | tf_op jit(solution)/shard_map/ppermute | solution.py:176
  39.3 11.2 %collective-permute-start.13 = (bf16[128,1024]{1,0:T(8,128)(2,1)S(1)}, bf16[128,1024]{1,0:T(8,128)(2,1)S(1)}, u32[]{:S(2)}, u32[]{:S(2)}) collective-permute-start(bf16[128,1024]{1,0:T(8,128)(2,1)S(1)} %collective-permute-done.6.refs_1_), channel_id=1, source_target_pairs={{0,2},{1,3},{2,0},{3,1},{4,6},{5,7},{6,4},{7,5},{8,10},{9,11},{10,... | collective-permute-start | bytes 786440 | tf_op jit(solution)/shard_map/ppermute | solution.py:176
  48.4 7.6 %collective-permute-start.11 = (bf16[128,1024]{1,0:T(8,128)(2,1)S(1)}, bf16[128,1024]{1,0:T(8,128)(2,1)S(1)}, u32[]{:S(2)}, u32[]{:S(2)}) collective-permute-start(bf16[128,1024]{1,0:T(8,128)(2,1)S(1)} %collective-permute-done.3.refs_0_), channel_id=1, source_target_pairs={{0,1},{1,0},{2,3},{3,2},{4,5},{5,4},{6,7},{7,6},{8,9},{9,8},{10,11... | collective-permute-start | bytes 786440 | tf_op jit(solution)/shard_map/ppermute | solution.py:184
  56.1 4.0 %copy-start.1 = (f32[1024]{0:T(1024)S(1)}, f32[1024]{0:T(1024)}, u32[]{:S(2)}) copy-start(f32[1024]{0:T(1024)} %param.10) | copy-start | bytes 12292
  56.1 4.1 %copy-start.2 = (s32[1024]{0:T(1024)S(1)}, s32[1024]{0:T(1024)}, u32[]{:S(2)}) copy-start(s32[1024]{0:T(1024)} %param.12) | copy-start | bytes 12292
  58.9 10.9 %collective-permute-start.15 = (bf16[256,1024]{1,0:T(8,128)(2,1)S(1)}, bf16[256,1024]{1,0:T(8,128)(2,1)S(1)}, u32[]{:S(2)}, u32[]{:S(2)}) collective-permute-start(bf16[256,1024]{1,0:T(8,128)(2,1)S(1)} %get-tuple-element.73), channel_id=1, source_target_pairs={{0,1},{1,0},{2,3},{3,2},{4,5},{5,4},{6,7},{7,6},{8,9},{9,8},{10,11... | collective-permute-start | bytes 1572872 | tf_op jit(solution)/shard_map/ppermute | solution.py:184
  59.7 12.0 %collective-permute-start.18 = (bf16[512,512]{1,0:T(8,128)(2,1)S(1)}, bf16[512,512]{1,0:T(8,128)(2,1)S(1)}, u32[]{:S(2)}, u32[]{:S(2)}) collective-permute-start(bf16[512,512]{1,0:T(8,128)(2,1)S(1)} %get-tuple-element.75), channel_id=1, source_target_pairs={{0,2},{1,3},{2,0},{3,1},{4,6},{5,7},{6,4},{7,5},{8,10},{9,11},{10,... | collective-permute-start | bytes 1572872 | tf_op jit(solution)/shard_map/ppermute | solution.py:176
  60.2 6.7 %copy-start.3 = (s32[100]{0:T(128)S(1)}, s32[100]{0:T(128)}, u32[]{:S(2)}) copy-start(s32[100]{0:T(128)} %param.11) | copy-start | bytes 1204
  60.2 9.7 %copy-start.4 = (f32[100]{0:T(128)S(1)}, f32[100]{0:T(128)}, u32[]{:S(2)}) copy-start(f32[100]{0:T(128)} %param.9) | copy-start | bytes 1204
  69.8 8.3 %collective-permute-start.16 = (bf16[256,512]{1,0:T(8,128)(2,1)S(1)}, bf16[256,512]{1,0:T(8,128)(2,1)S(1)}, u32[]{:S(2)}, u32[]{:S(2)}) collective-permute-start(bf16[256,512]{1,0:T(8,128)(2,1)S(1)} %add_convert_fusion.1), channel_id=1, source_target_pairs={{0,2},{1,3},{2,0},{3,1},{4,6},{5,7},{6,4},{7,5},{8,10},{9,11},{10,... | collective-permute-start | bytes 786440 | tf_op jit(solution)/shard_map/ppermute | solution.py:176
  71.8 6.6 %collective-permute-start.19 = (bf16[256,512]{1,0:T(8,128)(2,1)S(1)}, bf16[256,512]{1,0:T(8,128)(2,1)S(1)}, u32[]{:S(2)}, u32[]{:S(2)}) collective-permute-start(bf16[256,512]{1,0:T(8,128)(2,1)S(1)} %add_convert_fusion), channel_id=1, source_target_pairs={{0,1},{1,0},{2,3},{3,2},{4,5},{5,4},{6,7},{7,6},{8,9},{9,8},{10,11... | collective-permute-start | bytes 786440 | tf_op jit(solution)/shard_map/ppermute | solution.py:184
  78.3 7.8 %collective-permute-start.17 = (bf16[256,256]{1,0:T(8,128)(2,1)S(1)}, bf16[256,256]{1,0:T(8,128)(2,1)S(1)}, u32[]{:S(2)}, u32[]{:S(2)}) collective-permute-start(bf16[256,256]{1,0:T(8,128)(2,1)S(1)} %select_convert_fusion.1), channel_id=1, source_target_pairs={{0,4},{1,5},{2,6},{3,7},{4,0},{5,1},{6,2},{7,3},{8,12},{9,13},{10,... | collective-permute-start | bytes 393224 | tf_op jit(solution)/shard_map/ppermute | solution.py:176
  78.5 8.9 %collective-permute-start.20 = (bf16[256,256]{1,0:T(8,128)(2,1)S(1)}, bf16[256,256]{1,0:T(8,128)(2,1)S(1)}, u32[]{:S(2)}, u32[]{:S(2)}) collective-permute-start(bf16[256,256]{1,0:T(8,128)(2,1)S(1)} %select_convert_fusion), channel_id=1, source_target_pairs={{0,4},{1,5},{2,6},{3,7},{4,0},{5,1},{6,2},{7,3},{8,12},{9,13},{10,... | collective-permute-start | bytes 393224 | tf_op jit(solution)/shard_map/ppermute | solution.py:176
  87.6 5.6 %collective-permute-start.21 = (f32[256,128]{1,0:T(8,128)S(1)}, f32[256,128]{1,0:T(8,128)S(1)}, u32[]{:S(2)}, u32[]{:S(2)}) collective-permute-start(f32[256,128]{1,0:T(8,128)S(1)} %slice_select_fusion.1), channel_id=1, source_target_pairs={{0,1},{1,0},{2,3},{3,2},{4,5},{5,4},{6,7},{7,6},{8,9},{9,8},{10,11... | collective-permute-start | bytes 393224 | tf_op jit(solution)/shard_map/ppermute | solution.py:184
  88.1 5.9 %collective-permute-start.22 = (f32[256,128]{1,0:T(8,128)S(1)}, f32[256,128]{1,0:T(8,128)S(1)}, u32[]{:S(2)}, u32[]{:S(2)}) collective-permute-start(f32[256,128]{1,0:T(8,128)S(1)} %slice_select_fusion), channel_id=1, source_target_pairs={{0,1},{1,0},{2,3},{3,2},{4,5},{5,4},{6,7},{7,6},{8,9},{9,8},{10,11... | collective-permute-start | bytes 393224 | tf_op jit(solution)/shard_map/ppermute | solution.py:184
  89.8 7.8 %collective-permute-start.26 = (bf16[128,256]{1,0:T(8,128)(2,1)S(1)}, bf16[128,256]{1,0:T(8,128)(2,1)S(1)}, u32[]{:S(2)}, u32[]{:S(2)}) collective-permute-start(bf16[128,256]{1,0:T(8,128)(2,1)S(1)} %get-tuple-element.90), channel_id=1, source_target_pairs={{0,22},{1,23},{2,20},{3,21},{4,18},{5,19},{6,16},{7,17},{8,30},{9,... | collective-permute-start | bytes 196616 | tf_op jit(solution)/shard_map/ppermute | solution.py:303
  91.6 6.7 %collective-permute-start.25 = (bf16[128,256]{1,0:T(8,128)(2,1)S(1)}, bf16[128,256]{1,0:T(8,128)(2,1)S(1)}, u32[]{:S(2)}, u32[]{:S(2)}) collective-permute-start(bf16[128,256]{1,0:T(8,128)(2,1)S(1)} %get-tuple-element.91), channel_id=1, source_target_pairs={{0,20},{1,21},{2,22},{3,23},{4,16},{5,17},{6,18},{7,19},{8,28},{9,... | collective-permute-start | bytes 196616 | tf_op jit(solution)/shard_map/ppermute | solution.py:303
  91.6 6.9 %collective-permute-start.23 = (bf16[128,256]{1,0:T(8,128)(2,1)S(1)}, bf16[128,256]{1,0:T(8,128)(2,1)S(1)}, u32[]{:S(2)}, u32[]{:S(2)}) collective-permute-start(bf16[128,256]{1,0:T(8,128)(2,1)S(1)} %get-tuple-element.89), channel_id=1, source_target_pairs={{0,16},{1,17},{2,18},{3,19},{4,20},{5,21},{6,22},{7,23},{8,24},{9,... | collective-permute-start | bytes 196616 | tf_op jit(solution)/shard_map/ppermute | solution.py:303
  94.1 5.2 %collective-permute-start.24 = (bf16[128,256]{1,0:T(8,128)(2,1)S(1)}, bf16[128,256]{1,0:T(8,128)(2,1)S(1)}, u32[]{:S(2)}, u32[]{:S(2)}) collective-permute-start(bf16[128,256]{1,0:T(8,128)(2,1)S(1)} %get-tuple-element.76), channel_id=1, source_target_pairs={{0,18},{1,19},{2,16},{3,17},{4,22},{5,23},{6,20},{7,21},{8,26},{9,... | collective-permute-start | bytes 196616 | tf_op jit(solution)/shard_map/ppermute | solution.py:303

commit v5 on v4

--- a/solution.py
+++ b/solution.py
@@ -114,7 +114,7 @@
         input_output_aliases=aliases,
         compiler_params=pltpu.CompilerParams(vmem_limit_bytes=VMEM_MIB * 1024 * 1024),
         cost_estimate=pl.CostEstimate(
-            flops=(1 if loads else 2) * factor_count * width * size * size,
+            flops=(0 if loads else 3) * factor_count * width * size * size,
             bytes_accessed=2 * factor_count * size * size + 4 * size * size + 2 * width * size,
             transcendentals=0,
         ),
@@ -283,13 +283,11 @@
         packed = own_rows.astype(jnp.bfloat16).reshape(row_count, vir_devices, row_count)
         packed = jnp.transpose(packed, (1, 2, 0))
     if inner == 2:
-        def flipped(blocks):
-            blocks = blocks.reshape(2, 2, *blocks.shape[1:])
-            blocks = jnp.where(z_high == 1, jnp.flip(blocks, 0), blocks)
-            blocks = jnp.where(z_low == 1, jnp.flip(blocks, 1), blocks)
-            return blocks.reshape(4, *blocks.shape[2:])
-
-        turned = flipped(turned)
+        def picked(blocks):
+            blocks = [jnp.where(z_low == 1, blocks[k ^ 1], blocks[k]) for k in range(4)]
+            return [jnp.where(z_high == 1, blocks[k ^ 2], blocks[k]) for k in range(4)]
+
+        turned = picked([turned[k] for k in range(4)])
         came = []
         for step in range(4):
             route = [
@@ -301,10 +299,10 @@
             if step == 1:
                 leaving = after((leaving, other_half))[0]
             came.append(lax.ppermute(leaving, ("occ", "vir"), route))
-        partner = flipped(jnp.stack(came))
+        partner = jnp.concatenate(picked(came), axis=1).astype(jnp.float32)
     else:
         partner = y_swap(lax.all_to_all(packed, "vir", 0, 0))
-    partner = jnp.transpose(partner, (1, 0, 2)).reshape(row_count, size).astype(jnp.float32)
+        partner = jnp.transpose(partner, (1, 0, 2)).reshape(row_count, size).astype(jnp.float32)
 
     first = jnp.where(side == 0, own_rows, partner)
     second = jnp.where(side == 0, partner, own_rows)

time: 102 us -> 101 us (level)
  no operation moved by 1% of the time
where the time goes in v5:
time: 101 us
  starting transfers between devices  39 us (39%)
  Pallas kernels  31.2 us (31%)
  waiting for transfers between devices  25.2 us (25%)
  other arithmetic  2.68 us (3%)
  local copies, waits for them, and re-layouts  2.11 us (2%)
    pallas_call x5, Pallas kernels, ladder(): pl.pallas_call(functools.partial(ladder_kernel, distances, len(kept), sum...  24.5 us
    ppermute x11, waiting for transfers between devices, z_swap(): return lax.ppermute(block, 'vir', route)  18.1 us
    ppermute x11, starting transfers between devices, z_swap(): return lax.ppermute(block, 'vir', route)  15.4 us
    ppermute x11, starting transfers between devices, x_swap(): return lax.ppermute(block, 'vir', [(i, i ^ 1) for i in range(vir_devices)])  14.6 us
    pallas_call x1, Pallas kernels, keep_sums(): pl.pallas_call(functools.partial(keep_kernel, len(parts)), out_shape=[jax...  6.67 us
    ppermute x4, starting transfers between devices, per_device(): came.append(lax.ppermute(leaving, ('occ', 'vir'), route))  5.92 us
    ppermute x11, waiting for transfers between devices, x_swap(): return lax.ppermute(block, 'vir', [(i, i ^ 1) for i in range(vir_devices)])  4.67 us
    ppermute x1, starting transfers between devices, y_swap(): lax.ppermute(block, 'occ', [(i, (i + across) % occ_devices) for i in rang...  3.03 us
  transfers between devices with their start and end apart: 27, of which 13 were waited for; matrix products, arithmetic and copies ran while one was open for 2% of the time, Pallas kernels for 28%

profile of v5, /device:TPU:0, one launch (start us, length us, event | category | flops | bytes accessed | tf_op | source)
XLA Modules:
  0.0 100.7 jit_solution(9309189642787797411)
XLA Ops:
  1.1 3.0 %collective-permute-start.1 = (bf16[128,1024]{1,0:T(8,128)(2,1)S(1)}, bf16[128,1024]{1,0:T(8,128)(2,1)S(1)}, u32[]{:S(2)}, u32[]{:S(2)}) collective-permute-start(bf16[128,1024]{1,0:T(8,128)(2,1)S(1)} %get-tuple-element.87), channel_id=1, source_target_pairs={{0,16},{8,24},{16,0},{24,8},{1,17},{9,25},{17,1},{25,9},{2,18},{10... | collective-permute-start | bytes 786440 | tf_op jit(solution)/shard_map/ppermute | solution.py:179
  4.1 1.6 %collective-permute-start.8 = (bf16[128,1024]{1,0:T(8,128)(2,1)S(1)}, bf16[128,1024]{1,0:T(8,128)(2,1)S(1)}, u32[]{:S(2)}, u32[]{:S(2)}) collective-permute-start(bf16[128,1024]{1,0:T(8,128)(2,1)S(1)} %get-tuple-element.88.refs_0_), channel_id=1, source_target_pairs={{0,2},{1,3},{2,0},{3,1},{4,6},{5,7},{6,4},{7,5},{8,10},{9,11},{10,... | collective-permute-start | bytes 786440 | tf_op jit(solution)/shard_map/ppermute | solution.py:176
  5.7 1.5 %collective-permute-start = (bf16[128,1024]{1,0:T(8,128)(2,1)S(1)}, bf16[128,1024]{1,0:T(8,128)(2,1)S(1)}, u32[]{:S(2)}, u32[]{:S(2)}) collective-permute-start(bf16[128,1024]{1,0:T(8,128)(2,1)S(1)} %get-tuple-element.88.refs_0_), channel_id=1, source_target_pairs={{0,1},{1,0},{2,3},{3,2},{4,5},{5,4},{6,7},{7,6},{8,9},{9,8},{10,11... | collective-permute-start | bytes 786440 | tf_op jit(solution)/shard_map/ppermute | solution.py:184
  7.2 2.6 %collective-permute-start.4 = (bf16[128,1024]{1,0:T(8,128)(2,1)S(1)}, bf16[128,1024]{1,0:T(8,128)(2,1)S(1)}, u32[]{:S(2)}, u32[]{:S(2)}) collective-permute-start(bf16[128,1024]{1,0:T(8,128)(2,1)S(1)} %get-tuple-element.88.refs_0_), channel_id=1, source_target_pairs={{0,4},{1,5},{2,6},{3,7},{4,0},{5,1},{6,2},{7,3},{8,12},{9,13},{10,... | collective-permute-start | bytes 786440 | tf_op jit(solution)/shard_map/ppermute | solution.py:176
  10.4 1.8 %collective-permute-start.5 = (bf16[128,1024]{1,0:T(8,128)(2,1)S(1)}, bf16[128,1024]{1,0:T(8,128)(2,1)S(1)}, u32[]{:S(2)}, u32[]{:S(2)}) collective-permute-start(bf16[128,1024]{1,0:T(8,128)(2,1)S(1)} %collective-permute-done.1.refs_2_), channel_id=1, source_target_pairs={{0,2},{1,3},{2,0},{3,1},{4,6},{5,7},{6,4},{7,5},{8,10},{9,11},{10,... | collective-permute-start | bytes 786440 | tf_op jit(solution)/shard_map/ppermute | solution.py:176
  12.2 5.4 %collective-permute-done.8.refs_0_ = bf16[128,1024]{1,0:T(8,128)(2,1)S(1)} collective-permute-done((bf16[128,1024]{1,0:T(8,128)(2,1)S(1)}, bf16[128,1024]{1,0:T(8,128)(2,1)S(1)}, u32[]{:S(2)}, u32[]{:S(2)}) %collective-permute-start.8) | collective-permute-done | bytes 262176 | tf_op jit(solution)/shard_map/ppermute | solution.py:176
  17.6 2.8 %collective-permute-start.9 = (bf16[128,1024]{1,0:T(8,128)(2,1)S(1)}, bf16[128,1024]{1,0:T(8,128)(2,1)S(1)}, u32[]{:S(2)}, u32[]{:S(2)}) collective-permute-start(bf16[128,1024]{1,0:T(8,128)(2,1)S(1)} %collective-permute-done.8.refs_0_), channel_id=1, source_target_pairs={{0,1},{1,0},{2,3},{3,2},{4,5},{5,4},{6,7},{7,6},{8,9},{9,8},{10,11... | collective-permute-start | bytes 786440 | tf_op jit(solution)/shard_map/ppermute | solution.py:184
  20.5 1.2 %collective-permute-start.2 = (bf16[128,1024]{1,0:T(8,128)(2,1)S(1)}, bf16[128,1024]{1,0:T(8,128)(2,1)S(1)}, u32[]{:S(2)}, u32[]{:S(2)}) collective-permute-start(bf16[128,1024]{1,0:T(8,128)(2,1)S(1)} %collective-permute-done.1.refs_2_), channel_id=1, source_target_pairs={{0,4},{1,5},{2,6},{3,7},{4,0},{5,1},{6,2},{7,3},{8,12},{9,13},{10,... | collective-permute-start | bytes 786440 | tf_op jit(solution)/shard_map/ppermute | solution.py:176
  21.7 5.0 %shard_map.73 = (f32[256,1024]{1,0:T(8,128)S(1)}, f32[512,512]{1,0:T(8,128)S(1)}, bf16[1024,768]{1,0:T(8,128)(2,1)S(1)}, bf16[1024,768]{1,0:T(8,128)(2,1)S(1)}, bf16[3,1024,1024]{2,1,0:T(8,128)(2,1)S(1)}) custom-call(bf16[3,1024,1024]{2,1,0:T(8,128)(2,1)} %factor_ref.1, bf16[128,1024]{1,0:T(8,128)(2,1)S(1)} %get-tuple-element.88.refs_0_, ...), custom_call_target="tpu_custom_call" | custom-call | bytes 11010048 | tf_op jit(solution)/shard_map/pallas_call | solution.py:108
  26.9 1.8 %collective-permute-start.6 = (bf16[128,1024]{1,0:T(8,128)(2,1)S(1)}, bf16[128,1024]{1,0:T(8,128)(2,1)S(1)}, u32[]{:S(2)}, u32[]{:S(2)}) collective-permute-start(bf16[128,1024]{1,0:T(8,128)(2,1)S(1)} %collective-permute-done.4.refs_0_), channel_id=1, source_target_pairs={{0,1},{1,0},{2,3},{3,2},{4,5},{5,4},{6,7},{7,6},{8,9},{9,8},{10,11... | collective-permute-start | bytes 786440 | tf_op jit(solution)/shard_map/ppermute | solution.py:184
  28.7 2.9 %collective-permute-start.12 = (bf16[128,1024]{1,0:T(8,128)(2,1)S(1)}, bf16[128,1024]{1,0:T(8,128)(2,1)S(1)}, u32[]{:S(2)}, u32[]{:S(2)}) collective-permute-start(bf16[128,1024]{1,0:T(8,128)(2,1)S(1)} %collective-permute-done.4.refs_0_), channel_id=1, source_target_pairs={{0,2},{1,3},{2,0},{3,1},{4,6},{5,7},{6,4},{7,5},{8,10},{9,11},{10,... | collective-permute-start | bytes 786440 | tf_op jit(solution)/shard_map/ppermute | solution.py:176
  31.7 5.5 %shard_map.74 = (f32[256,1024]{1,0:T(8,128)S(1)}, f32[512,512]{1,0:T(8,128)S(1)}, bf16[1024,1536]{1,0:T(8,128)(2,1)S(1)}, bf16[1024,1536]{1,0:T(8,128)(2,1)S(1)}) custom-call(bf16[3,1024,1024]{2,1,0:T(8,128)(2,1)S(1)} %get-tuple-element.42.factor_ref, ...), custom_call_target="tpu_custom_call", output_to_operand_aliasing={{0}: (5, {}), {1}: (6, {})} | custom-call | flops 4831838208 | bytes 11534336 | tf_op jit(solution)/shard_map/pallas_call | solution.py:108
  37.3 2.0 %collective-permute-start.14 = (bf16[128,1024]{1,0:T(8,128)(2,1)S(1)}, bf16[128,1024]{1,0:T(8,128)(2,1)S(1)}, u32[]{:S(2)}, u32[]{:S(2)}) collective-permute-start(bf16[128,1024]{1,0:T(8,128)(2,1)S(1)} %collective-permute-done.2.refs_2_), channel_id=1, source_target_pairs={{0,1},{1,0},{2,3},{3,2},{4,5},{5,4},{6,7},{7,6},{8,9},{9,8},{10,11... | collective-permute-start | bytes 786440 | tf_op jit(solution)/shard_map/ppermute | solution.py:184
  39.3 2.0 %collective-permute-start.13 = (bf16[128,1024]{1,0:T(8,128)(2,1)S(1)}, bf16[128,1024]{1,0:T(8,128)(2,1)S(1)}, u32[]{:S(2)}, u32[]{:S(2)}) collective-permute-start(bf16[128,1024]{1,0:T(8,128)(2,1)S(1)} %collective-permute-done.6.refs_1_), channel_id=1, source_target_pairs={{0,2},{1,3},{2,0},{3,1},{4,6},{5,7},{6,4},{7,5},{8,10},{9,11},{10,... | collective-permute-start | bytes 786440 | tf_op jit(solution)/shard_map/ppermute | solution.py:176
  41.3 1.4 %collective-permute-done.7.refs_3_ = bf16[128,1024]{1,0:T(8,128)(2,1)S(1)} collective-permute-done((bf16[128,1024]{1,0:T(8,128)(2,1)S(1)}, bf16[128,1024]{1,0:T(8,128)(2,1)S(1)}, u32[]{:S(2)}, u32[]{:S(2)}) %collective-permute-start.7) | collective-permute-done | bytes 262176 | tf_op jit(solution)/shard_map/ppermute | solution.py:184
  42.7 5.7 %shard_map.75 = (f32[256,1024]{1,0:T(8,128)S(1)}, f32[512,512]{1,0:T(8,128)S(1)}, bf16[1024,1536]{1,0:T(8,128)(2,1)S(1)}, bf16[1024,1536]{1,0:T(8,128)(2,1)S(1)}) custom-call(bf16[3,1024,1024]{2,1,0:T(8,128)(2,1)S(1)} %get-tuple-element.42.factor_ref, ...), custom_call_target="tpu_custom_call", output_to_operand_aliasing={{0}: (5, {}), {1}: (6, {})} | custom-call | flops 4831838208 | bytes 11534336 | tf_op jit(solution)/shard_map/pallas_call | solution.py:108
  48.4 2.1 %collective-permute-start.11 = (bf16[128,1024]{1,0:T(8,128)(2,1)S(1)}, bf16[128,1024]{1,0:T(8,128)(2,1)S(1)}, u32[]{:S(2)}, u32[]{:S(2)}) collective-permute-start(bf16[128,1024]{1,0:T(8,128)(2,1)S(1)} %collective-permute-done.3.refs_0_), channel_id=1, source_target_pairs={{0,1},{1,0},{2,3},{3,2},{4,5},{5,4},{6,7},{7,6},{8,9},{9,8},{10,11... | collective-permute-start | bytes 786440 | tf_op jit(solution)/shard_map/ppermute | solution.py:184
  50.5 5.5 %shard_map.76 = (f32[256,1024]{1,0:T(8,128)S(1)}, f32[512,512]{1,0:T(8,128)S(1)}, bf16[1024,1536]{1,0:T(8,128)(2,1)S(1)}, bf16[1024,1536]{1,0:T(8,128)(2,1)S(1)}) custom-call(bf16[3,1024,1024]{2,1,0:T(8,128)(2,1)S(1)} %get-tuple-element.42.factor_ref, ...), custom_call_target="tpu_custom_call", output_to_operand_aliasing={{0}: (5, {}), {1}: (6, {})} | custom-call | flops 4831838208 | bytes 11534336 | tf_op jit(solution)/shard_map/pallas_call | solution.py:108
  56.1 2.8 %shard_map.77 = (bf16[256,1024]{1,0:T(8,128)(2,1)S(1)}, bf16[512,512]{1,0:T(8,128)(2,1)S(1)}, bf16[1024,768]{1,0:T(8,128)(2,1)S(1)}, bf16[1024,768]{1,0:T(8,128)(2,1)S(1)}) custom-call(bf16[3,1024,1024]{2,1,0:T(8,128)(2,1)S(1)} %get-tuple-element.42.factor_ref, bf16[128,1024]{1,0:T(8,128)(2,1)S(1)} %collective-permute-done.3.refs_0_, ...), custom_call_target="tpu_custom_call" | custom-call | flops 2415919104 | bytes 11010048 | tf_op jit(solution)/shard_map/pallas_call | solution.py:108
  60.2 6.7 %shard_map.78 = (f32[256,1024]{1,0:T(8,128)S(1)}, f32[512,512]{1,0:T(8,128)S(1)}) custom-call(bf16[1024,768]{1,0:T(8,128)(2,1)S(1)} %get-tuple-element.43.refs_0_, bf16[1024,768]{1,0:T(8,128)(2,1)S(1)} %get-tuple-element.66.refs_1_, bf16[1024,1536]{1,0:T(8,128)(2,1)S(1)} %get-tuple-element.55.refs_2_, bf16[1024,1536]{1,0:T(8,128)(2,1)S(1)} %get-tuple-element.67.refs_3_, ...), custom_call_target="tpu_custom_call" | custom-call | flops 6442450944 | bytes 27262976 | tf_op jit(solution)/shard_map/pallas_call | solution.py:145
  67.5 2.3 %collective-permute-done.15 = bf16[256,1024]{1,0:T(8,128)(2,1)S(1)} collective-permute-done((bf16[256,1024]{1,0:T(8,128)(2,1)S(1)}, bf16[256,1024]{1,0:T(8,128)(2,1)S(1)}, u32[]{:S(2)}, u32[]{:S(2)}) %collective-permute-start.15) | collective-permute-done | bytes 524320 | tf_op jit(solution)/shard_map/ppermute | solution.py:184
  70.2 1.5 %collective-permute-done.18 = bf16[512,512]{1,0:T(8,128)(2,1)S(1)} collective-permute-done((bf16[512,512]{1,0:T(8,128)(2,1)S(1)}, bf16[512,512]{1,0:T(8,128)(2,1)S(1)}, u32[]{:S(2)}, u32[]{:S(2)}) %collective-permute-start.18) | collective-permute-done | bytes 524320 | tf_op jit(solution)/shard_map/ppermute | solution.py:176
  71.8 1.3 %collective-permute-start.19 = (bf16[256,512]{1,0:T(8,128)(2,1)S(1)}, bf16[256,512]{1,0:T(8,128)(2,1)S(1)}, u32[]{:S(2)}, u32[]{:S(2)}) collective-permute-start(bf16[256,512]{1,0:T(8,128)(2,1)S(1)} %add_convert_fusion), channel_id=1, source_target_pairs={{0,1},{1,0},{2,3},{3,2},{4,5},{5,4},{6,7},{7,6},{8,9},{9,8},{10,11... | collective-permute-start | bytes 786440 | tf_op jit(solution)/shard_map/ppermute | solution.py:184
  73.1 5.0 %collective-permute-done.16 = bf16[256,512]{1,0:T(8,128)(2,1)S(1)} collective-permute-done((bf16[256,512]{1,0:T(8,128)(2,1)S(1)}, bf16[256,512]{1,0:T(8,128)(2,1)S(1)}, u32[]{:S(2)}, u32[]{:S(2)}) %collective-permute-start.16) | collective-permute-done | bytes 262176 | tf_op jit(solution)/shard_map/ppermute | solution.py:176
  78.5 3.0 %collective-permute-start.20 = (bf16[256,256]{1,0:T(8,128)(2,1)S(1)}, bf16[256,256]{1,0:T(8,128)(2,1)S(1)}, u32[]{:S(2)}, u32[]{:S(2)}) collective-permute-start(bf16[256,256]{1,0:T(8,128)(2,1)S(1)} %select_convert_fusion), channel_id=1, source_target_pairs={{0,4},{1,5},{2,6},{3,7},{4,0},{5,1},{6,2},{7,3},{8,12},{9,13},{10,... | collective-permute-start | bytes 393224 | tf_op jit(solution)/shard_map/ppermute | solution.py:176
  81.5 4.6 %collective-permute-done.17 = bf16[256,256]{1,0:T(8,128)(2,1)S(1)} collective-permute-done((bf16[256,256]{1,0:T(8,128)(2,1)S(1)}, bf16[256,256]{1,0:T(8,128)(2,1)S(1)}, u32[]{:S(2)}, u32[]{:S(2)}) %collective-permute-start.17) | collective-permute-done | bytes 131104 | tf_op jit(solution)/shard_map/ppermute | solution.py:176
  86.1 1.3 %collective-permute-done.20 = bf16[256,256]{1,0:T(8,128)(2,1)S(1)} collective-permute-done((bf16[256,256]{1,0:T(8,128)(2,1)S(1)}, bf16[256,256]{1,0:T(8,128)(2,1)S(1)}, u32[]{:S(2)}, u32[]{:S(2)}) %collective-permute-start.20) | collective-permute-done | bytes 131104 | tf_op jit(solution)/shard_map/ppermute | solution.py:176
  88.1 1.6 %collective-permute-start.22 = (f32[256,128]{1,0:T(8,128)S(1)}, f32[256,128]{1,0:T(8,128)S(1)}, u32[]{:S(2)}, u32[]{:S(2)}) collective-permute-start(f32[256,128]{1,0:T(8,128)S(1)} %slice_select_fusion), channel_id=1, source_target_pairs={{0,1},{1,0},{2,3},{3,2},{4,5},{5,4},{6,7},{7,6},{8,9},{9,8},{10,11... | collective-permute-start | bytes 393224 | tf_op jit(solution)/shard_map/ppermute | solution.py:184
  89.7 1.8 %collective-permute-start.23 = (bf16[128,256]{1,0:T(8,128)(2,1)S(1)}, bf16[128,256]{1,0:T(8,128)(2,1)S(1)}, u32[]{:S(2)}, u32[]{:S(2)}) collective-permute-start(bf16[128,256]{1,0:T(8,128)(2,1)S(1)} %get-tuple-element.96), channel_id=1, source_target_pairs={{0,22},{1,23},{2,20},{3,21},{4,18},{5,19},{6,16},{7,17},{8,30},{9,... | collective-permute-start | bytes 196616 | tf_op jit(solution)/shard_map/ppermute | solution.py:301
  91.5 1.5 %collective-permute-start.26 = (bf16[128,256]{1,0:T(8,128)(2,1)S(1)}, bf16[128,256]{1,0:T(8,128)(2,1)S(1)}, u32[]{:S(2)}, u32[]{:S(2)}) collective-permute-start(bf16[128,256]{1,0:T(8,128)(2,1)S(1)} %get-tuple-element.95), channel_id=1, source_target_pairs={{0,16},{1,17},{2,18},{3,19},{4,20},{5,21},{6,22},{7,23},{8,24},{9,... | collective-permute-start | bytes 196616 | tf_op jit(solution)/shard_map/ppermute | solution.py:301
  94.1 2.6 %collective-permute-start.25 = (bf16[128,256]{1,0:T(8,128)(2,1)S(1)}, bf16[128,256]{1,0:T(8,128)(2,1)S(1)}, u32[]{:S(2)}, u32[]{:S(2)}) collective-permute-start(bf16[128,256]{1,0:T(8,128)(2,1)S(1)} %get-tuple-element.76), channel_id=1, source_target_pairs={{0,18},{1,19},{2,16},{3,17},{4,22},{5,23},{6,20},{7,21},{8,26},{9,... | collective-permute-start | bytes 196616 | tf_op jit(solution)/shard_map/ppermute | solution.py:301
  99.5 1.3 %fusion = f32[2,128,1024]{2,1,0:T(8,128)} fusion(f32[1,128,1024]{2,1,0:T(8,128)S(1)} %get-tuple-element.86, f32[1,128,1024]{2,1,0:T(8,128)S(1)} %get-tuple-element.85, f32[2]{0:T(128)S(1)} %add.91, f32[128,1024]{1,0:T(8,128)S(1)} %broadcast_add_fusion, s32[1024]{0:T(1024)S(1)} %copy-done.2, s32[2,128]{1,0:T(2,128)S(1)} %broadcast_xor_fusion), kind=kLoop, calls=%fused_computation.1 | loop fusion | flops 1572864 | bytes 2626568 | tf_op jit(solution)/shard_map/jit(_where)/select_n | solution.py:336
  (71 shorter events, 9.1 us)
Async XLA Ops:
  0.0 60.0 %copy-start = (s32[8,2]{0,1:T(2,128)S(1)}, s32[8,2]{0,1:T(2,128)}, u32[]{:S(2)}) copy-start(s32[8,2]{0,1:T(2,128)} %param.13) | copy-start | bytes 196
  1.1 9.3 %collective-permute-start.1 = (bf16[128,1024]{1,0:T(8,128)(2,1)S(1)}, bf16[128,1024]{1,0:T(8,128)(2,1)S(1)}, u32[]{:S(2)}, u32[]{:S(2)}) collective-permute-start(bf16[128,1024]{1,0:T(8,128)(2,1)S(1)} %get-tuple-element.87), channel_id=1, source_target_pairs={{0,16},{8,24},{16,0},{24,8},{1,17},{9,25},{17,1},{25,9},{2,18},{10... | collective-permute-start | bytes 786440 | tf_op jit(solution)/shard_map/ppermute | solution.py:179
  4.1 13.5 %collective-permute-start.8 = (bf16[128,1024]{1,0:T(8,128)(2,1)S(1)}, bf16[128,1024]{1,0:T(8,128)(2,1)S(1)}, u32[]{:S(2)}, u32[]{:S(2)}) collective-permute-start(bf16[128,1024]{1,0:T(8,128)(2,1)S(1)} %get-tuple-element.88.refs_0_), channel_id=1, source_target_pairs={{0,2},{1,3},{2,0},{3,1},{4,6},{5,7},{6,4},{7,5},{8,10},{9,11},{10,... | collective-permute-start | bytes 786440 | tf_op jit(solution)/shard_map/ppermute | solution.py:176
  5.7 14.8 %collective-permute-start = (bf16[128,1024]{1,0:T(8,128)(2,1)S(1)}, bf16[128,1024]{1,0:T(8,128)(2,1)S(1)}, u32[]{:S(2)}, u32[]{:S(2)}) collective-permute-start(bf16[128,1024]{1,0:T(8,128)(2,1)S(1)} %get-tuple-element.88.refs_0_), channel_id=1, source_target_pairs={{0,1},{1,0},{2,3},{3,2},{4,5},{5,4},{6,7},{7,6},{8,9},{9,8},{10,11... | collective-permute-start | bytes 786440 | tf_op jit(solution)/shard_map/ppermute | solution.py:184
  7.2 19.5 %collective-permute-start.4 = (bf16[128,1024]{1,0:T(8,128)(2,1)S(1)}, bf16[128,1024]{1,0:T(8,128)(2,1)S(1)}, u32[]{:S(2)}, u32[]{:S(2)}) collective-permute-start(bf16[128,1024]{1,0:T(8,128)(2,1)S(1)} %get-tuple-element.88.refs_0_), channel_id=1, source_target_pairs={{0,4},{1,5},{2,6},{3,7},{4,0},{5,1},{6,2},{7,3},{8,12},{9,13},{10,... | collective-permute-start | bytes 786440 | tf_op jit(solution)/shard_map/ppermute | solution.py:176
  10.4 16.5 %collective-permute-start.5 = (bf16[128,1024]{1,0:T(8,128)(2,1)S(1)}, bf16[128,1024]{1,0:T(8,128)(2,1)S(1)}, u32[]{:S(2)}, u32[]{:S(2)}) collective-permute-start(bf16[128,1024]{1,0:T(8,128)(2,1)S(1)} %collective-permute-done.1.refs_2_), channel_id=1, source_target_pairs={{0,2},{1,3},{2,0},{3,1},{4,6},{5,7},{6,4},{7,5},{8,10},{9,11},{10,... | collective-permute-start | bytes 786440 | tf_op jit(solution)/shard_map/ppermute | solution.py:176
  17.6 14.0 %collective-permute-start.9 = (bf16[128,1024]{1,0:T(8,128)(2,1)S(1)}, bf16[128,1024]{1,0:T(8,128)(2,1)S(1)}, u32[]{:S(2)}, u32[]{:S(2)}) collective-permute-start(bf16[128,1024]{1,0:T(8,128)(2,1)S(1)} %collective-permute-done.8.refs_0_), channel_id=1, source_target_pairs={{0,1},{1,0},{2,3},{3,2},{4,5},{5,4},{6,7},{7,6},{8,9},{9,8},{10,11... | collective-permute-start | bytes 786440 | tf_op jit(solution)/shard_map/ppermute | solution.py:184
  20.5 11.3 %collective-permute-start.10 = (bf16[128,1024]{1,0:T(8,128)(2,1)S(1)}, bf16[128,1024]{1,0:T(8,128)(2,1)S(1)}, u32[]{:S(2)}, u32[]{:S(2)}) collective-permute-start(bf16[128,1024]{1,0:T(8,128)(2,1)S(1)} %collective-permute-done.1.refs_2_), channel_id=1, source_target_pairs={{0,1},{1,0},{2,3},{3,2},{4,5},{5,4},{6,7},{7,6},{8,9},{9,8},{10,11... | collective-permute-start | bytes 786440 | tf_op jit(solution)/shard_map/ppermute | solution.py:184
  20.5 16.8 %collective-permute-start.2 = (bf16[128,1024]{1,0:T(8,128)(2,1)S(1)}, bf16[128,1024]{1,0:T(8,128)(2,1)S(1)}, u32[]{:S(2)}, u32[]{:S(2)}) collective-permute-start(bf16[128,1024]{1,0:T(8,128)(2,1)S(1)} %collective-permute-done.1.refs_2_), channel_id=1, source_target_pairs={{0,4},{1,5},{2,6},{3,7},{4,0},{5,1},{6,2},{7,3},{8,12},{9,13},{10,... | collective-permute-start | bytes 786440 | tf_op jit(solution)/shard_map/ppermute | solution.py:176
  26.9 12.4 %collective-permute-start.6 = (bf16[128,1024]{1,0:T(8,128)(2,1)S(1)}, bf16[128,1024]{1,0:T(8,128)(2,1)S(1)}, u32[]{:S(2)}, u32[]{:S(2)}) collective-permute-start(bf16[128,1024]{1,0:T(8,128)(2,1)S(1)} %collective-permute-done.4.refs_0_), channel_id=1, source_target_pairs={{0,1},{1,0},{2,3},{3,2},{4,5},{5,4},{6,7},{7,6},{8,9},{9,8},{10,11... | collective-permute-start | bytes 786440 | tf_op jit(solution)/shard_map/ppermute | solution.py:184
  28.7 21.8 %collective-permute-start.12 = (bf16[128,1024]{1,0:T(8,128)(2,1)S(1)}, bf16[128,1024]{1,0:T(8,128)(2,1)S(1)}, u32[]{:S(2)}, u32[]{:S(2)}) collective-permute-start(bf16[128,1024]{1,0:T(8,128)(2,1)S(1)} %collective-permute-done.4.refs_0_), channel_id=1, source_target_pairs={{0,2},{1,3},{2,0},{3,1},{4,6},{5,7},{6,4},{7,5},{8,10},{9,11},{10,... | collective-permute-start | bytes 786440 | tf_op jit(solution)/shard_map/ppermute | solution.py:176
  31.6 11.1 %collective-permute-start.7 = (bf16[128,1024]{1,0:T(8,128)(2,1)S(1)}, bf16[128,1024]{1,0:T(8,128)(2,1)S(1)}, u32[]{:S(2)}, u32[]{:S(2)}) collective-permute-start(bf16[128,1024]{1,0:T(8,128)(2,1)S(1)} %collective-permute-done.5.refs_2_), channel_id=1, source_target_pairs={{0,1},{1,0},{2,3},{3,2},{4,5},{5,4},{6,7},{7,6},{8,9},{9,8},{10,11... | collective-permute-start | bytes 786440 | tf_op jit(solution)/shard_map/ppermute | solution.py:184
  37.3 13.2 %collective-permute-start.14 = (bf16[128,1024]{1,0:T(8,128)(2,1)S(1)}, bf16[128,1024]{1,0:T(8,128)(2,1)S(1)}, u32[]{:S(2)}, u32[]{:S(2)}) collective-permute-start(bf16[128,1024]{1,0:T(8,128)(2,1)S(1)} %collective-permute-done.2.refs_2_), channel_id=1, source_target_pairs={{0,1},{1,0},{2,3},{3,2},{4,5},{5,4},{6,7},{7,6},{8,9},{9,8},{10,11... | collective-permute-start | bytes 786440 | tf_op jit(solution)/shard_map/ppermute | solution.py:184
  39.3 9.1 %collective-permute-start.3 = (bf16[128,1024]{1,0:T(8,128)(2,1)S(1)}, bf16[128,1024]{1,0:T(8,128)(2,1)S(1)}, u32[]{:S(2)}, u32[]{:S(2)}) collective-permute-start(bf16[128,1024]{1,0:T(8,128)(2,1)S(1)} %collective-permute-done.2.refs_2_), channel_id=1, source_target_pairs={{0,2},{1,3},{2,0},{3,1},{4,6},{5,7},{6,4},{7,5},{8,10},{9,11},{10,... | collective-permute-start | bytes 786440 | tf_op jit(solution)/shard_map/ppermute | solution.py:176
  39.3 11.2 %collective-permute-start.13 = (bf16[128,1024]{1,0:T(8,128)(2,1)S(1)}, bf16[128,1024]{1,0:T(8,128)(2,1)S(1)}, u32[]{:S(2)}, u32[]{:S(2)}) collective-permute-start(bf16[128,1024]{1,0:T(8,128)(2,1)S(1)} %collective-permute-done.6.refs_1_), channel_id=1, source_target_pairs={{0,2},{1,3},{2,0},{3,1},{4,6},{5,7},{6,4},{7,5},{8,10},{9,11},{10,... | collective-permute-start | bytes 786440 | tf_op jit(solution)/shard_map/ppermute | solution.py:176
  48.4 7.6 %collective-permute-start.11 = (bf16[128,1024]{1,0:T(8,128)(2,1)S(1)}, bf16[128,1024]{1,0:T(8,128)(2,1)S(1)}, u32[]{:S(2)}, u32[]{:S(2)}) collective-permute-start(bf16[128,1024]{1,0:T(8,128)(2,1)S(1)} %collective-permute-done.3.refs_0_), channel_id=1, source_target_pairs={{0,1},{1,0},{2,3},{3,2},{4,5},{5,4},{6,7},{7,6},{8,9},{9,8},{10,11... | collective-permute-start | bytes 786440 | tf_op jit(solution)/shard_map/ppermute | solution.py:184
  56.1 4.0 %copy-start.1 = (f32[1024]{0:T(1024)S(1)}, f32[1024]{0:T(1024)}, u32[]{:S(2)}) copy-start(f32[1024]{0:T(1024)} %param.10) | copy-start | bytes 12292
  56.1 4.0 %copy-start.2 = (s32[1024]{0:T(1024)S(1)}, s32[1024]{0:T(1024)}, u32[]{:S(2)}) copy-start(s32[1024]{0:T(1024)} %param.12) | copy-start | bytes 12292
  58.9 10.9 %collective-permute-start.15 = (bf16[256,1024]{1,0:T(8,128)(2,1)S(1)}, bf16[256,1024]{1,0:T(8,128)(2,1)S(1)}, u32[]{:S(2)}, u32[]{:S(2)}) collective-permute-start(bf16[256,1024]{1,0:T(8,128)(2,1)S(1)} %get-tuple-element.73), channel_id=1, source_target_pairs={{0,1},{1,0},{2,3},{3,2},{4,5},{5,4},{6,7},{7,6},{8,9},{9,8},{10,11... | collective-permute-start | bytes 1572872 | tf_op jit(solution)/shard_map/ppermute | solution.py:184
  59.7 12.0 %collective-permute-start.18 = (bf16[512,512]{1,0:T(8,128)(2,1)S(1)}, bf16[512,512]{1,0:T(8,128)(2,1)S(1)}, u32[]{:S(2)}, u32[]{:S(2)}) collective-permute-start(bf16[512,512]{1,0:T(8,128)(2,1)S(1)} %get-tuple-element.75), channel_id=1, source_target_pairs={{0,2},{1,3},{2,0},{3,1},{4,6},{5,7},{6,4},{7,5},{8,10},{9,11},{10,... | collective-permute-start | bytes 1572872 | tf_op jit(solution)/shard_map/ppermute | solution.py:176
  60.2 6.7 %copy-start.3 = (s32[100]{0:T(128)S(1)}, s32[100]{0:T(128)}, u32[]{:S(2)}) copy-start(s32[100]{0:T(128)} %param.11) | copy-start | bytes 1204
  60.2 9.7 %copy-start.4 = (f32[100]{0:T(128)S(1)}, f32[100]{0:T(128)}, u32[]{:S(2)}) copy-start(f32[100]{0:T(128)} %param.9) | copy-start | bytes 1204
  69.9 8.3 %collective-permute-start.16 = (bf16[256,512]{1,0:T(8,128)(2,1)S(1)}, bf16[256,512]{1,0:T(8,128)(2,1)S(1)}, u32[]{:S(2)}, u32[]{:S(2)}) collective-permute-start(bf16[256,512]{1,0:T(8,128)(2,1)S(1)} %add_convert_fusion.1), channel_id=1, source_target_pairs={{0,2},{1,3},{2,0},{3,1},{4,6},{5,7},{6,4},{7,5},{8,10},{9,11},{10,... | collective-permute-start | bytes 786440 | tf_op jit(solution)/shard_map/ppermute | solution.py:176
  71.8 6.6 %collective-permute-start.19 = (bf16[256,512]{1,0:T(8,128)(2,1)S(1)}, bf16[256,512]{1,0:T(8,128)(2,1)S(1)}, u32[]{:S(2)}, u32[]{:S(2)}) collective-permute-start(bf16[256,512]{1,0:T(8,128)(2,1)S(1)} %add_convert_fusion), channel_id=1, source_target_pairs={{0,1},{1,0},{2,3},{3,2},{4,5},{5,4},{6,7},{7,6},{8,9},{9,8},{10,11... | collective-permute-start | bytes 786440 | tf_op jit(solution)/shard_map/ppermute | solution.py:184
  78.3 7.8 %collective-permute-start.17 = (bf16[256,256]{1,0:T(8,128)(2,1)S(1)}, bf16[256,256]{1,0:T(8,128)(2,1)S(1)}, u32[]{:S(2)}, u32[]{:S(2)}) collective-permute-start(bf16[256,256]{1,0:T(8,128)(2,1)S(1)} %select_convert_fusion.1), channel_id=1, source_target_pairs={{0,4},{1,5},{2,6},{3,7},{4,0},{5,1},{6,2},{7,3},{8,12},{9,13},{10,... | collective-permute-start | bytes 393224 | tf_op jit(solution)/shard_map/ppermute | solution.py:176
  78.5 8.9 %collective-permute-start.20 = (bf16[256,256]{1,0:T(8,128)(2,1)S(1)}, bf16[256,256]{1,0:T(8,128)(2,1)S(1)}, u32[]{:S(2)}, u32[]{:S(2)}) collective-permute-start(bf16[256,256]{1,0:T(8,128)(2,1)S(1)} %select_convert_fusion), channel_id=1, source_target_pairs={{0,4},{1,5},{2,6},{3,7},{4,0},{5,1},{6,2},{7,3},{8,12},{9,13},{10,... | collective-permute-start | bytes 393224 | tf_op jit(solution)/shard_map/ppermute | solution.py:176
  87.6 5.4 %collective-permute-start.21 = (f32[256,128]{1,0:T(8,128)S(1)}, f32[256,128]{1,0:T(8,128)S(1)}, u32[]{:S(2)}, u32[]{:S(2)}) collective-permute-start(f32[256,128]{1,0:T(8,128)S(1)} %slice_select_fusion.1), channel_id=1, source_target_pairs={{0,1},{1,0},{2,3},{3,2},{4,5},{5,4},{6,7},{7,6},{8,9},{9,8},{10,11... | collective-permute-start | bytes 393224 | tf_op jit(solution)/shard_map/ppermute | solution.py:184
  88.1 5.9 %collective-permute-start.22 = (f32[256,128]{1,0:T(8,128)S(1)}, f32[256,128]{1,0:T(8,128)S(1)}, u32[]{:S(2)}, u32[]{:S(2)}) collective-permute-start(f32[256,128]{1,0:T(8,128)S(1)} %slice_select_fusion), channel_id=1, source_target_pairs={{0,1},{1,0},{2,3},{3,2},{4,5},{5,4},{6,7},{7,6},{8,9},{9,8},{10,11... | collective-permute-start | bytes 393224 | tf_op jit(solution)/shard_map/ppermute | solution.py:184
  89.7 7.8 %collective-permute-start.23 = (bf16[128,256]{1,0:T(8,128)(2,1)S(1)}, bf16[128,256]{1,0:T(8,128)(2,1)S(1)}, u32[]{:S(2)}, u32[]{:S(2)}) collective-permute-start(bf16[128,256]{1,0:T(8,128)(2,1)S(1)} %get-tuple-element.96), channel_id=1, source_target_pairs={{0,22},{1,23},{2,20},{3,21},{4,18},{5,19},{6,16},{7,17},{8,30},{9,... | collective-permute-start | bytes 196616 | tf_op jit(solution)/shard_map/ppermute | solution.py:301
  91.5 6.7 %collective-permute-start.24 = (bf16[128,256]{1,0:T(8,128)(2,1)S(1)}, bf16[128,256]{1,0:T(8,128)(2,1)S(1)}, u32[]{:S(2)}, u32[]{:S(2)}) collective-permute-start(bf16[128,256]{1,0:T(8,128)(2,1)S(1)} %get-tuple-element.94), channel_id=1, source_target_pairs={{0,20},{1,21},{2,22},{3,23},{4,16},{5,17},{6,18},{7,19},{8,28},{9,... | collective-permute-start | bytes 196616 | tf_op jit(solution)/shard_map/ppermute | solution.py:301
  91.5 6.9 %collective-permute-start.26 = (bf16[128,256]{1,0:T(8,128)(2,1)S(1)}, bf16[128,256]{1,0:T(8,128)(2,1)S(1)}, u32[]{:S(2)}, u32[]{:S(2)}) collective-permute-start(bf16[128,256]{1,0:T(8,128)(2,1)S(1)} %get-tuple-element.95), channel_id=1, source_target_pairs={{0,16},{1,17},{2,18},{3,19},{4,20},{5,21},{6,22},{7,23},{8,24},{9,... | collective-permute-start | bytes 196616 | tf_op jit(solution)/shard_map/ppermute | solution.py:301
  94.1 5.2 %collective-permute-start.25 = (bf16[128,256]{1,0:T(8,128)(2,1)S(1)}, bf16[128,256]{1,0:T(8,128)(2,1)S(1)}, u32[]{:S(2)}, u32[]{:S(2)}) collective-permute-start(bf16[128,256]{1,0:T(8,128)(2,1)S(1)} %get-tuple-element.76), channel_id=1, source_target_pairs={{0,18},{1,19},{2,16},{3,17},{4,22},{5,23},{6,20},{7,21},{8,26},{9,... | collective-permute-start | bytes 196616 | tf_op jit(solution)/shard_map/ppermute | solution.py:301

commit v6 on v5

--- a/solution.py
+++ b/solution.py
@@ -114,7 +114,7 @@
         input_output_aliases=aliases,
         compiler_params=pltpu.CompilerParams(vmem_limit_bytes=VMEM_MIB * 1024 * 1024),
         cost_estimate=pl.CostEstimate(
-            flops=(0 if loads else 3) * factor_count * width * size * size,
+            flops=(1 if loads else 2) * factor_count * width * size * size,
             bytes_accessed=2 * factor_count * size * size + 4 * size * size + 2 * width * size,
             transcendentals=0,
         ),
@@ -255,7 +255,9 @@
         own_half = jnp.where(x_index == 0, turned[:, :row_count], turned[:, row_count:])
         other_half = jnp.concatenate(
             [
-                x_swap(jnp.where(x_index == 0, part[:, row_count:], part[:, :row_count]))
+                x_swap(
+                    jnp.where(x_index == 0, part[:, row_count:], part[:, :row_count]).astype(jnp.bfloat16)
+                ).astype(jnp.float32)
                 for part in (left, right)
             ],
             axis=0,

time: 101 us -> 101 us (level)
  starting transfers between devices: 39 us -> 33 us
  waiting for transfers between devices: 25.2 us -> 31 us
    ppermute x11, starting transfers between devices: 14.6 us -> 9.73 us  [x_swap(): return lax.ppermute(block, 'vir', [(i, i ^ 1) for i in range(vir_devices)])]
    ppermute x11, waiting for transfers between devices: 18.1 us -> 22.7 us  [z_swap(): return lax.ppermute(block, 'vir', route)]
    ppermute x11, starting transfers between devices: 15.4 us -> 14.3 us  [z_swap(): return lax.ppermute(block, 'vir', route)]
where the time goes in v6:
time: 101 us; the launch traced here: 100 us
  starting transfers between devices  33 us (33%)
  Pallas kernels  31.2 us (31%)
  waiting for transfers between devices  31 us (31%)
  other arithmetic  2.66 us (3%)
  local copies, waits for them, and re-layouts  2.09 us (2%)
    pallas_call x5, Pallas kernels, ladder(): pl.pallas_call(functools.partial(ladder_kernel, distances, len(kept), sum...  24.5 us
    ppermute x11, waiting for transfers between devices, z_swap(): return lax.ppermute(block, 'vir', route)  22.7 us
    ppermute x11, starting transfers between devices, z_swap(): return lax.ppermute(block, 'vir', route)  14.3 us
    ppermute x11, starting transfers between devices, x_swap(): return lax.ppermute(block, 'vir', [(i, i ^ 1) for i in range(vir_devices)])  9.73 us
    pallas_call x1, Pallas kernels, keep_sums(): pl.pallas_call(functools.partial(keep_kernel, len(parts)), out_shape=[jax...  6.67 us
    ppermute x4, starting transfers between devices, per_device(): came.append(lax.ppermute(leaving, ('occ', 'vir'), route))  5.92 us
    ppermute x11, waiting for transfers between devices, x_swap(): return lax.ppermute(block, 'vir', [(i, i ^ 1) for i in range(vir_devices)])  5.17 us
    ppermute x1, starting transfers between devices, y_swap(): lax.ppermute(block, 'occ', [(i, (i + across) % occ_devices) for i in rang...  3.03 us
  transfers between devices with their start and end apart: 27, of which 13 were waited for; matrix products, arithmetic and copies ran while one was open for 2% of the time, Pallas kernels for 28%

profile of v6, /device:TPU:0, one launch (start us, length us, event | category | flops | bytes accessed | tf_op | source)
XLA Modules:
  0.0 100.5 jit_solution(5418578431478414912)
XLA Ops:
  1.1 3.0 %collective-permute-start.1 = (bf16[128,1024]{1,0:T(8,128)(2,1)S(1)}, bf16[128,1024]{1,0:T(8,128)(2,1)S(1)}, u32[]{:S(2)}, u32[]{:S(2)}) collective-permute-start(bf16[128,1024]{1,0:T(8,128)(2,1)S(1)} %get-tuple-element.87), channel_id=1, source_target_pairs={{0,16},{8,24},{16,0},{24,8},{1,17},{9,25},{17,1},{25,9},{2,18},{10... | collective-permute-start | bytes 786440 | tf_op jit(solution)/shard_map/ppermute | solution.py:179
  4.1 1.5 %collective-permute-start = (bf16[128,1024]{1,0:T(8,128)(2,1)S(1)}, bf16[128,1024]{1,0:T(8,128)(2,1)S(1)}, u32[]{:S(2)}, u32[]{:S(2)}) collective-permute-start(bf16[128,1024]{1,0:T(8,128)(2,1)S(1)} %get-tuple-element.88.refs_0_), channel_id=1, source_target_pairs={{0,1},{1,0},{2,3},{3,2},{4,5},{5,4},{6,7},{7,6},{8,9},{9,8},{10,11... | collective-permute-start | bytes 786440 | tf_op jit(solution)/shard_map/ppermute | solution.py:184
  5.6 1.6 %collective-permute-start.8 = (bf16[128,1024]{1,0:T(8,128)(2,1)S(1)}, bf16[128,1024]{1,0:T(8,128)(2,1)S(1)}, u32[]{:S(2)}, u32[]{:S(2)}) collective-permute-start(bf16[128,1024]{1,0:T(8,128)(2,1)S(1)} %get-tuple-element.88.refs_0_), channel_id=1, source_target_pairs={{0,2},{1,3},{2,0},{3,1},{4,6},{5,7},{6,4},{7,5},{8,10},{9,11},{10,... | collective-permute-start | bytes 786440 | tf_op jit(solution)/shard_map/ppermute | solution.py:176
  7.2 2.6 %collective-permute-start.4 = (bf16[128,1024]{1,0:T(8,128)(2,1)S(1)}, bf16[128,1024]{1,0:T(8,128)(2,1)S(1)}, u32[]{:S(2)}, u32[]{:S(2)}) collective-permute-start(bf16[128,1024]{1,0:T(8,128)(2,1)S(1)} %get-tuple-element.88.refs_0_), channel_id=1, source_target_pairs={{0,4},{1,5},{2,6},{3,7},{4,0},{5,1},{6,2},{7,3},{8,12},{9,13},{10,... | collective-permute-start | bytes 786440 | tf_op jit(solution)/shard_map/ppermute | solution.py:176
  10.4 1.8 %collective-permute-start.5 = (bf16[128,1024]{1,0:T(8,128)(2,1)S(1)}, bf16[128,1024]{1,0:T(8,128)(2,1)S(1)}, u32[]{:S(2)}, u32[]{:S(2)}) collective-permute-start(bf16[128,1024]{1,0:T(8,128)(2,1)S(1)} %collective-permute-done.1.refs_2_), channel_id=1, source_target_pairs={{0,2},{1,3},{2,0},{3,1},{4,6},{5,7},{6,4},{7,5},{8,10},{9,11},{10,... | collective-permute-start | bytes 786440 | tf_op jit(solution)/shard_map/ppermute | solution.py:176
  12.2 2.6 %collective-permute-start.2 = (bf16[128,1024]{1,0:T(8,128)(2,1)S(1)}, bf16[128,1024]{1,0:T(8,128)(2,1)S(1)}, u32[]{:S(2)}, u32[]{:S(2)}) collective-permute-start(bf16[128,1024]{1,0:T(8,128)(2,1)S(1)} %collective-permute-done.1.refs_2_), channel_id=1, source_target_pairs={{0,4},{1,5},{2,6},{3,7},{4,0},{5,1},{6,2},{7,3},{8,12},{9,13},{10,... | collective-permute-start | bytes 786440 | tf_op jit(solution)/shard_map/ppermute | solution.py:176
  14.8 1.5 %collective-permute-start.10 = (bf16[128,1024]{1,0:T(8,128)(2,1)S(1)}, bf16[128,1024]{1,0:T(8,128)(2,1)S(1)}, u32[]{:S(2)}, u32[]{:S(2)}) collective-permute-start(bf16[128,1024]{1,0:T(8,128)(2,1)S(1)} %collective-permute-done.1.refs_2_), channel_id=1, source_target_pairs={{0,1},{1,0},{2,3},{3,2},{4,5},{5,4},{6,7},{7,6},{8,9},{9,8},{10,11... | collective-permute-start | bytes 786440 | tf_op jit(solution)/shard_map/ppermute | solution.py:184
  16.3 5.3 %collective-permute-done.8.refs_0_ = bf16[128,1024]{1,0:T(8,128)(2,1)S(1)} collective-permute-done((bf16[128,1024]{1,0:T(8,128)(2,1)S(1)}, bf16[128,1024]{1,0:T(8,128)(2,1)S(1)}, u32[]{:S(2)}, u32[]{:S(2)}) %collective-permute-start.8) | collective-permute-done | bytes 262176 | tf_op jit(solution)/shard_map/ppermute | solution.py:176
  22.1 5.0 %shard_map.73 = (f32[256,1024]{1,0:T(8,128)S(1)}, f32[512,512]{1,0:T(8,128)S(1)}, bf16[1024,768]{1,0:T(8,128)(2,1)S(1)}, bf16[1024,768]{1,0:T(8,128)(2,1)S(1)}, bf16[3,1024,1024]{2,1,0:T(8,128)(2,1)S(1)}) custom-call(bf16[3,1024,1024]{2,1,0:T(8,128)(2,1)} %factor_ref.1, bf16[128,1024]{1,0:T(8,128)(2,1)S(1)} %get-tuple-element.88.refs_0_, ...), custom_call_target="tpu_custom_call" | custom-call | flops 805306368 | bytes 11010048 | tf_op jit(solution)/shard_map/pallas_call | solution.py:108
  27.1 2.7 %collective-permute-done.5.refs_2_ = bf16[128,1024]{1,0:T(8,128)(2,1)S(1)} collective-permute-done((bf16[128,1024]{1,0:T(8,128)(2,1)S(1)}, bf16[128,1024]{1,0:T(8,128)(2,1)S(1)}, u32[]{:S(2)}, u32[]{:S(2)}) %collective-permute-start.5) | collective-permute-done | bytes 262176 | tf_op jit(solution)/shard_map/ppermute | solution.py:176
  30.4 2.0 %collective-permute-done.2.refs_2_ = bf16[128,1024]{1,0:T(8,128)(2,1)S(1)} collective-permute-done((bf16[128,1024]{1,0:T(8,128)(2,1)S(1)}, bf16[128,1024]{1,0:T(8,128)(2,1)S(1)}, u32[]{:S(2)}, u32[]{:S(2)}) %collective-permute-start.2) | collective-permute-done | bytes 262176 | tf_op jit(solution)/shard_map/ppermute | solution.py:176
  33.9 5.5 %shard_map.74 = (f32[256,1024]{1,0:T(8,128)S(1)}, f32[512,512]{1,0:T(8,128)S(1)}, bf16[1024,1536]{1,0:T(8,128)(2,1)S(1)}, bf16[1024,1536]{1,0:T(8,128)(2,1)S(1)}) custom-call(bf16[3,1024,1024]{2,1,0:T(8,128)(2,1)S(1)} %get-tuple-element.42.factor_ref, ...), custom_call_target="tpu_custom_call", output_to_operand_aliasing={{0}: (5, {}), {1}: (6, {})} | custom-call | flops 3221225472 | bytes 11534336 | tf_op jit(solution)/shard_map/pallas_call | solution.py:108
  40.3 1.7 %collective-permute-start.13 = (bf16[128,1024]{1,0:T(8,128)(2,1)S(1)}, bf16[128,1024]{1,0:T(8,128)(2,1)S(1)}, u32[]{:S(2)}, u32[]{:S(2)}) collective-permute-start(bf16[128,1024]{1,0:T(8,128)(2,1)S(1)} %collective-permute-done.6.refs_1_), channel_id=1, source_target_pairs={{0,2},{1,3},{2,0},{3,1},{4,6},{5,7},{6,4},{7,5},{8,10},{9,11},{10,... | collective-permute-start | bytes 786440 | tf_op jit(solution)/shard_map/ppermute | solution.py:176
  42.0 2.2 %collective-permute-done.7.refs_3_ = bf16[128,1024]{1,0:T(8,128)(2,1)S(1)} collective-permute-done((bf16[128,1024]{1,0:T(8,128)(2,1)S(1)}, bf16[128,1024]{1,0:T(8,128)(2,1)S(1)}, u32[]{:S(2)}, u32[]{:S(2)}) %collective-permute-start.7) | collective-permute-done | bytes 262176 | tf_op jit(solution)/shard_map/ppermute | solution.py:184
  44.2 5.7 %shard_map.75 = (f32[256,1024]{1,0:T(8,128)S(1)}, f32[512,512]{1,0:T(8,128)S(1)}, bf16[1024,1536]{1,0:T(8,128)(2,1)S(1)}, bf16[1024,1536]{1,0:T(8,128)(2,1)S(1)}) custom-call(bf16[3,1024,1024]{2,1,0:T(8,128)(2,1)S(1)} %get-tuple-element.42.factor_ref, ...), custom_call_target="tpu_custom_call", output_to_operand_aliasing={{0}: (5, {}), {1}: (6, {})} | custom-call | flops 3221225472 | bytes 11534336 | tf_op jit(solution)/shard_map/pallas_call | solution.py:108
  50.0 5.5 %shard_map.76 = (f32[256,1024]{1,0:T(8,128)S(1)}, f32[512,512]{1,0:T(8,128)S(1)}, bf16[1024,1536]{1,0:T(8,128)(2,1)S(1)}, bf16[1024,1536]{1,0:T(8,128)(2,1)S(1)}) custom-call(bf16[3,1024,1024]{2,1,0:T(8,128)(2,1)S(1)} %get-tuple-element.42.factor_ref, ...), custom_call_target="tpu_custom_call", output_to_operand_aliasing={{0}: (5, {}), {1}: (6, {})} | custom-call | flops 3221225472 | bytes 11534336 | tf_op jit(solution)/shard_map/pallas_call | solution.py:108
  56.4 2.8 %shard_map.77 = (bf16[256,1024]{1,0:T(8,128)(2,1)S(1)}, bf16[512,512]{1,0:T(8,128)(2,1)S(1)}, bf16[1024,768]{1,0:T(8,128)(2,1)S(1)}, bf16[1024,768]{1,0:T(8,128)(2,1)S(1)}) custom-call(bf16[3,1024,1024]{2,1,0:T(8,128)(2,1)S(1)} %get-tuple-element.42.factor_ref, bf16[128,1024]{1,0:T(8,128)(2,1)S(1)} %collective-permute-done.3.refs_0_, ...), custom_call_target="tpu_custom_call" | custom-call | flops 1610612736 | bytes 11010048 | tf_op jit(solution)/shard_map/pallas_call | solution.py:108
  59.4 1.3 %collective-permute-start.15 = (bf16[256,1024]{1,0:T(8,128)(2,1)S(1)}, bf16[256,1024]{1,0:T(8,128)(2,1)S(1)}, u32[]{:S(2)}, u32[]{:S(2)}) collective-permute-start(bf16[256,1024]{1,0:T(8,128)(2,1)S(1)} %get-tuple-element.73), channel_id=1, source_target_pairs={{0,1},{1,0},{2,3},{3,2},{4,5},{5,4},{6,7},{7,6},{8,9},{9,8},{10,11... | collective-permute-start | bytes 1572872 | tf_op jit(solution)/shard_map/ppermute | solution.py:184
  60.7 6.7 %shard_map.78 = (f32[256,1024]{1,0:T(8,128)S(1)}, f32[512,512]{1,0:T(8,128)S(1)}) custom-call(bf16[1024,768]{1,0:T(8,128)(2,1)S(1)} %get-tuple-element.43.refs_0_, bf16[1024,768]{1,0:T(8,128)(2,1)S(1)} %get-tuple-element.66.refs_1_, bf16[1024,1536]{1,0:T(8,128)(2,1)S(1)} %get-tuple-element.55.refs_2_, bf16[1024,1536]{1,0:T(8,128)(2,1)S(1)} %get-tuple-element.67.refs_3_, ...), custom_call_target="tpu_custom_call" | custom-call | flops 6442450944 | bytes 27262976 | tf_op jit(solution)/shard_map/pallas_call | solution.py:145
  68.0 2.2 %collective-permute-done.15 = bf16[256,1024]{1,0:T(8,128)(2,1)S(1)} collective-permute-done((bf16[256,1024]{1,0:T(8,128)(2,1)S(1)}, bf16[256,1024]{1,0:T(8,128)(2,1)S(1)}, u32[]{:S(2)}, u32[]{:S(2)}) %collective-permute-start.15) | collective-permute-done | bytes 524320 | tf_op jit(solution)/shard_map/ppermute | solution.py:184
  70.5 2.1 %collective-permute-done.18 = bf16[512,512]{1,0:T(8,128)(2,1)S(1)} collective-permute-done((bf16[512,512]{1,0:T(8,128)(2,1)S(1)}, bf16[512,512]{1,0:T(8,128)(2,1)S(1)}, u32[]{:S(2)}, u32[]{:S(2)}) %collective-permute-start.18) | collective-permute-done | bytes 524320 | tf_op jit(solution)/shard_map/ppermute | solution.py:176
  73.6 4.7 %collective-permute-done.16 = bf16[256,512]{1,0:T(8,128)(2,1)S(1)} collective-permute-done((bf16[256,512]{1,0:T(8,128)(2,1)S(1)}, bf16[256,512]{1,0:T(8,128)(2,1)S(1)}, u32[]{:S(2)}, u32[]{:S(2)}) %collective-permute-start.16) | collective-permute-done | bytes 262176 | tf_op jit(solution)/shard_map/ppermute | solution.py:176
  78.5 1.1 %collective-permute-start.17 = (bf16[256,256]{1,0:T(8,128)(2,1)S(1)}, bf16[256,256]{1,0:T(8,128)(2,1)S(1)}, u32[]{:S(2)}, u32[]{:S(2)}) collective-permute-start(bf16[256,256]{1,0:T(8,128)(2,1)S(1)} %select_convert_fusion.1), channel_id=1, source_target_pairs={{0,4},{1,5},{2,6},{3,7},{4,0},{5,1},{6,2},{7,3},{8,12},{9,13},{10,... | collective-permute-start | bytes 393224 | tf_op jit(solution)/shard_map/ppermute | solution.py:176
  79.7 2.0 %collective-permute-start.20 = (bf16[256,256]{1,0:T(8,128)(2,1)S(1)}, bf16[256,256]{1,0:T(8,128)(2,1)S(1)}, u32[]{:S(2)}, u32[]{:S(2)}) collective-permute-start(bf16[256,256]{1,0:T(8,128)(2,1)S(1)} %select_convert_fusion), channel_id=1, source_target_pairs={{0,4},{1,5},{2,6},{3,7},{4,0},{5,1},{6,2},{7,3},{8,12},{9,13},{10,... | collective-permute-start | bytes 393224 | tf_op jit(solution)/shard_map/ppermute | solution.py:176
  81.7 4.5 %collective-permute-done.17 = bf16[256,256]{1,0:T(8,128)(2,1)S(1)} collective-permute-done((bf16[256,256]{1,0:T(8,128)(2,1)S(1)}, bf16[256,256]{1,0:T(8,128)(2,1)S(1)}, u32[]{:S(2)}, u32[]{:S(2)}) %collective-permute-start.17) | collective-permute-done | bytes 131104 | tf_op jit(solution)/shard_map/ppermute | solution.py:176
  86.2 1.4 %collective-permute-done.20 = bf16[256,256]{1,0:T(8,128)(2,1)S(1)} collective-permute-done((bf16[256,256]{1,0:T(8,128)(2,1)S(1)}, bf16[256,256]{1,0:T(8,128)(2,1)S(1)}, u32[]{:S(2)}, u32[]{:S(2)}) %collective-permute-start.20) | collective-permute-done | bytes 131104 | tf_op jit(solution)/shard_map/ppermute | solution.py:176
  87.7 1.5 %collective-permute-start.21 = (bf16[256,128]{1,0:T(8,128)(2,1)S(1)}, bf16[256,128]{1,0:T(8,128)(2,1)S(1)}, u32[]{:S(2)}, u32[]{:S(2)}) collective-permute-start(bf16[256,128]{1,0:T(8,128)(2,1)S(1)} %fusion.6), channel_id=1, source_target_pairs={{0,1},{1,0},{2,3},{3,2},{4,5},{5,4},{6,7},{7,6},{8,9},{9,8},{10,11... | collective-permute-start | bytes 196616 | tf_op jit(solution)/shard_map/ppermute | solution.py:184
  89.9 3.0 %collective-permute-start.23 = (bf16[128,256]{1,0:T(8,128)(2,1)S(1)}, bf16[128,256]{1,0:T(8,128)(2,1)S(1)}, u32[]{:S(2)}, u32[]{:S(2)}) collective-permute-start(bf16[128,256]{1,0:T(8,128)(2,1)S(1)} %get-tuple-element.96), channel_id=1, source_target_pairs={{0,22},{1,23},{2,20},{3,21},{4,18},{5,19},{6,16},{7,17},{8,30},{9,... | collective-permute-start | bytes 196616 | tf_op jit(solution)/shard_map/ppermute | solution.py:303
  92.9 1.2 %collective-permute-start.24 = (bf16[128,256]{1,0:T(8,128)(2,1)S(1)}, bf16[128,256]{1,0:T(8,128)(2,1)S(1)}, u32[]{:S(2)}, u32[]{:S(2)}) collective-permute-start(bf16[128,256]{1,0:T(8,128)(2,1)S(1)} %get-tuple-element.94), channel_id=1, source_target_pairs={{0,20},{1,21},{2,22},{3,23},{4,16},{5,17},{6,18},{7,19},{8,28},{9,... | collective-permute-start | bytes 196616 | tf_op jit(solution)/shard_map/ppermute | solution.py:303
  94.1 1.6 %collective-permute-start.26 = (bf16[128,256]{1,0:T(8,128)(2,1)S(1)}, bf16[128,256]{1,0:T(8,128)(2,1)S(1)}, u32[]{:S(2)}, u32[]{:S(2)}) collective-permute-start(bf16[128,256]{1,0:T(8,128)(2,1)S(1)} %get-tuple-element.95), channel_id=1, source_target_pairs={{0,16},{1,17},{2,18},{3,19},{4,20},{5,21},{6,22},{7,23},{8,24},{9,... | collective-permute-start | bytes 196616 | tf_op jit(solution)/shard_map/ppermute | solution.py:303
  97.0 2.1 %collective-permute-done.24 = bf16[128,256]{1,0:T(8,128)(2,1)S(1)} collective-permute-done((bf16[128,256]{1,0:T(8,128)(2,1)S(1)}, bf16[128,256]{1,0:T(8,128)(2,1)S(1)}, u32[]{:S(2)}, u32[]{:S(2)}) %collective-permute-start.24) | collective-permute-done | bytes 65568 | tf_op jit(solution)/shard_map/ppermute | solution.py:303
  99.2 1.3 %fusion = f32[2,128,1024]{2,1,0:T(8,128)} fusion(f32[1,128,1024]{2,1,0:T(8,128)S(1)} %get-tuple-element.86, f32[1,128,1024]{2,1,0:T(8,128)S(1)} %get-tuple-element.85, f32[2]{0:T(128)S(1)} %add.91, f32[128,1024]{1,0:T(8,128)S(1)} %broadcast_add_fusion, s32[1024]{0:T(1024)S(1)} %copy-done.2, s32[2,128]{1,0:T(2,128)S(1)} %broadcast_xor_fusion), kind=kLoop, calls=%fused_computation.1 | loop fusion | flops 1572864 | bytes 2626568 | tf_op jit(solution)/shard_map/jit(_where)/select_n | solution.py:338
  (69 shorter events, 10.5 us)
Async XLA Ops:
  0.0 59.2 %copy-start = (s32[8,2]{0,1:T(2,128)S(1)}, s32[8,2]{0,1:T(2,128)}, u32[]{:S(2)}) copy-start(s32[8,2]{0,1:T(2,128)} %param.13) | copy-start | bytes 196
  1.1 9.3 %collective-permute-start.1 = (bf16[128,1024]{1,0:T(8,128)(2,1)S(1)}, bf16[128,1024]{1,0:T(8,128)(2,1)S(1)}, u32[]{:S(2)}, u32[]{:S(2)}) collective-permute-start(bf16[128,1024]{1,0:T(8,128)(2,1)S(1)} %get-tuple-element.87), channel_id=1, source_target_pairs={{0,16},{8,24},{16,0},{24,8},{1,17},{9,25},{17,1},{25,9},{2,18},{10... | collective-permute-start | bytes 786440 | tf_op jit(solution)/shard_map/ppermute | solution.py:179
  4.1 10.7 %collective-permute-start = (bf16[128,1024]{1,0:T(8,128)(2,1)S(1)}, bf16[128,1024]{1,0:T(8,128)(2,1)S(1)}, u32[]{:S(2)}, u32[]{:S(2)}) collective-permute-start(bf16[128,1024]{1,0:T(8,128)(2,1)S(1)} %get-tuple-element.88.refs_0_), channel_id=1, source_target_pairs={{0,1},{1,0},{2,3},{3,2},{4,5},{5,4},{6,7},{7,6},{8,9},{9,8},{10,11... | collective-permute-start | bytes 786440 | tf_op jit(solution)/shard_map/ppermute | solution.py:184
  5.6 16.0 %collective-permute-start.8 = (bf16[128,1024]{1,0:T(8,128)(2,1)S(1)}, bf16[128,1024]{1,0:T(8,128)(2,1)S(1)}, u32[]{:S(2)}, u32[]{:S(2)}) collective-permute-start(bf16[128,1024]{1,0:T(8,128)(2,1)S(1)} %get-tuple-element.88.refs_0_), channel_id=1, source_target_pairs={{0,2},{1,3},{2,0},{3,1},{4,6},{5,7},{6,4},{7,5},{8,10},{9,11},{10,... | collective-permute-start | bytes 786440 | tf_op jit(solution)/shard_map/ppermute | solution.py:176
  7.2 19.9 %collective-permute-start.4 = (bf16[128,1024]{1,0:T(8,128)(2,1)S(1)}, bf16[128,1024]{1,0:T(8,128)(2,1)S(1)}, u32[]{:S(2)}, u32[]{:S(2)}) collective-permute-start(bf16[128,1024]{1,0:T(8,128)(2,1)S(1)} %get-tuple-element.88.refs_0_), channel_id=1, source_target_pairs={{0,4},{1,5},{2,6},{3,7},{4,0},{5,1},{6,2},{7,3},{8,12},{9,13},{10,... | collective-permute-start | bytes 786440 | tf_op jit(solution)/shard_map/ppermute | solution.py:176
  10.4 19.4 %collective-permute-start.5 = (bf16[128,1024]{1,0:T(8,128)(2,1)S(1)}, bf16[128,1024]{1,0:T(8,128)(2,1)S(1)}, u32[]{:S(2)}, u32[]{:S(2)}) collective-permute-start(bf16[128,1024]{1,0:T(8,128)(2,1)S(1)} %collective-permute-done.1.refs_2_), channel_id=1, source_target_pairs={{0,2},{1,3},{2,0},{3,1},{4,6},{5,7},{6,4},{7,5},{8,10},{9,11},{10,... | collective-permute-start | bytes 786440 | tf_op jit(solution)/shard_map/ppermute | solution.py:176
  12.2 20.1 %collective-permute-start.2 = (bf16[128,1024]{1,0:T(8,128)(2,1)S(1)}, bf16[128,1024]{1,0:T(8,128)(2,1)S(1)}, u32[]{:S(2)}, u32[]{:S(2)}) collective-permute-start(bf16[128,1024]{1,0:T(8,128)(2,1)S(1)} %collective-permute-done.1.refs_2_), channel_id=1, source_target_pairs={{0,4},{1,5},{2,6},{3,7},{4,0},{5,1},{6,2},{7,3},{8,12},{9,13},{10,... | collective-permute-start | bytes 786440 | tf_op jit(solution)/shard_map/ppermute | solution.py:176
  14.8 18.1 %collective-permute-start.10 = (bf16[128,1024]{1,0:T(8,128)(2,1)S(1)}, bf16[128,1024]{1,0:T(8,128)(2,1)S(1)}, u32[]{:S(2)}, u32[]{:S(2)}) collective-permute-start(bf16[128,1024]{1,0:T(8,128)(2,1)S(1)} %collective-permute-done.1.refs_2_), channel_id=1, source_target_pairs={{0,1},{1,0},{2,3},{3,2},{4,5},{5,4},{6,7},{7,6},{8,9},{9,8},{10,11... | collective-permute-start | bytes 786440 | tf_op jit(solution)/shard_map/ppermute | solution.py:184
  21.6 12.3 %collective-permute-start.9 = (bf16[128,1024]{1,0:T(8,128)(2,1)S(1)}, bf16[128,1024]{1,0:T(8,128)(2,1)S(1)}, u32[]{:S(2)}, u32[]{:S(2)}) collective-permute-start(bf16[128,1024]{1,0:T(8,128)(2,1)S(1)} %collective-permute-done.8.refs_0_), channel_id=1, source_target_pairs={{0,1},{1,0},{2,3},{3,2},{4,5},{5,4},{6,7},{7,6},{8,9},{9,8},{10,11... | collective-permute-start | bytes 786440 | tf_op jit(solution)/shard_map/ppermute | solution.py:184
  29.8 10.5 %collective-permute-start.6 = (bf16[128,1024]{1,0:T(8,128)(2,1)S(1)}, bf16[128,1024]{1,0:T(8,128)(2,1)S(1)}, u32[]{:S(2)}, u32[]{:S(2)}) collective-permute-start(bf16[128,1024]{1,0:T(8,128)(2,1)S(1)} %collective-permute-done.4.refs_0_), channel_id=1, source_target_pairs={{0,1},{1,0},{2,3},{3,2},{4,5},{5,4},{6,7},{7,6},{8,9},{9,8},{10,11... | collective-permute-start | bytes 786440 | tf_op jit(solution)/shard_map/ppermute | solution.py:184
  30.4 19.6 %collective-permute-start.12 = (bf16[128,1024]{1,0:T(8,128)(2,1)S(1)}, bf16[128,1024]{1,0:T(8,128)(2,1)S(1)}, u32[]{:S(2)}, u32[]{:S(2)}) collective-permute-start(bf16[128,1024]{1,0:T(8,128)(2,1)S(1)} %collective-permute-done.4.refs_0_), channel_id=1, source_target_pairs={{0,2},{1,3},{2,0},{3,1},{4,6},{5,7},{6,4},{7,5},{8,10},{9,11},{10,... | collective-permute-start | bytes 786440 | tf_op jit(solution)/shard_map/ppermute | solution.py:176
  32.3 11.9 %collective-permute-start.7 = (bf16[128,1024]{1,0:T(8,128)(2,1)S(1)}, bf16[128,1024]{1,0:T(8,128)(2,1)S(1)}, u32[]{:S(2)}, u32[]{:S(2)}) collective-permute-start(bf16[128,1024]{1,0:T(8,128)(2,1)S(1)} %collective-permute-done.5.refs_2_), channel_id=1, source_target_pairs={{0,1},{1,0},{2,3},{3,2},{4,5},{5,4},{6,7},{7,6},{8,9},{9,8},{10,11... | collective-permute-start | bytes 786440 | tf_op jit(solution)/shard_map/ppermute | solution.py:184
  32.9 17.0 %collective-permute-start.3 = (bf16[128,1024]{1,0:T(8,128)(2,1)S(1)}, bf16[128,1024]{1,0:T(8,128)(2,1)S(1)}, u32[]{:S(2)}, u32[]{:S(2)}) collective-permute-start(bf16[128,1024]{1,0:T(8,128)(2,1)S(1)} %collective-permute-done.2.refs_2_), channel_id=1, source_target_pairs={{0,2},{1,3},{2,0},{3,1},{4,6},{5,7},{6,4},{7,5},{8,10},{9,11},{10,... | collective-permute-start | bytes 786440 | tf_op jit(solution)/shard_map/ppermute | solution.py:176
  39.4 10.6 %collective-permute-start.14 = (bf16[128,1024]{1,0:T(8,128)(2,1)S(1)}, bf16[128,1024]{1,0:T(8,128)(2,1)S(1)}, u32[]{:S(2)}, u32[]{:S(2)}) collective-permute-start(bf16[128,1024]{1,0:T(8,128)(2,1)S(1)} %collective-permute-done.2.refs_2_), channel_id=1, source_target_pairs={{0,1},{1,0},{2,3},{3,2},{4,5},{5,4},{6,7},{7,6},{8,9},{9,8},{10,11... | collective-permute-start | bytes 786440 | tf_op jit(solution)/shard_map/ppermute | solution.py:184
  40.3 9.7 %collective-permute-start.13 = (bf16[128,1024]{1,0:T(8,128)(2,1)S(1)}, bf16[128,1024]{1,0:T(8,128)(2,1)S(1)}, u32[]{:S(2)}, u32[]{:S(2)}) collective-permute-start(bf16[128,1024]{1,0:T(8,128)(2,1)S(1)} %collective-permute-done.6.refs_1_), channel_id=1, source_target_pairs={{0,2},{1,3},{2,0},{3,1},{4,6},{5,7},{6,4},{7,5},{8,10},{9,11},{10,... | collective-permute-start | bytes 786440 | tf_op jit(solution)/shard_map/ppermute | solution.py:176
  49.9 6.4 %collective-permute-start.11 = (bf16[128,1024]{1,0:T(8,128)(2,1)S(1)}, bf16[128,1024]{1,0:T(8,128)(2,1)S(1)}, u32[]{:S(2)}, u32[]{:S(2)}) collective-permute-start(bf16[128,1024]{1,0:T(8,128)(2,1)S(1)} %collective-permute-done.3.refs_0_), channel_id=1, source_target_pairs={{0,1},{1,0},{2,3},{3,2},{4,5},{5,4},{6,7},{7,6},{8,9},{9,8},{10,11... | collective-permute-start | bytes 786440 | tf_op jit(solution)/shard_map/ppermute | solution.py:184
  56.3 2.9 %copy-start.2 = (s32[1024]{0:T(1024)S(1)}, s32[1024]{0:T(1024)}, u32[]{:S(2)}) copy-start(s32[1024]{0:T(1024)} %param.12) | copy-start | bytes 12292
  56.3 3.0 %copy-start.1 = (f32[1024]{0:T(1024)S(1)}, f32[1024]{0:T(1024)}, u32[]{:S(2)}) copy-start(f32[1024]{0:T(1024)} %param.10) | copy-start | bytes 12292
  59.4 10.7 %collective-permute-start.15 = (bf16[256,1024]{1,0:T(8,128)(2,1)S(1)}, bf16[256,1024]{1,0:T(8,128)(2,1)S(1)}, u32[]{:S(2)}, u32[]{:S(2)}) collective-permute-start(bf16[256,1024]{1,0:T(8,128)(2,1)S(1)} %get-tuple-element.73), channel_id=1, source_target_pairs={{0,1},{1,0},{2,3},{3,2},{4,5},{5,4},{6,7},{7,6},{8,9},{9,8},{10,11... | collective-permute-start | bytes 1572872 | tf_op jit(solution)/shard_map/ppermute | solution.py:184
  60.7 12.0 %collective-permute-start.18 = (bf16[512,512]{1,0:T(8,128)(2,1)S(1)}, bf16[512,512]{1,0:T(8,128)(2,1)S(1)}, u32[]{:S(2)}, u32[]{:S(2)}) collective-permute-start(bf16[512,512]{1,0:T(8,128)(2,1)S(1)} %get-tuple-element.75), channel_id=1, source_target_pairs={{0,2},{1,3},{2,0},{3,1},{4,6},{5,7},{6,4},{7,5},{8,10},{9,11},{10,... | collective-permute-start | bytes 1572872 | tf_op jit(solution)/shard_map/ppermute | solution.py:176
  60.7 6.7 %copy-start.3 = (s32[100]{0:T(128)S(1)}, s32[100]{0:T(128)}, u32[]{:S(2)}) copy-start(s32[100]{0:T(128)} %param.11) | copy-start | bytes 1204
  60.7 9.6 %copy-start.4 = (f32[100]{0:T(128)S(1)}, f32[100]{0:T(128)}, u32[]{:S(2)}) copy-start(f32[100]{0:T(128)} %param.9) | copy-start | bytes 1204
  70.2 8.1 %collective-permute-start.16 = (bf16[256,512]{1,0:T(8,128)(2,1)S(1)}, bf16[256,512]{1,0:T(8,128)(2,1)S(1)}, u32[]{:S(2)}, u32[]{:S(2)}) collective-permute-start(bf16[256,512]{1,0:T(8,128)(2,1)S(1)} %add_convert_fusion.1), channel_id=1, source_target_pairs={{0,2},{1,3},{2,0},{3,1},{4,6},{5,7},{6,4},{7,5},{8,10},{9,11},{10,... | collective-permute-start | bytes 786440 | tf_op jit(solution)/shard_map/ppermute | solution.py:176
  72.7 6.8 %collective-permute-start.19 = (bf16[256,512]{1,0:T(8,128)(2,1)S(1)}, bf16[256,512]{1,0:T(8,128)(2,1)S(1)}, u32[]{:S(2)}, u32[]{:S(2)}) collective-permute-start(bf16[256,512]{1,0:T(8,128)(2,1)S(1)} %add_convert_fusion), channel_id=1, source_target_pairs={{0,1},{1,0},{2,3},{3,2},{4,5},{5,4},{6,7},{7,6},{8,9},{9,8},{10,11... | collective-permute-start | bytes 786440 | tf_op jit(solution)/shard_map/ppermute | solution.py:184
  78.5 7.7 %collective-permute-start.17 = (bf16[256,256]{1,0:T(8,128)(2,1)S(1)}, bf16[256,256]{1,0:T(8,128)(2,1)S(1)}, u32[]{:S(2)}, u32[]{:S(2)}) collective-permute-start(bf16[256,256]{1,0:T(8,128)(2,1)S(1)} %select_convert_fusion.1), channel_id=1, source_target_pairs={{0,4},{1,5},{2,6},{3,7},{4,0},{5,1},{6,2},{7,3},{8,12},{9,13},{10,... | collective-permute-start | bytes 393224 | tf_op jit(solution)/shard_map/ppermute | solution.py:176
  79.7 7.9 %collective-permute-start.20 = (bf16[256,256]{1,0:T(8,128)(2,1)S(1)}, bf16[256,256]{1,0:T(8,128)(2,1)S(1)}, u32[]{:S(2)}, u32[]{:S(2)}) collective-permute-start(bf16[256,256]{1,0:T(8,128)(2,1)S(1)} %select_convert_fusion), channel_id=1, source_target_pairs={{0,4},{1,5},{2,6},{3,7},{4,0},{5,1},{6,2},{7,3},{8,12},{9,13},{10,... | collective-permute-start | bytes 393224 | tf_op jit(solution)/shard_map/ppermute | solution.py:176
  87.7 6.4 %collective-permute-start.21 = (bf16[256,128]{1,0:T(8,128)(2,1)S(1)}, bf16[256,128]{1,0:T(8,128)(2,1)S(1)}, u32[]{:S(2)}, u32[]{:S(2)}) collective-permute-start(bf16[256,128]{1,0:T(8,128)(2,1)S(1)} %fusion.6), channel_id=1, source_target_pairs={{0,1},{1,0},{2,3},{3,2},{4,5},{5,4},{6,7},{7,6},{8,9},{9,8},{10,11... | collective-permute-start | bytes 196616 | tf_op jit(solution)/shard_map/ppermute | solution.py:184
  89.2 6.5 %collective-permute-start.22 = (bf16[256,128]{1,0:T(8,128)(2,1)S(1)}, bf16[256,128]{1,0:T(8,128)(2,1)S(1)}, u32[]{:S(2)}, u32[]{:S(2)}) collective-permute-start(bf16[256,128]{1,0:T(8,128)(2,1)S(1)} %fusion.5), channel_id=1, source_target_pairs={{0,1},{1,0},{2,3},{3,2},{4,5},{5,4},{6,7},{7,6},{8,9},{9,8},{10,11... | collective-permute-start | bytes 196616 | tf_op jit(solution)/shard_map/ppermute | solution.py:184
  89.8 6.8 %collective-permute-start.25 = (bf16[128,256]{1,0:T(8,128)(2,1)S(1)}, bf16[128,256]{1,0:T(8,128)(2,1)S(1)}, u32[]{:S(2)}, u32[]{:S(2)}) collective-permute-start(bf16[128,256]{1,0:T(8,128)(2,1)S(1)} %get-tuple-element.76), channel_id=1, source_target_pairs={{0,18},{1,19},{2,16},{3,17},{4,22},{5,23},{6,20},{7,21},{8,26},{9,... | collective-permute-start | bytes 196616 | tf_op jit(solution)/shard_map/ppermute | solution.py:303
  89.9 7.1 %collective-permute-start.23 = (bf16[128,256]{1,0:T(8,128)(2,1)S(1)}, bf16[128,256]{1,0:T(8,128)(2,1)S(1)}, u32[]{:S(2)}, u32[]{:S(2)}) collective-permute-start(bf16[128,256]{1,0:T(8,128)(2,1)S(1)} %get-tuple-element.96), channel_id=1, source_target_pairs={{0,22},{1,23},{2,20},{3,21},{4,18},{5,19},{6,16},{7,17},{8,30},{9,... | collective-permute-start | bytes 196616 | tf_op jit(solution)/shard_map/ppermute | solution.py:303
  92.9 6.2 %collective-permute-start.24 = (bf16[128,256]{1,0:T(8,128)(2,1)S(1)}, bf16[128,256]{1,0:T(8,128)(2,1)S(1)}, u32[]{:S(2)}, u32[]{:S(2)}) collective-permute-start(bf16[128,256]{1,0:T(8,128)(2,1)S(1)} %get-tuple-element.94), channel_id=1, source_target_pairs={{0,20},{1,21},{2,22},{3,23},{4,16},{5,17},{6,18},{7,19},{8,28},{9,... | collective-permute-start | bytes 196616 | tf_op jit(solution)/shard_map/ppermute | solution.py:303
  94.1 5.0 %collective-permute-start.26 = (bf16[128,256]{1,0:T(8,128)(2,1)S(1)}, bf16[128,256]{1,0:T(8,128)(2,1)S(1)}, u32[]{:S(2)}, u32[]{:S(2)}) collective-permute-start(bf16[128,256]{1,0:T(8,128)(2,1)S(1)} %get-tuple-element.95), channel_id=1, source_target_pairs={{0,16},{1,17},{2,18},{3,19},{4,20},{5,21},{6,22},{7,23},{8,24},{9,... | collective-permute-start | bytes 196616 | tf_op jit(solution)/shard_map/ppermute | solution.py:303

commit v7 on v5

--- a/solution.py
+++ b/solution.py
@@ -297,7 +297,7 @@
             ]
             leaving = turned[step]
             if step == 1:
-                leaving = after((leaving, other_half))[0]
+                leaving = after((leaving, other_half[:GROUP_ROWS]))[0]
             came.append(lax.ppermute(leaving, ("occ", "vir"), route))
         partner = jnp.concatenate(picked(came), axis=1).astype(jnp.float32)
     else:

time: 101 us -> 101 us (level)
  no operation moved by 1% of the time
where the time goes in v7:
time: 101 us
  starting transfers between devices  39 us (39%)
  Pallas kernels  31.2 us (31%)
  waiting for transfers between devices  25.2 us (25%)
  other arithmetic  2.68 us (3%)
  local copies, waits for them, and re-layouts  2.11 us (2%)
    pallas_call x5, Pallas kernels, ladder(): pl.pallas_call(functools.partial(ladder_kernel, distances, len(kept), sum...  24.5 us
    ppermute x11, waiting for transfers between devices, z_swap(): return lax.ppermute(block, 'vir', route)  18.1 us
    ppermute x11, starting transfers between devices, z_swap(): return lax.ppermute(block, 'vir', route)  15.4 us
    ppermute x11, starting transfers between devices, x_swap(): return lax.ppermute(block, 'vir', [(i, i ^ 1) for i in range(vir_devices)])  14.6 us
    pallas_call x1, Pallas kernels, keep_sums(): pl.pallas_call(functools.partial(keep_kernel, len(parts)), out_shape=[jax...  6.67 us
    ppermute x4, starting transfers between devices, per_device(): came.append(lax.ppermute(leaving, ('occ', 'vir'), route))  5.92 us
    ppermute x11, waiting for transfers between devices, x_swap(): return lax.ppermute(block, 'vir', [(i, i ^ 1) for i in range(vir_devices)])  4.67 us
    ppermute x1, starting transfers between devices, y_swap(): lax.ppermute(block, 'occ', [(i, (i + across) % occ_devices) for i in rang...  3.03 us
  transfers between devices with their start and end apart: 27, of which 13 were waited for; matrix products, arithmetic and copies ran while one was open for 2% of the time, Pallas kernels for 28%

profile of v7, /device:TPU:0, one launch (start us, length us, event | category | flops | bytes accessed | tf_op | source)
XLA Modules:
  0.0 100.7 jit_solution(9309189642787797411)
XLA Ops:
  1.1 3.0 %collective-permute-start.1 = (bf16[128,1024]{1,0:T(8,128)(2,1)S(1)}, bf16[128,1024]{1,0:T(8,128)(2,1)S(1)}, u32[]{:S(2)}, u32[]{:S(2)}) collective-permute-start(bf16[128,1024]{1,0:T(8,128)(2,1)S(1)} %get-tuple-element.87), channel_id=1, source_target_pairs={{0,16},{8,24},{16,0},{24,8},{1,17},{9,25},{17,1},{25,9},{2,18},{10... | collective-permute-start | bytes 786440 | tf_op jit(solution)/shard_map/ppermute | solution.py:179
  4.1 1.6 %collective-permute-start.8 = (bf16[128,1024]{1,0:T(8,128)(2,1)S(1)}, bf16[128,1024]{1,0:T(8,128)(2,1)S(1)}, u32[]{:S(2)}, u32[]{:S(2)}) collective-permute-start(bf16[128,1024]{1,0:T(8,128)(2,1)S(1)} %get-tuple-element.88.refs_0_), channel_id=1, source_target_pairs={{0,2},{1,3},{2,0},{3,1},{4,6},{5,7},{6,4},{7,5},{8,10},{9,11},{10,... | collective-permute-start | bytes 786440 | tf_op jit(solution)/shard_map/ppermute | solution.py:176
  5.7 1.5 %collective-permute-start = (bf16[128,1024]{1,0:T(8,128)(2,1)S(1)}, bf16[128,1024]{1,0:T(8,128)(2,1)S(1)}, u32[]{:S(2)}, u32[]{:S(2)}) collective-permute-start(bf16[128,1024]{1,0:T(8,128)(2,1)S(1)} %get-tuple-element.88.refs_0_), channel_id=1, source_target_pairs={{0,1},{1,0},{2,3},{3,2},{4,5},{5,4},{6,7},{7,6},{8,9},{9,8},{10,11... | collective-permute-start | bytes 786440 | tf_op jit(solution)/shard_map/ppermute | solution.py:184
  7.2 2.6 %collective-permute-start.4 = (bf16[128,1024]{1,0:T(8,128)(2,1)S(1)}, bf16[128,1024]{1,0:T(8,128)(2,1)S(1)}, u32[]{:S(2)}, u32[]{:S(2)}) collective-permute-start(bf16[128,1024]{1,0:T(8,128)(2,1)S(1)} %get-tuple-element.88.refs_0_), channel_id=1, source_target_pairs={{0,4},{1,5},{2,6},{3,7},{4,0},{5,1},{6,2},{7,3},{8,12},{9,13},{10,... | collective-permute-start | bytes 786440 | tf_op jit(solution)/shard_map/ppermute | solution.py:176
  10.4 1.8 %collective-permute-start.5 = (bf16[128,1024]{1,0:T(8,128)(2,1)S(1)}, bf16[128,1024]{1,0:T(8,128)(2,1)S(1)}, u32[]{:S(2)}, u32[]{:S(2)}) collective-permute-start(bf16[128,1024]{1,0:T(8,128)(2,1)S(1)} %collective-permute-done.1.refs_2_), channel_id=1, source_target_pairs={{0,2},{1,3},{2,0},{3,1},{4,6},{5,7},{6,4},{7,5},{8,10},{9,11},{10,... | collective-permute-start | bytes 786440 | tf_op jit(solution)/shard_map/ppermute | solution.py:176
  12.2 5.4 %collective-permute-done.8.refs_0_ = bf16[128,1024]{1,0:T(8,128)(2,1)S(1)} collective-permute-done((bf16[128,1024]{1,0:T(8,128)(2,1)S(1)}, bf16[128,1024]{1,0:T(8,128)(2,1)S(1)}, u32[]{:S(2)}, u32[]{:S(2)}) %collective-permute-start.8) | collective-permute-done | bytes 262176 | tf_op jit(solution)/shard_map/ppermute | solution.py:176
  17.6 2.8 %collective-permute-start.9 = (bf16[128,1024]{1,0:T(8,128)(2,1)S(1)}, bf16[128,1024]{1,0:T(8,128)(2,1)S(1)}, u32[]{:S(2)}, u32[]{:S(2)}) collective-permute-start(bf16[128,1024]{1,0:T(8,128)(2,1)S(1)} %collective-permute-done.8.refs_0_), channel_id=1, source_target_pairs={{0,1},{1,0},{2,3},{3,2},{4,5},{5,4},{6,7},{7,6},{8,9},{9,8},{10,11... | collective-permute-start | bytes 786440 | tf_op jit(solution)/shard_map/ppermute | solution.py:184
  20.5 1.2 %collective-permute-start.2 = (bf16[128,1024]{1,0:T(8,128)(2,1)S(1)}, bf16[128,1024]{1,0:T(8,128)(2,1)S(1)}, u32[]{:S(2)}, u32[]{:S(2)}) collective-permute-start(bf16[128,1024]{1,0:T(8,128)(2,1)S(1)} %collective-permute-done.1.refs_2_), channel_id=1, source_target_pairs={{0,4},{1,5},{2,6},{3,7},{4,0},{5,1},{6,2},{7,3},{8,12},{9,13},{10,... | collective-permute-start | bytes 786440 | tf_op jit(solution)/shard_map/ppermute | solution.py:176
  21.7 5.0 %shard_map.73 = (f32[256,1024]{1,0:T(8,128)S(1)}, f32[512,512]{1,0:T(8,128)S(1)}, bf16[1024,768]{1,0:T(8,128)(2,1)S(1)}, bf16[1024,768]{1,0:T(8,128)(2,1)S(1)}, bf16[3,1024,1024]{2,1,0:T(8,128)(2,1)S(1)}) custom-call(bf16[3,1024,1024]{2,1,0:T(8,128)(2,1)} %factor_ref.1, bf16[128,1024]{1,0:T(8,128)(2,1)S(1)} %get-tuple-element.88.refs_0_, ...), custom_call_target="tpu_custom_call" | custom-call | bytes 11010048 | tf_op jit(solution)/shard_map/pallas_call | solution.py:108
  26.9 1.8 %collective-permute-start.6 = (bf16[128,1024]{1,0:T(8,128)(2,1)S(1)}, bf16[128,1024]{1,0:T(8,128)(2,1)S(1)}, u32[]{:S(2)}, u32[]{:S(2)}) collective-permute-start(bf16[128,1024]{1,0:T(8,128)(2,1)S(1)} %collective-permute-done.4.refs_0_), channel_id=1, source_target_pairs={{0,1},{1,0},{2,3},{3,2},{4,5},{5,4},{6,7},{7,6},{8,9},{9,8},{10,11... | collective-permute-start | bytes 786440 | tf_op jit(solution)/shard_map/ppermute | solution.py:184
  28.7 2.9 %collective-permute-start.12 = (bf16[128,1024]{1,0:T(8,128)(2,1)S(1)}, bf16[128,1024]{1,0:T(8,128)(2,1)S(1)}, u32[]{:S(2)}, u32[]{:S(2)}) collective-permute-start(bf16[128,1024]{1,0:T(8,128)(2,1)S(1)} %collective-permute-done.4.refs_0_), channel_id=1, source_target_pairs={{0,2},{1,3},{2,0},{3,1},{4,6},{5,7},{6,4},{7,5},{8,10},{9,11},{10,... | collective-permute-start | bytes 786440 | tf_op jit(solution)/shard_map/ppermute | solution.py:176
  31.7 5.5 %shard_map.74 = (f32[256,1024]{1,0:T(8,128)S(1)}, f32[512,512]{1,0:T(8,128)S(1)}, bf16[1024,1536]{1,0:T(8,128)(2,1)S(1)}, bf16[1024,1536]{1,0:T(8,128)(2,1)S(1)}) custom-call(bf16[3,1024,1024]{2,1,0:T(8,128)(2,1)S(1)} %get-tuple-element.42.factor_ref, ...), custom_call_target="tpu_custom_call", output_to_operand_aliasing={{0}: (5, {}), {1}: (6, {})} | custom-call | flops 4831838208 | bytes 11534336 | tf_op jit(solution)/shard_map/pallas_call | solution.py:108
  37.3 2.0 %collective-permute-start.14 = (bf16[128,1024]{1,0:T(8,128)(2,1)S(1)}, bf16[128,1024]{1,0:T(8,128)(2,1)S(1)}, u32[]{:S(2)}, u32[]{:S(2)}) collective-permute-start(bf16[128,1024]{1,0:T(8,128)(2,1)S(1)} %collective-permute-done.2.refs_2_), channel_id=1, source_target_pairs={{0,1},{1,0},{2,3},{3,2},{4,5},{5,4},{6,7},{7,6},{8,9},{9,8},{10,11... | collective-permute-start | bytes 786440 | tf_op jit(solution)/shard_map/ppermute | solution.py:184
  39.3 2.0 %collective-permute-start.13 = (bf16[128,1024]{1,0:T(8,128)(2,1)S(1)}, bf16[128,1024]{1,0:T(8,128)(2,1)S(1)}, u32[]{:S(2)}, u32[]{:S(2)}) collective-permute-start(bf16[128,1024]{1,0:T(8,128)(2,1)S(1)} %collective-permute-done.6.refs_1_), channel_id=1, source_target_pairs={{0,2},{1,3},{2,0},{3,1},{4,6},{5,7},{6,4},{7,5},{8,10},{9,11},{10,... | collective-permute-start | bytes 786440 | tf_op jit(solution)/shard_map/ppermute | solution.py:176
  41.3 1.4 %collective-permute-done.7.refs_3_ = bf16[128,1024]{1,0:T(8,128)(2,1)S(1)} collective-permute-done((bf16[128,1024]{1,0:T(8,128)(2,1)S(1)}, bf16[128,1024]{1,0:T(8,128)(2,1)S(1)}, u32[]{:S(2)}, u32[]{:S(2)}) %collective-permute-start.7) | collective-permute-done | bytes 262176 | tf_op jit(solution)/shard_map/ppermute | solution.py:184
  42.7 5.7 %shard_map.75 = (f32[256,1024]{1,0:T(8,128)S(1)}, f32[512,512]{1,0:T(8,128)S(1)}, bf16[1024,1536]{1,0:T(8,128)(2,1)S(1)}, bf16[1024,1536]{1,0:T(8,128)(2,1)S(1)}) custom-call(bf16[3,1024,1024]{2,1,0:T(8,128)(2,1)S(1)} %get-tuple-element.42.factor_ref, ...), custom_call_target="tpu_custom_call", output_to_operand_aliasing={{0}: (5, {}), {1}: (6, {})} | custom-call | flops 4831838208 | bytes 11534336 | tf_op jit(solution)/shard_map/pallas_call | solution.py:108
  48.4 2.1 %collective-permute-start.11 = (bf16[128,1024]{1,0:T(8,128)(2,1)S(1)}, bf16[128,1024]{1,0:T(8,128)(2,1)S(1)}, u32[]{:S(2)}, u32[]{:S(2)}) collective-permute-start(bf16[128,1024]{1,0:T(8,128)(2,1)S(1)} %collective-permute-done.3.refs_0_), channel_id=1, source_target_pairs={{0,1},{1,0},{2,3},{3,2},{4,5},{5,4},{6,7},{7,6},{8,9},{9,8},{10,11... | collective-permute-start | bytes 786440 | tf_op jit(solution)/shard_map/ppermute | solution.py:184
  50.5 5.5 %shard_map.76 = (f32[256,1024]{1,0:T(8,128)S(1)}, f32[512,512]{1,0:T(8,128)S(1)}, bf16[1024,1536]{1,0:T(8,128)(2,1)S(1)}, bf16[1024,1536]{1,0:T(8,128)(2,1)S(1)}) custom-call(bf16[3,1024,1024]{2,1,0:T(8,128)(2,1)S(1)} %get-tuple-element.42.factor_ref, ...), custom_call_target="tpu_custom_call", output_to_operand_aliasing={{0}: (5, {}), {1}: (6, {})} | custom-call | flops 4831838208 | bytes 11534336 | tf_op jit(solution)/shard_map/pallas_call | solution.py:108
  56.1 2.8 %shard_map.77 = (bf16[256,1024]{1,0:T(8,128)(2,1)S(1)}, bf16[512,512]{1,0:T(8,128)(2,1)S(1)}, bf16[1024,768]{1,0:T(8,128)(2,1)S(1)}, bf16[1024,768]{1,0:T(8,128)(2,1)S(1)}) custom-call(bf16[3,1024,1024]{2,1,0:T(8,128)(2,1)S(1)} %get-tuple-element.42.factor_ref, bf16[128,1024]{1,0:T(8,128)(2,1)S(1)} %collective-permute-done.3.refs_0_, ...), custom_call_target="tpu_custom_call" | custom-call | flops 2415919104 | bytes 11010048 | tf_op jit(solution)/shard_map/pallas_call | solution.py:108
  60.2 6.7 %shard_map.78 = (f32[256,1024]{1,0:T(8,128)S(1)}, f32[512,512]{1,0:T(8,128)S(1)}) custom-call(bf16[1024,768]{1,0:T(8,128)(2,1)S(1)} %get-tuple-element.43.refs_0_, bf16[1024,768]{1,0:T(8,128)(2,1)S(1)} %get-tuple-element.66.refs_1_, bf16[1024,1536]{1,0:T(8,128)(2,1)S(1)} %get-tuple-element.55.refs_2_, bf16[1024,1536]{1,0:T(8,128)(2,1)S(1)} %get-tuple-element.67.refs_3_, ...), custom_call_target="tpu_custom_call" | custom-call | flops 6442450944 | bytes 27262976 | tf_op jit(solution)/shard_map/pallas_call | solution.py:145
  67.5 2.3 %collective-permute-done.15 = bf16[256,1024]{1,0:T(8,128)(2,1)S(1)} collective-permute-done((bf16[256,1024]{1,0:T(8,128)(2,1)S(1)}, bf16[256,1024]{1,0:T(8,128)(2,1)S(1)}, u32[]{:S(2)}, u32[]{:S(2)}) %collective-permute-start.15) | collective-permute-done | bytes 524320 | tf_op jit(solution)/shard_map/ppermute | solution.py:184
  70.2 1.5 %collective-permute-done.18 = bf16[512,512]{1,0:T(8,128)(2,1)S(1)} collective-permute-done((bf16[512,512]{1,0:T(8,128)(2,1)S(1)}, bf16[512,512]{1,0:T(8,128)(2,1)S(1)}, u32[]{:S(2)}, u32[]{:S(2)}) %collective-permute-start.18) | collective-permute-done | bytes 524320 | tf_op jit(solution)/shard_map/ppermute | solution.py:176
  71.8 1.3 %collective-permute-start.19 = (bf16[256,512]{1,0:T(8,128)(2,1)S(1)}, bf16[256,512]{1,0:T(8,128)(2,1)S(1)}, u32[]{:S(2)}, u32[]{:S(2)}) collective-permute-start(bf16[256,512]{1,0:T(8,128)(2,1)S(1)} %add_convert_fusion), channel_id=1, source_target_pairs={{0,1},{1,0},{2,3},{3,2},{4,5},{5,4},{6,7},{7,6},{8,9},{9,8},{10,11... | collective-permute-start | bytes 786440 | tf_op jit(solution)/shard_map/ppermute | solution.py:184
  73.1 5.0 %collective-permute-done.16 = bf16[256,512]{1,0:T(8,128)(2,1)S(1)} collective-permute-done((bf16[256,512]{1,0:T(8,128)(2,1)S(1)}, bf16[256,512]{1,0:T(8,128)(2,1)S(1)}, u32[]{:S(2)}, u32[]{:S(2)}) %collective-permute-start.16) | collective-permute-done | bytes 262176 | tf_op jit(solution)/shard_map/ppermute | solution.py:176
  78.5 3.0 %collective-permute-start.20 = (bf16[256,256]{1,0:T(8,128)(2,1)S(1)}, bf16[256,256]{1,0:T(8,128)(2,1)S(1)}, u32[]{:S(2)}, u32[]{:S(2)}) collective-permute-start(bf16[256,256]{1,0:T(8,128)(2,1)S(1)} %select_convert_fusion), channel_id=1, source_target_pairs={{0,4},{1,5},{2,6},{3,7},{4,0},{5,1},{6,2},{7,3},{8,12},{9,13},{10,... | collective-permute-start | bytes 393224 | tf_op jit(solution)/shard_map/ppermute | solution.py:176
  81.5 4.6 %collective-permute-done.17 = bf16[256,256]{1,0:T(8,128)(2,1)S(1)} collective-permute-done((bf16[256,256]{1,0:T(8,128)(2,1)S(1)}, bf16[256,256]{1,0:T(8,128)(2,1)S(1)}, u32[]{:S(2)}, u32[]{:S(2)}) %collective-permute-start.17) | collective-permute-done | bytes 131104 | tf_op jit(solution)/shard_map/ppermute | solution.py:176
  86.1 1.3 %collective-permute-done.20 = bf16[256,256]{1,0:T(8,128)(2,1)S(1)} collective-permute-done((bf16[256,256]{1,0:T(8,128)(2,1)S(1)}, bf16[256,256]{1,0:T(8,128)(2,1)S(1)}, u32[]{:S(2)}, u32[]{:S(2)}) %collective-permute-start.20) | collective-permute-done | bytes 131104 | tf_op jit(solution)/shard_map/ppermute | solution.py:176
  88.1 1.6 %collective-permute-start.22 = (f32[256,128]{1,0:T(8,128)S(1)}, f32[256,128]{1,0:T(8,128)S(1)}, u32[]{:S(2)}, u32[]{:S(2)}) collective-permute-start(f32[256,128]{1,0:T(8,128)S(1)} %slice_select_fusion), channel_id=1, source_target_pairs={{0,1},{1,0},{2,3},{3,2},{4,5},{5,4},{6,7},{7,6},{8,9},{9,8},{10,11... | collective-permute-start | bytes 393224 | tf_op jit(solution)/shard_map/ppermute | solution.py:184
  89.7 1.8 %collective-permute-start.23 = (bf16[128,256]{1,0:T(8,128)(2,1)S(1)}, bf16[128,256]{1,0:T(8,128)(2,1)S(1)}, u32[]{:S(2)}, u32[]{:S(2)}) collective-permute-start(bf16[128,256]{1,0:T(8,128)(2,1)S(1)} %get-tuple-element.96), channel_id=1, source_target_pairs={{0,22},{1,23},{2,20},{3,21},{4,18},{5,19},{6,16},{7,17},{8,30},{9,... | collective-permute-start | bytes 196616 | tf_op jit(solution)/shard_map/ppermute | solution.py:301
  91.5 1.5 %collective-permute-start.26 = (bf16[128,256]{1,0:T(8,128)(2,1)S(1)}, bf16[128,256]{1,0:T(8,128)(2,1)S(1)}, u32[]{:S(2)}, u32[]{:S(2)}) collective-permute-start(bf16[128,256]{1,0:T(8,128)(2,1)S(1)} %get-tuple-element.95), channel_id=1, source_target_pairs={{0,16},{1,17},{2,18},{3,19},{4,20},{5,21},{6,22},{7,23},{8,24},{9,... | collective-permute-start | bytes 196616 | tf_op jit(solution)/shard_map/ppermute | solution.py:301
  94.1 2.6 %collective-permute-start.25 = (bf16[128,256]{1,0:T(8,128)(2,1)S(1)}, bf16[128,256]{1,0:T(8,128)(2,1)S(1)}, u32[]{:S(2)}, u32[]{:S(2)}) collective-permute-start(bf16[128,256]{1,0:T(8,128)(2,1)S(1)} %get-tuple-element.76), channel_id=1, source_target_pairs={{0,18},{1,19},{2,16},{3,17},{4,22},{5,23},{6,20},{7,21},{8,26},{9,... | collective-permute-start | bytes 196616 | tf_op jit(solution)/shard_map/ppermute | solution.py:301
  99.5 1.3 %fusion = f32[2,128,1024]{2,1,0:T(8,128)} fusion(f32[1,128,1024]{2,1,0:T(8,128)S(1)} %get-tuple-element.86, f32[1,128,1024]{2,1,0:T(8,128)S(1)} %get-tuple-element.85, f32[2]{0:T(128)S(1)} %add.91, f32[128,1024]{1,0:T(8,128)S(1)} %broadcast_add_fusion, s32[1024]{0:T(1024)S(1)} %copy-done.2, s32[2,128]{1,0:T(2,128)S(1)} %broadcast_xor_fusion), kind=kLoop, calls=%fused_computation.1 | loop fusion | flops 1572864 | bytes 2626568 | tf_op jit(solution)/shard_map/jit(_where)/select_n | solution.py:336
  (71 shorter events, 9.1 us)
Async XLA Ops:
  0.0 60.0 %copy-start = (s32[8,2]{0,1:T(2,128)S(1)}, s32[8,2]{0,1:T(2,128)}, u32[]{:S(2)}) copy-start(s32[8,2]{0,1:T(2,128)} %param.13) | copy-start | bytes 196
  1.1 9.3 %collective-permute-start.1 = (bf16[128,1024]{1,0:T(8,128)(2,1)S(1)}, bf16[128,1024]{1,0:T(8,128)(2,1)S(1)}, u32[]{:S(2)}, u32[]{:S(2)}) collective-permute-start(bf16[128,1024]{1,0:T(8,128)(2,1)S(1)} %get-tuple-element.87), channel_id=1, source_target_pairs={{0,16},{8,24},{16,0},{24,8},{1,17},{9,25},{17,1},{25,9},{2,18},{10... | collective-permute-start | bytes 786440 | tf_op jit(solution)/shard_map/ppermute | solution.py:179
  4.1 13.5 %collective-permute-start.8 = (bf16[128,1024]{1,0:T(8,128)(2,1)S(1)}, bf16[128,1024]{1,0:T(8,128)(2,1)S(1)}, u32[]{:S(2)}, u32[]{:S(2)}) collective-permute-start(bf16[128,1024]{1,0:T(8,128)(2,1)S(1)} %get-tuple-element.88.refs_0_), channel_id=1, source_target_pairs={{0,2},{1,3},{2,0},{3,1},{4,6},{5,7},{6,4},{7,5},{8,10},{9,11},{10,... | collective-permute-start | bytes 786440 | tf_op jit(solution)/shard_map/ppermute | solution.py:176
  5.7 14.8 %collective-permute-start = (bf16[128,1024]{1,0:T(8,128)(2,1)S(1)}, bf16[128,1024]{1,0:T(8,128)(2,1)S(1)}, u32[]{:S(2)}, u32[]{:S(2)}) collective-permute-start(bf16[128,1024]{1,0:T(8,128)(2,1)S(1)} %get-tuple-element.88.refs_0_), channel_id=1, source_target_pairs={{0,1},{1,0},{2,3},{3,2},{4,5},{5,4},{6,7},{7,6},{8,9},{9,8},{10,11... | collective-permute-start | bytes 786440 | tf_op jit(solution)/shard_map/ppermute | solution.py:184
  7.2 19.5 %collective-permute-start.4 = (bf16[128,1024]{1,0:T(8,128)(2,1)S(1)}, bf16[128,1024]{1,0:T(8,128)(2,1)S(1)}, u32[]{:S(2)}, u32[]{:S(2)}) collective-permute-start(bf16[128,1024]{1,0:T(8,128)(2,1)S(1)} %get-tuple-element.88.refs_0_), channel_id=1, source_target_pairs={{0,4},{1,5},{2,6},{3,7},{4,0},{5,1},{6,2},{7,3},{8,12},{9,13},{10,... | collective-permute-start | bytes 786440 | tf_op jit(solution)/shard_map/ppermute | solution.py:176
  10.4 16.5 %collective-permute-start.5 = (bf16[128,1024]{1,0:T(8,128)(2,1)S(1)}, bf16[128,1024]{1,0:T(8,128)(2,1)S(1)}, u32[]{:S(2)}, u32[]{:S(2)}) collective-permute-start(bf16[128,1024]{1,0:T(8,128)(2,1)S(1)} %collective-permute-done.1.refs_2_), channel_id=1, source_target_pairs={{0,2},{1,3},{2,0},{3,1},{4,6},{5,7},{6,4},{7,5},{8,10},{9,11},{10,... | collective-permute-start | bytes 786440 | tf_op jit(solution)/shard_map/ppermute | solution.py:176
  17.6 14.0 %collective-permute-start.9 = (bf16[128,1024]{1,0:T(8,128)(2,1)S(1)}, bf16[128,1024]{1,0:T(8,128)(2,1)S(1)}, u32[]{:S(2)}, u32[]{:S(2)}) collective-permute-start(bf16[128,1024]{1,0:T(8,128)(2,1)S(1)} %collective-permute-done.8.refs_0_), channel_id=1, source_target_pairs={{0,1},{1,0},{2,3},{3,2},{4,5},{5,4},{6,7},{7,6},{8,9},{9,8},{10,11... | collective-permute-start | bytes 786440 | tf_op jit(solution)/shard_map/ppermute | solution.py:184
  20.5 11.3 %collective-permute-start.10 = (bf16[128,1024]{1,0:T(8,128)(2,1)S(1)}, bf16[128,1024]{1,0:T(8,128)(2,1)S(1)}, u32[]{:S(2)}, u32[]{:S(2)}) collective-permute-start(bf16[128,1024]{1,0:T(8,128)(2,1)S(1)} %collective-permute-done.1.refs_2_), channel_id=1, source_target_pairs={{0,1},{1,0},{2,3},{3,2},{4,5},{5,4},{6,7},{7,6},{8,9},{9,8},{10,11... | collective-permute-start | bytes 786440 | tf_op jit(solution)/shard_map/ppermute | solution.py:184
  20.5 16.8 %collective-permute-start.2 = (bf16[128,1024]{1,0:T(8,128)(2,1)S(1)}, bf16[128,1024]{1,0:T(8,128)(2,1)S(1)}, u32[]{:S(2)}, u32[]{:S(2)}) collective-permute-start(bf16[128,1024]{1,0:T(8,128)(2,1)S(1)} %collective-permute-done.1.refs_2_), channel_id=1, source_target_pairs={{0,4},{1,5},{2,6},{3,7},{4,0},{5,1},{6,2},{7,3},{8,12},{9,13},{10,... | collective-permute-start | bytes 786440 | tf_op jit(solution)/shard_map/ppermute | solution.py:176
  26.9 12.4 %collective-permute-start.6 = (bf16[128,1024]{1,0:T(8,128)(2,1)S(1)}, bf16[128,1024]{1,0:T(8,128)(2,1)S(1)}, u32[]{:S(2)}, u32[]{:S(2)}) collective-permute-start(bf16[128,1024]{1,0:T(8,128)(2,1)S(1)} %collective-permute-done.4.refs_0_), channel_id=1, source_target_pairs={{0,1},{1,0},{2,3},{3,2},{4,5},{5,4},{6,7},{7,6},{8,9},{9,8},{10,11... | collective-permute-start | bytes 786440 | tf_op jit(solution)/shard_map/ppermute | solution.py:184
  28.7 21.8 %collective-permute-start.12 = (bf16[128,1024]{1,0:T(8,128)(2,1)S(1)}, bf16[128,1024]{1,0:T(8,128)(2,1)S(1)}, u32[]{:S(2)}, u32[]{:S(2)}) collective-permute-start(bf16[128,1024]{1,0:T(8,128)(2,1)S(1)} %collective-permute-done.4.refs_0_), channel_id=1, source_target_pairs={{0,2},{1,3},{2,0},{3,1},{4,6},{5,7},{6,4},{7,5},{8,10},{9,11},{10,... | collective-permute-start | bytes 786440 | tf_op jit(solution)/shard_map/ppermute | solution.py:176
  31.6 11.1 %collective-permute-start.7 = (bf16[128,1024]{1,0:T(8,128)(2,1)S(1)}, bf16[128,1024]{1,0:T(8,128)(2,1)S(1)}, u32[]{:S(2)}, u32[]{:S(2)}) collective-permute-start(bf16[128,1024]{1,0:T(8,128)(2,1)S(1)} %collective-permute-done.5.refs_2_), channel_id=1, source_target_pairs={{0,1},{1,0},{2,3},{3,2},{4,5},{5,4},{6,7},{7,6},{8,9},{9,8},{10,11... | collective-permute-start | bytes 786440 | tf_op jit(solution)/shard_map/ppermute | solution.py:184
  37.3 13.2 %collective-permute-start.14 = (bf16[128,1024]{1,0:T(8,128)(2,1)S(1)}, bf16[128,1024]{1,0:T(8,128)(2,1)S(1)}, u32[]{:S(2)}, u32[]{:S(2)}) collective-permute-start(bf16[128,1024]{1,0:T(8,128)(2,1)S(1)} %collective-permute-done.2.refs_2_), channel_id=1, source_target_pairs={{0,1},{1,0},{2,3},{3,2},{4,5},{5,4},{6,7},{7,6},{8,9},{9,8},{10,11... | collective-permute-start | bytes 786440 | tf_op jit(solution)/shard_map/ppermute | solution.py:184
  39.3 9.1 %collective-permute-start.3 = (bf16[128,1024]{1,0:T(8,128)(2,1)S(1)}, bf16[128,1024]{1,0:T(8,128)(2,1)S(1)}, u32[]{:S(2)}, u32[]{:S(2)}) collective-permute-start(bf16[128,1024]{1,0:T(8,128)(2,1)S(1)} %collective-permute-done.2.refs_2_), channel_id=1, source_target_pairs={{0,2},{1,3},{2,0},{3,1},{4,6},{5,7},{6,4},{7,5},{8,10},{9,11},{10,... | collective-permute-start | bytes 786440 | tf_op jit(solution)/shard_map/ppermute | solution.py:176
  39.3 11.2 %collective-permute-start.13 = (bf16[128,1024]{1,0:T(8,128)(2,1)S(1)}, bf16[128,1024]{1,0:T(8,128)(2,1)S(1)}, u32[]{:S(2)}, u32[]{:S(2)}) collective-permute-start(bf16[128,1024]{1,0:T(8,128)(2,1)S(1)} %collective-permute-done.6.refs_1_), channel_id=1, source_target_pairs={{0,2},{1,3},{2,0},{3,1},{4,6},{5,7},{6,4},{7,5},{8,10},{9,11},{10,... | collective-permute-start | bytes 786440 | tf_op jit(solution)/shard_map/ppermute | solution.py:176
  48.4 7.6 %collective-permute-start.11 = (bf16[128,1024]{1,0:T(8,128)(2,1)S(1)}, bf16[128,1024]{1,0:T(8,128)(2,1)S(1)}, u32[]{:S(2)}, u32[]{:S(2)}) collective-permute-start(bf16[128,1024]{1,0:T(8,128)(2,1)S(1)} %collective-permute-done.3.refs_0_), channel_id=1, source_target_pairs={{0,1},{1,0},{2,3},{3,2},{4,5},{5,4},{6,7},{7,6},{8,9},{9,8},{10,11... | collective-permute-start | bytes 786440 | tf_op jit(solution)/shard_map/ppermute | solution.py:184
  56.1 4.0 %copy-start.1 = (f32[1024]{0:T(1024)S(1)}, f32[1024]{0:T(1024)}, u32[]{:S(2)}) copy-start(f32[1024]{0:T(1024)} %param.10) | copy-start | bytes 12292
  56.1 4.0 %copy-start.2 = (s32[1024]{0:T(1024)S(1)}, s32[1024]{0:T(1024)}, u32[]{:S(2)}) copy-start(s32[1024]{0:T(1024)} %param.12) | copy-start | bytes 12292
  58.9 10.9 %collective-permute-start.15 = (bf16[256,1024]{1,0:T(8,128)(2,1)S(1)}, bf16[256,1024]{1,0:T(8,128)(2,1)S(1)}, u32[]{:S(2)}, u32[]{:S(2)}) collective-permute-start(bf16[256,1024]{1,0:T(8,128)(2,1)S(1)} %get-tuple-element.73), channel_id=1, source_target_pairs={{0,1},{1,0},{2,3},{3,2},{4,5},{5,4},{6,7},{7,6},{8,9},{9,8},{10,11... | collective-permute-start | bytes 1572872 | tf_op jit(solution)/shard_map/ppermute | solution.py:184
  59.7 12.0 %collective-permute-start.18 = (bf16[512,512]{1,0:T(8,128)(2,1)S(1)}, bf16[512,512]{1,0:T(8,128)(2,1)S(1)}, u32[]{:S(2)}, u32[]{:S(2)}) collective-permute-start(bf16[512,512]{1,0:T(8,128)(2,1)S(1)} %get-tuple-element.75), channel_id=1, source_target_pairs={{0,2},{1,3},{2,0},{3,1},{4,6},{5,7},{6,4},{7,5},{8,10},{9,11},{10,... | collective-permute-start | bytes 1572872 | tf_op jit(solution)/shard_map/ppermute | solution.py:176
  60.2 6.7 %copy-start.3 = (s32[100]{0:T(128)S(1)}, s32[100]{0:T(128)}, u32[]{:S(2)}) copy-start(s32[100]{0:T(128)} %param.11) | copy-start | bytes 1204
  60.2 9.7 %copy-start.4 = (f32[100]{0:T(128)S(1)}, f32[100]{0:T(128)}, u32[]{:S(2)}) copy-start(f32[100]{0:T(128)} %param.9) | copy-start | bytes 1204
  69.9 8.3 %collective-permute-start.16 = (bf16[256,512]{1,0:T(8,128)(2,1)S(1)}, bf16[256,512]{1,0:T(8,128)(2,1)S(1)}, u32[]{:S(2)}, u32[]{:S(2)}) collective-permute-start(bf16[256,512]{1,0:T(8,128)(2,1)S(1)} %add_convert_fusion.1), channel_id=1, source_target_pairs={{0,2},{1,3},{2,0},{3,1},{4,6},{5,7},{6,4},{7,5},{8,10},{9,11},{10,... | collective-permute-start | bytes 786440 | tf_op jit(solution)/shard_map/ppermute | solution.py:176
  71.8 6.6 %collective-permute-start.19 = (bf16[256,512]{1,0:T(8,128)(2,1)S(1)}, bf16[256,512]{1,0:T(8,128)(2,1)S(1)}, u32[]{:S(2)}, u32[]{:S(2)}) collective-permute-start(bf16[256,512]{1,0:T(8,128)(2,1)S(1)} %add_convert_fusion), channel_id=1, source_target_pairs={{0,1},{1,0},{2,3},{3,2},{4,5},{5,4},{6,7},{7,6},{8,9},{9,8},{10,11... | collective-permute-start | bytes 786440 | tf_op jit(solution)/shard_map/ppermute | solution.py:184
  78.3 7.8 %collective-permute-start.17 = (bf16[256,256]{1,0:T(8,128)(2,1)S(1)}, bf16[256,256]{1,0:T(8,128)(2,1)S(1)}, u32[]{:S(2)}, u32[]{:S(2)}) collective-permute-start(bf16[256,256]{1,0:T(8,128)(2,1)S(1)} %select_convert_fusion.1), channel_id=1, source_target_pairs={{0,4},{1,5},{2,6},{3,7},{4,0},{5,1},{6,2},{7,3},{8,12},{9,13},{10,... | collective-permute-start | bytes 393224 | tf_op jit(solution)/shard_map/ppermute | solution.py:176
  78.5 8.9 %collective-permute-start.20 = (bf16[256,256]{1,0:T(8,128)(2,1)S(1)}, bf16[256,256]{1,0:T(8,128)(2,1)S(1)}, u32[]{:S(2)}, u32[]{:S(2)}) collective-permute-start(bf16[256,256]{1,0:T(8,128)(2,1)S(1)} %select_convert_fusion), channel_id=1, source_target_pairs={{0,4},{1,5},{2,6},{3,7},{4,0},{5,1},{6,2},{7,3},{8,12},{9,13},{10,... | collective-permute-start | bytes 393224 | tf_op jit(solution)/shard_map/ppermute | solution.py:176
  87.6 5.4 %collective-permute-start.21 = (f32[256,128]{1,0:T(8,128)S(1)}, f32[256,128]{1,0:T(8,128)S(1)}, u32[]{:S(2)}, u32[]{:S(2)}) collective-permute-start(f32[256,128]{1,0:T(8,128)S(1)} %slice_select_fusion.1), channel_id=1, source_target_pairs={{0,1},{1,0},{2,3},{3,2},{4,5},{5,4},{6,7},{7,6},{8,9},{9,8},{10,11... | collective-permute-start | bytes 393224 | tf_op jit(solution)/shard_map/ppermute | solution.py:184
  88.1 5.9 %collective-permute-start.22 = (f32[256,128]{1,0:T(8,128)S(1)}, f32[256,128]{1,0:T(8,128)S(1)}, u32[]{:S(2)}, u32[]{:S(2)}) collective-permute-start(f32[256,128]{1,0:T(8,128)S(1)} %slice_select_fusion), channel_id=1, source_target_pairs={{0,1},{1,0},{2,3},{3,2},{4,5},{5,4},{6,7},{7,6},{8,9},{9,8},{10,11... | collective-permute-start | bytes 393224 | tf_op jit(solution)/shard_map/ppermute | solution.py:184
  89.7 7.8 %collective-permute-start.23 = (bf16[128,256]{1,0:T(8,128)(2,1)S(1)}, bf16[128,256]{1,0:T(8,128)(2,1)S(1)}, u32[]{:S(2)}, u32[]{:S(2)}) collective-permute-start(bf16[128,256]{1,0:T(8,128)(2,1)S(1)} %get-tuple-element.96), channel_id=1, source_target_pairs={{0,22},{1,23},{2,20},{3,21},{4,18},{5,19},{6,16},{7,17},{8,30},{9,... | collective-permute-start | bytes 196616 | tf_op jit(solution)/shard_map/ppermute | solution.py:301
  91.5 6.7 %collective-permute-start.24 = (bf16[128,256]{1,0:T(8,128)(2,1)S(1)}, bf16[128,256]{1,0:T(8,128)(2,1)S(1)}, u32[]{:S(2)}, u32[]{:S(2)}) collective-permute-start(bf16[128,256]{1,0:T(8,128)(2,1)S(1)} %get-tuple-element.94), channel_id=1, source_target_pairs={{0,20},{1,21},{2,22},{3,23},{4,16},{5,17},{6,18},{7,19},{8,28},{9,... | collective-permute-start | bytes 196616 | tf_op jit(solution)/shard_map/ppermute | solution.py:301
  91.5 6.9 %collective-permute-start.26 = (bf16[128,256]{1,0:T(8,128)(2,1)S(1)}, bf16[128,256]{1,0:T(8,128)(2,1)S(1)}, u32[]{:S(2)}, u32[]{:S(2)}) collective-permute-start(bf16[128,256]{1,0:T(8,128)(2,1)S(1)} %get-tuple-element.95), channel_id=1, source_target_pairs={{0,16},{1,17},{2,18},{3,19},{4,20},{5,21},{6,22},{7,23},{8,24},{9,... | collective-permute-start | bytes 196616 | tf_op jit(solution)/shard_map/ppermute | solution.py:301
  94.1 5.2 %collective-permute-start.25 = (bf16[128,256]{1,0:T(8,128)(2,1)S(1)}, bf16[128,256]{1,0:T(8,128)(2,1)S(1)}, u32[]{:S(2)}, u32[]{:S(2)}) collective-permute-start(bf16[128,256]{1,0:T(8,128)(2,1)S(1)} %get-tuple-element.76), channel_id=1, source_target_pairs={{0,18},{1,19},{2,16},{3,17},{4,22},{5,23},{6,20},{7,21},{8,26},{9,... | collective-permute-start | bytes 196616 | tf_op jit(solution)/shard_map/ppermute | solution.py:301
